TPU v7x, 512 devices: a whole 4x4x16 slice. The times are simulated.
512 devices in a mesh: depth: 8 (over x, z_hi), row: 4 (over y), col: 16 (over z_lo, core).
Axes of the slice: x: 4, y: 4, z: 16 (z_hi: 2, z_lo: 8; z = z_hi * 8 + z_lo), core: 2. Of those that a mesh axis runs over, the one named last changes fastest.
Arguments:
- x_out: float32 [8192, 768], P(('depth', 'col'), 'row'), may hold values from -6 to 6
- v_out: float32 [8192, 768], P(('depth', 'col'), 'row'), may hold values from -6 to 6
- dx_out: float32 [8192, 768], P(('depth', 'col'), 'row'), may hold values from -6 to 6
- dv_out: float32 [8192, 768], P(('depth', 'col'), 'row'), may hold values from -6 to 6
- gate_weight: bfloat16 [14336, 8192], P(('col', 'row'), 'depth'), may hold values from -0.0625 to 0.0625
- up_weight: bfloat16 [14336, 8192], P(('col', 'row'), 'depth'), may hold values from -0.0625 to 0.0625
- down_weight: bfloat16 [14336, 8192], P(('col', 'row'), 'depth'), may hold values from -0.046875 to 0.046875
Outputs:
- x_prev: float32 [8192, 768], P(('depth', 'col'), 'row')
- v_prev: float32 [8192, 768], P(('depth', 'col'), 'row')
- dx_prev: float32 [8192, 768], P(('depth', 'col'), 'row')
- grad_gate: float32 [14336, 8192], P(('col', 'row'), 'depth')
- grad_up: float32 [14336, 8192], P(('col', 'row'), 'depth')
- grad_down: float32 [14336, 8192], P(('col', 'row'), 'depth')
All inputs are finite; a program needn't handle non-finite values.
Results may differ from a plain program's by a relative error of at most 0.0061.
Values may be sent and summed in bfloat16 or wider, within the bound.
No kernel may reach another device: no remote copies, remote signals or barrier semaphores. Data moves between devices by JAX's collectives and lax.ppermute only.
A program may use at most 64 MiB of HBM per device.

v0:
```python
import jax
import jax.numpy as jnp
from jax import lax
from jax.sharding import PartitionSpec as P

momentum = 0.5


def contract(left, right, left_dim, right_dim):
    return lax.dot_general(
        left, right, (((left_dim,), (right_dim,)), ((), ())), preferred_element_type=jnp.float32
    )


def reduce_hidden(term_fn, count_rows):
    return lax.psum_scatter(
        term_fn(jnp.int32(0), count_rows * lax.axis_size("col")),
        "col",
        scatter_dimension=0,
        tiled=True,
    )


def nonlinear(gate, up_val, d_act):
    sig = jax.nn.sigmoid(gate)
    act = (gate * sig * up_val).astype(jnp.bfloat16)
    d_gate = (d_act * up_val * sig * (1.0 + gate * (1.0 - sig))).astype(jnp.bfloat16)
    d_up = (d_act * gate * sig).astype(jnp.bfloat16)
    return (act, d_gate, d_up)


def on_device(x_out, v_out, dx_out, dv_out, gate_weight, up_weight, down_weight):
    x_prev = x_out - v_out
    x_half = x_prev.astype(jnp.bfloat16)
    df_half = ((1.0 - momentum) * (dx_out + dv_out)).astype(jnp.bfloat16)
    x_cols, df_cols = (
        lax.all_gather(x_half, "col", axis=0, tiled=True),
        lax.all_gather(df_half, "col", axis=0, tiled=True),
    )
    gate_full, up_full, down_full, x_all, df_all = (
        lax.all_gather(gate_weight, "row", axis=0, tiled=True),
        lax.all_gather(up_weight, "row", axis=0, tiled=True),
        lax.all_gather(down_weight, "row", axis=0, tiled=True),
        lax.all_gather(x_cols, "row", axis=1, tiled=True),
        lax.all_gather(df_cols, "row", axis=1, tiled=True),
    )
    gate_part = contract(gate_full, x_cols, 1, 0)
    up_part = contract(up_full, x_cols, 1, 0)
    dact_part = contract(down_full, df_cols, 1, 0)
    gate, up_val, d_act = lax.psum((gate_part, up_part, dact_part), "depth")
    act, d_gate, d_up = nonlinear(gate, up_val, d_act)
    count_rows = x_out.shape[0]

    def down_term(start, count):
        return contract(down_full, act, 0, 0)

    y_out = reduce_hidden(down_term, count_rows)
    v_prev = (v_out - (1.0 - momentum) * y_out) / momentum

    def input_term(start, count):
        return contract(gate_full, d_gate, 0, 0) + contract(up_full, d_up, 0, 0)

    dx_prev = dx_out + reduce_hidden(input_term, count_rows)
    act_rows, dgate_rows, dup_rows = (
        lax.all_to_all(act, "row", split_axis=0, concat_axis=1, tiled=True),
        lax.all_to_all(d_gate, "row", split_axis=0, concat_axis=1, tiled=True),
        lax.all_to_all(d_up, "row", split_axis=0, concat_axis=1, tiled=True),
    )
    grad_gate = contract(dgate_rows, x_all, 1, 1)
    grad_up = contract(dup_rows, x_all, 1, 1)
    grad_down = contract(act_rows, df_all, 1, 1)
    return (x_prev, v_prev, dx_prev, grad_gate, grad_up, grad_down)


def solution(mesh):
    return jax.shard_map(
        on_device,
        mesh=mesh,
        in_specs=(
            P(("depth", "col"), "row"),
            P(("depth", "col"), "row"),
            P(("depth", "col"), "row"),
            P(("depth", "col"), "row"),
            P(("col", "row"), "depth"),
            P(("col", "row"), "depth"),
            P(("col", "row"), "depth"),
        ),
        out_specs=(
            P(("depth", "col"), "row"),
            P(("depth", "col"), "row"),
            P(("depth", "col"), "row"),
            P(("col", "row"), "depth"),
            P(("col", "row"), "depth"),
            P(("col", "row"), "depth"),
        ),
        check_vma=False,
    )
```

profile of v0, /device:TPU:1, one launch (start us, length us, event | category | flops | bytes accessed | tf_op | source)
XLA Modules:
  0.0 794.9 jit_solution(966769226064688869)
XLA Ops:
  10.4 0.9 copy.43
  12.1 40.1 %all_gather.21 = bf16[1024,192]{1,0:T(8,128)(2,1)S(1)} all-gather(bf16[64,192]{1,0:T(8,128)(2,1)S(1)} %get-tuple-element.33), channel_id=1, replica_groups=mesh['depth'=8,'row'=4,'col'=16] {'col'}, dimensions={0}, use_global_device_ids=true | all-gather | bytes 417792 | tf_op jit(solution)/shard_map/all_gather | solution.py:37
  52.2 27.7 %all_gather.25 = bf16[1024,192]{1,0:T(8,128)(2,1)S(1)} all-gather(bf16[64,192]{1,0:T(8,128)(2,1)S(1)} %copy.44), channel_id=1, replica_groups=mesh['depth'=8,'row'=4,'col'=16] {'col'}, dimensions={0}, use_global_device_ids=true | all-gather | bytes 417792 | tf_op jit(solution)/shard_map/all_gather | solution.py:38
  80.0 3.2 convolution_bitcast_fusion.2
  83.1 7.2 all-gather.6.cloned.1.call-done
  90.4 3.2 convolution_bitcast_fusion.3
  93.5 35.4 %all-gather.10.cloned.1.call-done = bf16[896,1024]{1,0:T(8,128)(2,1)} async-done(((bf16[224,1024]{1,0:T(8,128)(2,1)}), bf16[896,1024]{1,0:T(8,128)(2,1)}) %all-gather.10.cloned.1.call-update) | async-done | bytes 1835024 | tf_op jit(solution)/shard_map/all_gather | solution.py:43
  128.9 3.2 convolution_bitcast_fusion.1
  132.2 0.9 copy.47
  134.2 374.6 %all-reduce.3.cloned.1.call-done = (f32[896,192]{0,1:T(8,128)}, f32[896,192]{0,1:T(8,128)}, f32[896,192]{0,1:T(8,128)}) async-done(((f32[896,192]{0,1:T(8,128)}, f32[896,192]{0,1:T(8,128)}, f32[896,192]{0,1:T(8,128)}), (f32[896,192]{0,1:T(8,128)}, f32[896,192]{0,1:T(8,128)}, f32[896,192]{0,1:T(8,128)})) %all-reduce.3.cloned.1.call-update) | async-done | bytes 2064400 | tf_op jit(solution)/shard_map/psum | solution.py:50
  508.8 1.9 multiply_convert_fusion
  512.9 1.3 copy.55
  515.4 1.3 copy.53
  517.9 4.4 all-to-all-start
  524.6 5.1 all-to-all-done
  529.7 3.5 all-to-all-start.1
  533.2 14.0 %all-gather.12.cloned.1.call-done = bf16[1024,768]{0,1:T(8,128)(2,1)} async-done(((bf16[1024,192]{0,1:T(8,128)(2,1)}), bf16[1024,768]{0,1:T(8,128)(2,1)}) %all-gather.12.cloned.1.call-update) | async-done | bytes 1572880 | tf_op jit(solution)/shard_map/all_gather | solution.py:44
  547.2 3.0 fusion.3
  550.2 3.5 all-to-all-start.2
  553.7 1.5 fusion.4
  555.1 26.9 %all-gather.14.cloned.1.call-done = bf16[1024,768]{0,1:T(8,128)(2,1)} async-done(((bf16[1024,192]{0,1:T(8,128)(2,1)}), bf16[1024,768]{0,1:T(8,128)(2,1)}) %all-gather.14.cloned.1.call-update) | async-done | bytes 1572880 | tf_op jit(solution)/shard_map/all_gather | solution.py:45
  582.0 2.9 fusion.5
  584.9 98.4 %reduce-scatter.9.cloned.1.call-done = f32[64,192]{1,0:T(8,128)} async-done(((f32[1024,192]{1,0:T(8,128)}), f32[64,192]{1,0:T(8,128)}) %reduce-scatter.9.cloned.1.call-update) | async-done | bytes 49168
  685.0 101.5 %reduce-scatter.7.cloned.1.call-done = f32[64,192]{1,0:T(8,128)} async-done(((f32[1024,192]{1,0:T(8,128)}), f32[64,192]{1,0:T(8,128)}) %reduce-scatter.7.cloned.1.call-update) | async-done | bytes 49168
  (56 shorter events, 15.2 us)
Async XLA Ops:
  7.2 4.3 copy-start.7
  7.2 4.3 copy-start.6
  7.2 72.8 %all-gather.8.cloned.1.call-start = ((), (), s32[]{:S(2)}) async-start(), calls=%async_computation.6 | async-start | bytes 2293760 | tf_op jit(solution)/shard_map/all_gather | solution.py:42
  7.9 82.4 %all-gather.6.cloned.1.call-start = ((), (), s32[]{:S(2)}) async-start(), calls=%async_computation.5 | async-start | bytes 2293760 | tf_op jit(solution)/shard_map/all_gather | solution.py:41
  8.7 120.2 %all-gather.10.cloned.1.call-start = ((), (), s32[]{:S(2)}) async-start(), calls=%async_computation.7 | async-start | bytes 2293760 | tf_op jit(solution)/shard_map/all_gather | solution.py:43
  9.4 499.4 %all-reduce.3.cloned.1.call-start = ((), (), s32[]{:S(2)}) async-start(), calls=%async_computation.12 | async-start | bytes 4128768 | tf_op jit(solution)/shard_map/psum | solution.py:50
  132.1 415.1 %all-gather.12.cloned.1.call-start = ((), (), s32[]{:S(2)}) async-start(), calls=%async_computation.8 | async-start | bytes 1966080 | tf_op jit(solution)/shard_map/all_gather | solution.py:44
  133.1 448.9 %all-gather.14.cloned.1.call-start = ((), (), s32[]{:S(2)}) async-start(), calls=%async_computation.9 | async-start | bytes 1966080 | tf_op jit(solution)/shard_map/all_gather | solution.py:45
  134.1 376.6 %copy-start.2 = (bf16[896,1024]{1,0:T(8,128)(2,1)S(1)}, bf16[896,1024]{1,0:T(8,128)(2,1)}, u32[]{:S(2)}) copy-start(bf16[896,1024]{1,0:T(8,128)(2,1)} %all-gather.6.cloned.1.call-done) | copy-start | bytes 5505028
  134.1 549.2 %reduce-scatter.9.cloned.1.call-start = ((), (), s32[]{:S(2)}) async-start(), calls=%async_computation.11 | async-start | bytes 1114112
  510.7 0.7 copy-start.4
  510.7 1.6 copy-start
  512.9 1.9 copy-start.1
  514.3 272.2 %reduce-scatter.7.cloned.1.call-start = ((), (), s32[]{:S(2)}) async-start(), calls=%async_computation.10 | async-start | bytes 1114112
  515.4 1.4 copy-start.5
  517.9 11.8 %all-to-all-start = ((bf16[4,224,192]{1,2,0:T(8,128)(2,1)}), bf16[4,224,192]{1,2,0:T(8,128)(2,1)S(1)}, u32[]{:S(2)}, u32[]{:S(2)}) async-start(bf16[4,224,192]{1,2,0:T(8,128)(2,1)} %copy.46), calls=%async_computation | async-start | bytes 786432 | tf_op jit(solution)/shard_map/all_to_all | solution.py:66
  529.7 20.5 %all-to-all-start.1 = ((bf16[4,224,192]{1,2,0:T(8,128)(2,1)}), bf16[4,224,192]{1,2,0:T(8,128)(2,1)S(1)}, u32[]{:S(2)}, u32[]{:S(2)}) async-start(bf16[4,224,192]{1,2,0:T(8,128)(2,1)} %copy.48), calls=%async_computation.1 | async-start | bytes 786432 | tf_op jit(solution)/shard_map/all_to_all | solution.py:67
  547.2 6.5 copy-start.3
  550.2 31.8 %all-to-all-start.2 = ((bf16[4,224,192]{1,2,0:T(8,128)(2,1)}), bf16[4,224,192]{1,2,0:T(8,128)(2,1)S(1)}, u32[]{:S(2)}, u32[]{:S(2)}) async-start(bf16[4,224,192]{1,2,0:T(8,128)(2,1)} %copy.49), calls=%async_computation.2 | async-start | bytes 786432 | tf_op jit(solution)/shard_map/all_to_all | solution.py:65
Sparse Core Ops, SparseCore 0:
  10.1 41.6 all-gather.7
  53.9 36.3 all-gather.5
  92.5 36.3 all-gather.9
  132.5 376.2 all-reduce.2
  510.7 36.3 all-gather.11
  549.1 32.8 all-gather.13
  584.8 98.4 reduce-scatter.8
  686.3 100.0 reduce-scatter.6
where the time goes:
time: 802 us; the launch traced here: 795 us
  waiting for transfers between devices  665 us (83%)
  blocking collectives  67.9 us (8%)
  matrix products  18.6 us (2%)
  local copies, waits for them, and re-layouts  14.8 us (2%)
  between operations  14.3 us (2%)
  starting transfers between devices  11.6 us (1%)
    psum x1, waiting for transfers between devices, on_device(): gate, up_val, d_act = lax.psum((gate_part, up_part, dact_part), 'depth')  375 us
    unnamed x10, waiting for transfers between devices  202 us
    all_gather x1, blocking collectives, on_device(): lax.all_gather(x_half, 'col', axis=0, tiled=True)  40.1 us
    all_gather x1, waiting for transfers between devices, on_device(): lax.all_gather(down_weight, 'row', axis=0, tiled=True)  35.4 us
    all_gather x1, blocking collectives, on_device(): lax.all_gather(df_half, 'col', axis=0, tiled=True)  27.7 us
    all_gather x1, waiting for transfers between devices, on_device(): lax.all_gather(df_cols, 'row', axis=1, tiled=True)  26.9 us
    dot_general x9, matrix products, contract(): lax.dot_general(left, right, (((left_dim,), (right_dim,)), ((), ())), pre...  18.6 us
  transfers between devices with their start and end apart: 11, of which 8 were waited for; matrix products, arithmetic and copies ran while one was open for 4% of the time, Pallas kernels for 0%

commit v1 on v0

v1 whole, which is shorter than its diff:
```python
import jax
import jax.numpy as jnp
from jax import lax
from jax.sharding import PartitionSpec as P

momentum = 0.5
BF = jnp.bfloat16
F32 = jnp.float32


def copies(block, count):
    return jnp.broadcast_to(block[None], (count,) + block.shape)


def nonlinear(gate, up_val, d_act):
    sig = jax.nn.sigmoid(gate)
    act = (gate * sig * up_val).astype(BF)
    d_gate = (d_act * up_val * sig * (1.0 + gate * (1.0 - sig))).astype(BF)
    d_up = (d_act * gate * sig).astype(BF)
    return jnp.stack([act, d_gate, d_up])


def make(depth, rows, cols):
    count_x, count_z = depth // 2, cols // 2
    x_groups = [[2 * x + h for x in range(count_x)] for h in range(2)]
    z_groups = [[2 * z + k for z in range(count_z)] for k in range(2)]
    swap_core = [(c, c ^ 1) for c in range(cols)]
    swap_half = [(d, d ^ 1) for d in range(depth)]

    def over_x(blocks):
        return lax.all_to_all(blocks, "depth", 0, 0, axis_index_groups=x_groups)

    def over_z(blocks):
        return lax.all_to_all(blocks, "col", 0, 0, axis_index_groups=z_groups)

    def over_row(blocks):
        return lax.all_to_all(blocks, "row", 0, 0)

    def other_core(block):
        return lax.ppermute(block, "col", swap_core)

    def on_device(x_out, v_out, dx_out, dv_out, gate_weight, up_weight, down_weight):
        feats, toks = x_out.shape
        half = toks // 2
        hid = gate_weight.shape[0]
        core = lax.axis_index("col") % 2
        first = core == 0

        gate_w = jnp.concatenate([gate_weight, other_core(gate_weight)])
        up_w = jnp.concatenate([up_weight, other_core(up_weight)])
        down_w = jnp.concatenate([down_weight, other_core(down_weight)])

        x_prev = x_out - v_out
        x_half = x_prev.astype(BF)
        df_half = ((1.0 - momentum) * (dx_out + dv_out)).astype(BF)
        both = jnp.stack([x_half.T, df_half.T]).reshape(2, 2, half, feats)
        mine = jnp.where(first, both[:, 0], both[:, 1])
        theirs = other_core(jnp.where(first, both[:, 1], both[:, 0]))
        block = jnp.where(
            first, jnp.concatenate([mine, theirs], -1), jnp.concatenate([theirs, mine], -1)
        )

        along_z = over_z(copies(block, count_z))
        inputs = over_row(copies(along_z, rows))
        other_inputs = other_core(inputs)

        def forward(weight, which):
            return jnp.einsum(
                "hzf,rztf->hrt",
                weight.reshape(2 * hid, count_z, 2 * feats),
                inputs[:, :, which],
                preferred_element_type=F32,
            ).reshape(count_x, 2 * hid // count_x, rows * half)

        parts = jnp.stack(
            [forward(gate_w, 0), forward(up_w, 0), forward(down_w, 1)], 1
        ).astype(BF)
        sums = over_x(parts).astype(F32).sum(0)
        sums = sums + lax.ppermute(sums.astype(BF), "depth", swap_half).astype(F32)
        hidden = over_x(copies(nonlinear(sums[0], sums[1], sums[2]), count_x))
        hidden = jnp.swapaxes(hidden, 0, 1).reshape(3, 2 * hid, rows * half)
        other_hidden = other_core(hidden[:, hid:])

        def backward(weight, which):
            return jnp.einsum(
                "hrt,hzf->rztf",
                hidden[which].reshape(2 * hid, rows, half),
                weight.reshape(2 * hid, count_z, 2 * feats),
                preferred_element_type=F32,
            )

        terms = jnp.stack(
            [backward(down_w, 0), backward(gate_w, 1) + backward(up_w, 2)], 2
        ).astype(BF)
        terms = over_row(terms).astype(F32).sum(0).astype(BF)
        terms = over_z(terms).astype(F32).sum(0)
        low, high = terms[..., :feats], terms[..., feats:]
        mine = jnp.where(first, low, high)
        theirs = other_core(jnp.where(first, high, low))
        done = jnp.where(
            first, jnp.concatenate([mine, theirs], 1), jnp.concatenate([theirs, mine], 1)
        )
        done = jnp.swapaxes(done, 1, 2)
        v_prev = (v_out - (1.0 - momentum) * done[0]) / momentum
        dx_prev = dx_out + done[1]

        def gradient(which, source):
            def term(hid_part, in_part):
                return jnp.einsum(
                    "hrt,rztf->hzf",
                    hid_part.reshape(hid, rows, half),
                    in_part,
                    preferred_element_type=F32,
                )

            total = term(hidden[which, :hid], inputs[:, :, source]) + term(
                other_hidden[which], other_inputs[:, :, source]
            )
            return total.reshape(hid, count_z * 2 * feats)

        return (x_prev, v_prev, dx_prev, gradient(1, 0), gradient(2, 0), gradient(0, 1))

    return on_device


def solution(mesh):
    tokens = P(("depth", "col"), "row")
    weights = P(("col", "row"), "depth")
    return jax.shard_map(
        make(mesh.shape["depth"], mesh.shape["row"], mesh.shape["col"]),
        mesh=mesh,
        in_specs=(tokens,) * 4 + (weights,) * 3,
        out_specs=(tokens,) * 3 + (weights,) * 3,
        check_vma=False,
    )
```

time: 802 us -> 219 us (0.27)
  waiting for transfers between devices: 665 us -> 19.4 us
  starting transfers between devices: 11.6 us -> 91.3 us
  local copies, waits for them, and re-layouts: 14.8 us -> 31.2 us
  blocking collectives: 67.9 us -> 54.1 us
  between operations: 14.3 us -> 1.18 us
    psum x1 -> x0, waiting for transfers between devices: 375 us -> none  [on_device(): gate, up_val, d_act = lax.psum((gate_part, up_part, dact_part), 'depth')]
    unnamed x10 -> x0, waiting for transfers between devices: 202 us -> none
    all_gather x5 -> x0, waiting for transfers between devices: 83.5 us -> none  [the longest x1 35.4 us: on_device(): lax.all_gather(down_weight, 'row', axis=0, tiled=True)]
    all_gather x2 -> x0, blocking collectives: 67.9 us -> none  [the longest x1 40.1 us: on_device(): lax.all_gather(x_half, 'col', axis=0, tiled=True)]
    all_to_all x0 -> x3, blocking collectives: none -> 54.1 us  [the longest x1 27.7 us: over_z(): return lax.all_to_all(blocks, 'col', 0, 0, axis_index_groups=z_groups)]
    ppermute x0 -> x8, starting transfers between devices: none -> 49 us  [the longest x7 41.1 us: other_core(): return lax.ppermute(block, 'col', swap_core)]
    all_to_all x3, starting transfers between devices: 11.3 us -> 42.3 us  [the longest x1 33.6 us: over_z(): return lax.all_to_all(blocks, 'col', 0, 0, axis_index_groups=z_groups)]
    another operation x0 -> x11, local copies, waits for them, and re-layouts: none -> 13.8 us  [the longest x6 12.1 us: backward(): hidden[which].reshape(2 * hid, rows, half)]
  transfers between devices with their start and end apart: 11 -> 11, of which waited for: 8 -> 4; matrix products, arithmetic and copies ran while one was open for 4% -> 11% of each run, Pallas kernels for 0% -> 0%
where the time goes in v1:
time: 219 us; the launch traced here: 218 us
  starting transfers between devices  91.3 us (42%)
  blocking collectives  54.1 us (25%)
  local copies, waits for them, and re-layouts  31.2 us (14%)
  waiting for transfers between devices  19.4 us (9%)
  matrix products  13.2 us (6%)
  other arithmetic  7.66 us (3%)
    ppermute x7, starting transfers between devices, other_core(): return lax.ppermute(block, 'col', swap_core)  41.1 us
    all_to_all x1, starting transfers between devices, over_z(): return lax.all_to_all(blocks, 'col', 0, 0, axis_index_groups=z_groups)  33.6 us
    all_to_all x1, blocking collectives, over_z(): return lax.all_to_all(blocks, 'col', 0, 0, axis_index_groups=z_groups)  27.7 us
    all_to_all x2, blocking collectives, over_x(): return lax.all_to_all(blocks, 'depth', 0, 0, axis_index_groups=x_groups)  26.4 us
    another operation x6, local copies, waits for them, and re-layouts, backward(): hidden[which].reshape(2 * hid, rows, half)  12.1 us
    all_to_all x2, starting transfers between devices, over_row(): return lax.all_to_all(blocks, 'row', 0, 0)  8.67 us
    dot_general x6, matrix products, term(): jnp.einsum('hrt,rztf->hzf', hid_part.reshape(hid, rows, half), in_part, p...  8.15 us
    ppermute x1, waiting for transfers between devices, on_device(): sums = sums + lax.ppermute(sums.astype(BF), 'depth', swap_half).astype(F32)  8.14 us
  transfers between devices with their start and end apart: 11, of which 4 were waited for; matrix products, arithmetic and copies ran while one was open for 11% of the time, Pallas kernels for 0%

profile of v1, /device:TPU:1, one launch (start us, length us, event | category | flops | bytes accessed | tf_op | source)
XLA Modules:
  0.0 218.1 jit_solution(7764414689586927620)
XLA Ops:
  3.5 8.8 %collective-permute-start.2 = (bf16[2,96,64]{1,2,0:T(8,128)(2,1)S(1)}, bf16[2,96,64]{1,2,0:T(8,128)(2,1)S(1)}, u32[]{:S(2)}, u32[]{:S(2)}) collective-permute-start(bf16[2,96,64]{1,2,0:T(8,128)(2,1)S(1)} %bitcast.224), channel_id=1, source_target_pairs={{0,1},{1,0},{2,3},{3,2},{4,5},{5,4},{6,7},{7,6},{8,9},{9,8},{10,11... | collective-permute-start | bytes 73736 | tf_op jit(solution)/shard_map/ppermute | solution.py:40
  13.3 27.7 %all_to_all.30 = bf16[8,2,96,128]{3,2,1,0:T(8,128)(2,1)S(1)} all-to-all(bf16[8,2,96,128]{3,2,1,0:T(8,128)(2,1)S(1)} %broadcast_in_dim.6), channel_id=1, replica_groups={{0,2,4,6,8,10,12,14},{1,3,5,7,9,11,13,15},{16,18,20,22,24,26,28,30},{17..., dimensions={0} | all-to-all | bytes 786432 | tf_op jit(solution)/shard_map/all_to_all | solution.py:34
  42.5 4.3 %all-to-all-start.1 = ((bf16[4,8,2,96,128]{4,3,1,2,0:T(8,128)(2,1)}), bf16[4,8,2,96,128]{4,3,1,2,0:T(8,128)(2,1)S(1)}, u32[]{:S(2)}, u32[]{:S(2)}) async-start(bf16[4,8,2,96,128]{4,3,1,2,0:T(8,128)(2,1)} %broadcast_in_dim.7), calls=%async_computation.1 | async-start | bytes 3145728 | tf_op jit(solution)/shard_map/all_to_all | solution.py:37
  46.8 5.2 %collective-permute-start.1 = (bf16[224,1024]{1,0:T(8,128)(2,1)S(1)}, bf16[224,1024]{1,0:T(8,128)(2,1)S(1)}, u32[]{:S(2)}, u32[]{:S(2)}) collective-permute-start(bf16[224,1024]{1,0:T(8,128)(2,1)S(1)} %copy-done.7), channel_id=1, source_target_pairs={{0,1},{1,0},{2,3},{3,2},{4,5},{5,4},{6,7},{7,6},{8,9},{9,8},{10,11... | collective-permute-start | bytes 1376264 | tf_op jit(solution)/shard_map/ppermute | solution.py:40
  52.0 1.9 collective-permute-start
  53.9 2.4 %collective-permute-start.3 = (bf16[224,1024]{1,0:T(8,128)(2,1)}, bf16[224,1024]{1,0:T(8,128)(2,1)S(1)}, u32[]{:S(2)}, u32[]{:S(2)}) collective-permute-start(bf16[224,1024]{1,0:T(8,128)(2,1)} %param.12), channel_id=1, source_target_pairs={{0,1},{1,0},{2,3},{3,2},{4,5},{5,4},{6,7},{7,6},{8,9},{9,8},{10,11... | collective-permute-start | bytes 1376264 | tf_op jit(solution)/shard_map/ppermute | solution.py:40
  60.6 3.7 %all-to-all-done.1 = bf16[4,8,2,96,128]{4,3,1,2,0:T(8,128)(2,1)S(1)} async-done(((bf16[4,8,2,96,128]{4,3,1,2,0:T(8,128)(2,1)}), bf16[4,8,2,96,128]{4,3,1,2,0:T(8,128)(2,1)S(1)}, u32[]{:S(2)}, u32[]{:S(2)}) %all-to-all-start.1) | async-done | bytes 1572896 | tf_op jit(solution)/shard_map/all_to_all | solution.py:37
  67.2 14.3 %all_to_all.31 = bf16[4,3,112,384]{3,2,1,0:T(8,128)(2,1)S(1)} all-to-all(bf16[4,3,112,384]{3,2,1,0:T(8,128)(2,1)S(1)} %copy.109), channel_id=1, replica_groups={{0,128,256,384},{64,192,320,448},{1,129,257,385},{65,193,321,449},{2,13..., dimensions={0} | all-to-all | bytes 2064384 | tf_op jit(solution)/shard_map/all_to_all | solution.py:31
  81.7 7.9 %collective-permute-start.4 = (bf16[3,112,384]{2,1,0:T(8,128)(2,1)S(1)}, bf16[3,112,384]{2,1,0:T(8,128)(2,1)S(1)}, u32[]{:S(2)}, u32[]{:S(2)}) collective-permute-start(bf16[3,112,384]{2,1,0:T(8,128)(2,1)S(1)} %convert_element_type.37), channel_id=1, source_target_pairs={{0,64},{64,0},{128,192},{192,128},{256,320},{320,256},{384,448},{4... | collective-permute-start | bytes 774152 | tf_op jit(solution)/shard_map/ppermute | solution.py:79
  89.7 8.1 %collective-permute-done.4 = bf16[3,112,384]{2,1,0:T(8,128)(2,1)S(1)} collective-permute-done((bf16[3,112,384]{2,1,0:T(8,128)(2,1)S(1)}, bf16[3,112,384]{2,1,0:T(8,128)(2,1)S(1)}, u32[]{:S(2)}, u32[]{:S(2)}) %collective-permute-start.4) | collective-permute-done | bytes 258080 | tf_op jit(solution)/shard_map/ppermute | solution.py:79
  98.1 12.1 %all_to_all.32 = bf16[4,3,112,384]{3,2,1,0:T(8,128)(2,1)S(1)} all-to-all(bf16[4,3,112,384]{3,2,1,0:T(8,128)(2,1)S(1)} %broadcast_in_dim.8), channel_id=1, replica_groups={{0,128,256,384},{64,192,320,448},{1,129,257,385},{65,193,321,449},{2,13..., dimensions={0} | all-to-all | bytes 2064384 | tf_op jit(solution)/shard_map/all_to_all | solution.py:31
  111.3 2.0 reshape.144
  113.3 2.0 copy.152
  115.4 2.0 reshape.145
  117.4 2.0 copy.155
  119.4 2.0 reshape.143
  121.4 2.0 copy.149
  123.5 2.0 fusion.15
  128.5 4.4 %all-to-all-start.4 = ((bf16[4,8,2,96,128]{4,3,1,2,0:T(8,128)(2,1)}), bf16[4,8,2,96,128]{4,3,1,2,0:T(8,128)(2,1)}, u32[]{:S(2)}, u32[]{:S(2)}) async-start(bf16[4,8,2,96,128]{4,3,1,2,0:T(8,128)(2,1)} %copy.117), calls=%async_computation.4 | async-start | bytes 3145728 | tf_op jit(solution)/shard_map/all_to_all | solution.py:37
  134.2 12.3 %collective-permute-start.7 = (bf16[4,8,2,96,128]{4,3,0,1,2:T(8,128)(2,1)}, bf16[4,8,2,96,128]{4,3,0,1,2:T(8,128)(2,1)}, u32[]{:S(2)}, u32[]{:S(2)}) collective-permute-start(bf16[4,8,2,96,128]{4,3,0,1,2:T(8,128)(2,1)} %copy.104), channel_id=1, source_target_pairs={{0,1},{1,0},{2,3},{3,2},{4,5},{5,4},{6,7},{7,6},{8,9},{9,8},{10,11... | collective-permute-start | bytes 4718600 | tf_op jit(solution)/shard_map/ppermute | solution.py:40
  154.2 33.6 %all-to-all-start.5 = ((bf16[8,2,96,128]{3,2,1,0:T(8,128)(2,1)}), bf16[8,2,96,128]{3,2,1,0:T(8,128)(2,1)S(1)}, u32[]{:S(2)}, u32[]{:S(2)}) async-start(bf16[8,2,96,128]{3,2,1,0:T(8,128)(2,1)} %copy.119), calls=%async_computation.5 | async-start | bytes 786432 | tf_op jit(solution)/shard_map/all_to_all | solution.py:34
  193.5 1.9 fusion.7
  198.5 6.7 %all-to-all-done.5 = bf16[8,2,96,128]{3,2,1,0:T(8,128)(2,1)S(1)} async-done(((bf16[8,2,96,128]{3,2,1,0:T(8,128)(2,1)}), bf16[8,2,96,128]{3,2,1,0:T(8,128)(2,1)S(1)}, u32[]{:S(2)}, u32[]{:S(2)}) %all-to-all-start.5) | async-done | bytes 393248 | tf_op jit(solution)/shard_map/all_to_all | solution.py:34
  205.4 8.5 %collective-permute-start.5 = (f32[2,96,64]{2,1,0:T(8,128)S(1)}, f32[2,96,64]{2,1,0:T(8,128)S(1)}, u32[]{:S(2)}, u32[]{:S(2)}) collective-permute-start(f32[2,96,64]{2,1,0:T(8,128)S(1)} %get-tuple-element.33), channel_id=1, source_target_pairs={{0,1},{1,0},{2,3},{3,2},{4,5},{5,4},{6,7},{7,6},{8,9},{9,8},{10,11... | collective-permute-start | bytes 147464 | tf_op jit(solution)/shard_map/ppermute | solution.py:40
  (102 shorter events, 38.8 us)
Async XLA Ops:
  3.5 9.6 %collective-permute-start.2 = (bf16[2,96,64]{1,2,0:T(8,128)(2,1)S(1)}, bf16[2,96,64]{1,2,0:T(8,128)(2,1)S(1)}, u32[]{:S(2)}, u32[]{:S(2)}) collective-permute-start(bf16[2,96,64]{1,2,0:T(8,128)(2,1)S(1)} %bitcast.224), channel_id=1, source_target_pairs={{0,1},{1,0},{2,3},{3,2},{4,5},{5,4},{6,7},{7,6},{8,9},{9,8},{10,11... | collective-permute-start | bytes 73736 | tf_op jit(solution)/shard_map/ppermute | solution.py:40
  42.5 4.3 %copy-start.7 = (bf16[224,1024]{1,0:T(8,128)(2,1)S(1)}, bf16[224,1024]{1,0:T(8,128)(2,1)}, u32[]{:S(2)}) copy-start(bf16[224,1024]{1,0:T(8,128)(2,1)} %param.11) | copy-start | bytes 1376260
  42.5 21.8 %all-to-all-start.1 = ((bf16[4,8,2,96,128]{4,3,1,2,0:T(8,128)(2,1)}), bf16[4,8,2,96,128]{4,3,1,2,0:T(8,128)(2,1)S(1)}, u32[]{:S(2)}, u32[]{:S(2)}) async-start(bf16[4,8,2,96,128]{4,3,1,2,0:T(8,128)(2,1)} %broadcast_in_dim.7), calls=%async_computation.1 | async-start | bytes 3145728 | tf_op jit(solution)/shard_map/all_to_all | solution.py:37
  46.8 9.5 %collective-permute-start.1 = (bf16[224,1024]{1,0:T(8,128)(2,1)S(1)}, bf16[224,1024]{1,0:T(8,128)(2,1)S(1)}, u32[]{:S(2)}, u32[]{:S(2)}) collective-permute-start(bf16[224,1024]{1,0:T(8,128)(2,1)S(1)} %copy-done.7), channel_id=1, source_target_pairs={{0,1},{1,0},{2,3},{3,2},{4,5},{5,4},{6,7},{7,6},{8,9},{9,8},{10,11... | collective-permute-start | bytes 1376264 | tf_op jit(solution)/shard_map/ppermute | solution.py:40
  52.0 4.7 %collective-permute-start = (bf16[224,1024]{1,0:T(8,128)(2,1)}, bf16[224,1024]{1,0:T(8,128)(2,1)S(1)}, u32[]{:S(2)}, u32[]{:S(2)}) collective-permute-start(bf16[224,1024]{1,0:T(8,128)(2,1)} %param.13), channel_id=1, source_target_pairs={{0,1},{1,0},{2,3},{3,2},{4,5},{5,4},{6,7},{7,6},{8,9},{9,8},{10,11... | collective-permute-start | bytes 1376264 | tf_op jit(solution)/shard_map/ppermute | solution.py:40
  53.9 5.3 %collective-permute-start.3 = (bf16[224,1024]{1,0:T(8,128)(2,1)}, bf16[224,1024]{1,0:T(8,128)(2,1)S(1)}, u32[]{:S(2)}, u32[]{:S(2)}) collective-permute-start(bf16[224,1024]{1,0:T(8,128)(2,1)} %param.12), channel_id=1, source_target_pairs={{0,1},{1,0},{2,3},{3,2},{4,5},{5,4},{6,7},{7,6},{8,9},{9,8},{10,11... | collective-permute-start | bytes 1376264 | tf_op jit(solution)/shard_map/ppermute | solution.py:40
  56.7 8.5 %copy-start = (bf16[56,8,8,128]{3,2,1,0:T(8,128)(2,1)}, bf16[56,8,8,128]{3,2,1,0:T(8,128)(2,1)S(1)}, u32[]{:S(2)}) copy-start(bf16[56,8,8,128]{3,2,1,0:T(8,128)(2,1)S(1)} %copy.166) | copy-start | bytes 2752516
  65.1 1.2 copy-start.2
  81.7 16.1 %collective-permute-start.4 = (bf16[3,112,384]{2,1,0:T(8,128)(2,1)S(1)}, bf16[3,112,384]{2,1,0:T(8,128)(2,1)S(1)}, u32[]{:S(2)}, u32[]{:S(2)}) collective-permute-start(bf16[3,112,384]{2,1,0:T(8,128)(2,1)S(1)} %convert_element_type.37), channel_id=1, source_target_pairs={{0,64},{64,0},{128,192},{192,128},{256,320},{320,256},{384,448},{4... | collective-permute-start | bytes 774152 | tf_op jit(solution)/shard_map/ppermute | solution.py:79
  123.4 2.0 copy-start.3
  123.5 2.0 copy-start.10
  128.5 23.2 %all-to-all-start.4 = ((bf16[4,8,2,96,128]{4,3,1,2,0:T(8,128)(2,1)}), bf16[4,8,2,96,128]{4,3,1,2,0:T(8,128)(2,1)}, u32[]{:S(2)}, u32[]{:S(2)}) async-start(bf16[4,8,2,96,128]{4,3,1,2,0:T(8,128)(2,1)} %copy.117), calls=%async_computation.4 | async-start | bytes 3145728 | tf_op jit(solution)/shard_map/all_to_all | solution.py:37
  132.9 13.7 %copy-start.12 = (f32[64,192]{1,0:T(8,128)S(1)}, f32[64,192]{1,0:T(8,128)}, u32[]{:S(2)}) copy-start(f32[64,192]{1,0:T(8,128)} %param.9) | copy-start | bytes 147460
  132.9 14.4 %copy-start.11 = (f32[64,192]{1,0:T(8,128)S(1)}, f32[64,192]{1,0:T(8,128)}, u32[]{:S(2)}) copy-start(f32[64,192]{1,0:T(8,128)} %param.8) | copy-start | bytes 147460
  134.2 59.3 %collective-permute-start.7 = (bf16[4,8,2,96,128]{4,3,0,1,2:T(8,128)(2,1)}, bf16[4,8,2,96,128]{4,3,0,1,2:T(8,128)(2,1)}, u32[]{:S(2)}, u32[]{:S(2)}) collective-permute-start(bf16[4,8,2,96,128]{4,3,0,1,2:T(8,128)(2,1)} %copy.104), channel_id=1, source_target_pairs={{0,1},{1,0},{2,3},{3,2},{4,5},{5,4},{6,7},{7,6},{8,9},{9,8},{10,11... | collective-permute-start | bytes 4718600 | tf_op jit(solution)/shard_map/ppermute | solution.py:40
  149.8 42.1 %collective-permute-start.6 = (bf16[3,224,384]{2,1,0:T(8,128)(2,1)}, bf16[3,224,384]{2,1,0:T(8,128)(2,1)}, u32[]{:S(2)}, u32[]{:S(2)}) collective-permute-start(bf16[3,224,384]{2,1,0:T(8,128)(2,1)} %slice.117), channel_id=1, source_target_pairs={{0,1},{1,0},{2,3},{3,2},{4,5},{5,4},{6,7},{7,6},{8,9},{9,8},{10,11... | collective-permute-start | bytes 1548296 | tf_op jit(solution)/shard_map/ppermute | solution.py:40
  154.2 34.1 %copy-start.6 = (bf16[1,224,384]{2,1,0:T(8,128)(2,1)S(1)}, bf16[1,224,384]{2,1,0:T(8,128)(2,1)}, u32[]{:S(2)}) copy-start(bf16[1,224,384]{2,1,0:T(8,128)(2,1)} %get-tuple-element.16) | copy-start | bytes 516100
  154.2 34.2 %copy-start.5 = (bf16[1,224,384]{2,1,0:T(8,128)(2,1)S(1)}, bf16[1,224,384]{2,1,0:T(8,128)(2,1)}, u32[]{:S(2)}) copy-start(bf16[1,224,384]{2,1,0:T(8,128)(2,1)} %get-tuple-element.17) | copy-start | bytes 516100
  154.2 51.1 %all-to-all-start.5 = ((bf16[8,2,96,128]{3,2,1,0:T(8,128)(2,1)}), bf16[8,2,96,128]{3,2,1,0:T(8,128)(2,1)S(1)}, u32[]{:S(2)}, u32[]{:S(2)}) async-start(bf16[8,2,96,128]{3,2,1,0:T(8,128)(2,1)} %copy.119), calls=%async_computation.5 | async-start | bytes 786432 | tf_op jit(solution)/shard_map/all_to_all | solution.py:34
  189.2 1.4 copy-start.13
  193.4 2.1 copy-start.4
  205.4 11.2 %collective-permute-start.5 = (f32[2,96,64]{2,1,0:T(8,128)S(1)}, f32[2,96,64]{2,1,0:T(8,128)S(1)}, u32[]{:S(2)}, u32[]{:S(2)}) collective-permute-start(f32[2,96,64]{2,1,0:T(8,128)S(1)} %get-tuple-element.33), channel_id=1, source_target_pairs={{0,1},{1,0},{2,3},{3,2},{4,5},{5,4},{6,7},{7,6},{8,9},{9,8},{10,11... | collective-permute-start | bytes 147464 | tf_op jit(solution)/shard_map/ppermute | solution.py:40
  215.5 1.1 copy-start.8
  215.5 1.1 copy-start.9
  (1 other events, 1.0 us)

commit v2 on v1

v2 whole, which is shorter than its diff:
```python
import jax
import jax.numpy as jnp
from jax import lax
from jax.sharding import PartitionSpec as P

momentum = 0.5
BF = jnp.bfloat16
F32 = jnp.float32


def copies(block, count):
    return jnp.broadcast_to(block[None], (count,) + block.shape)


def dot(left, right, left_dim, right_dim):
    return lax.dot_general(
        left, right, (((left_dim,), (right_dim,)), ((), ())), preferred_element_type=F32
    )


def nonlinear(gate, up_val, d_act):
    sig = jax.nn.sigmoid(gate)
    act = (gate * sig * up_val).astype(BF)
    d_gate = (d_act * up_val * sig * (1.0 + gate * (1.0 - sig))).astype(BF)
    d_up = (d_act * gate * sig).astype(BF)
    return jnp.stack([act, d_gate, d_up])


def make(depth, rows, cols):
    count_x, count_z = depth // 2, cols // 2
    x_groups = [[2 * x + h for x in range(count_x)] for h in range(2)]
    z_groups = [[2 * z + k for z in range(count_z)] for k in range(2)]
    swap_core = [(c, c ^ 1) for c in range(cols)]
    swap_half = [(d, d ^ 1) for d in range(depth)]

    def over_x(blocks):
        return lax.all_to_all(blocks, "depth", 0, 0, axis_index_groups=x_groups)

    def over_z(blocks):
        return lax.all_to_all(blocks, "col", 0, 0, axis_index_groups=z_groups)

    def over_row(blocks):
        return lax.all_to_all(blocks, "row", 0, 0)

    def other_core(block):
        return lax.ppermute(block, "col", swap_core)

    def other_half(block):
        return lax.ppermute(block, "depth", swap_half)

    def on_device(x_out, v_out, dx_out, dv_out, gate_weight, up_weight, down_weight):
        feats, toks = x_out.shape
        half = toks // 2
        hid = gate_weight.shape[0]
        part = 2 * hid // count_x
        tokens = rows * half
        wide = count_z * 2 * feats
        first = lax.axis_index("col") % 2 == 0

        def pick(one, two):
            return jnp.where(first, one, two)

        x_prev = x_out - v_out
        x_half = x_prev.astype(BF)
        df_half = ((1.0 - momentum) * (dx_out + dv_out)).astype(BF)
        both = jnp.stack([x_half.T, df_half.T]).reshape(2, 2, half, feats)
        mine = pick(both[:, 0], both[:, 1])
        theirs = other_core(pick(both[:, 1], both[:, 0]))
        block = pick(
            jnp.concatenate([mine, theirs], -1), jnp.concatenate([theirs, mine], -1)
        )
        block, gate_weight, up_weight, down_weight = lax.optimization_barrier(
            (block, gate_weight, up_weight, down_weight)
        )

        gate_w = jnp.concatenate([gate_weight, other_core(gate_weight)])
        up_w = jnp.concatenate([up_weight, other_core(up_weight)])
        down_w = jnp.concatenate([down_weight, other_core(down_weight)])

        along_z = jnp.swapaxes(over_z(copies(block, count_z)), 0, 1)
        inputs = over_row(copies(along_z, rows))

        def matrix(which):
            return jnp.swapaxes(inputs[:, which], 1, 2).reshape(tokens, wide)

        x_mat, df_mat = matrix(0), matrix(1)

        def hidden_part(weight, mat):
            return dot(weight, mat, 1, 1).astype(BF).reshape(count_x, 1, part, tokens)

        parts = jnp.concatenate(
            [hidden_part(gate_w, x_mat), hidden_part(up_w, x_mat), hidden_part(down_w, df_mat)], 1
        )
        sums = over_x(parts).astype(F32).sum(0)
        sums = sums + other_half(sums.astype(BF)).astype(F32)
        hidden = over_x(copies(nonlinear(sums[0], sums[1], sums[2]), count_x))
        act, d_gate, d_up = [hidden[:, i].reshape(2 * hid, tokens) for i in range(3)]

        y_part = dot(act, down_w, 0, 0)
        dx_part = dot(d_gate, gate_w, 0, 0) + dot(d_up, up_w, 0, 0)

        def blocks_of(total):
            blocks = total.astype(BF).reshape(rows, half, count_z, 2 * feats)
            return jnp.swapaxes(blocks, 1, 2)

        terms = jnp.stack([blocks_of(y_part), blocks_of(dx_part)], 2)
        terms = over_row(terms).astype(F32).sum(0).astype(BF)
        terms = over_z(terms).astype(F32).sum(0)
        low, high = terms[..., :feats], terms[..., feats:]
        theirs = other_core(pick(high, low))
        mine = pick(low, high)
        done = pick(jnp.concatenate([mine, theirs], 1), jnp.concatenate([theirs, mine], 1))
        v_prev = (v_out - (1.0 - momentum) * done[0].T) / momentum
        dx_prev = dx_out + done[1].T

        x_far, df_far = other_core(x_mat), other_core(df_mat)
        hidden_far = other_core(hidden[count_x // 2 :])

        def gradient(which, near, far):
            mine = hidden[: count_x // 2, which].reshape(hid, tokens)
            theirs = hidden_far[:, which].reshape(hid, tokens)
            return dot(mine, near, 1, 0) + dot(theirs, far, 1, 0)

        grad_down = gradient(0, df_mat, df_far)
        grad_gate = gradient(1, x_mat, x_far)
        grad_up = gradient(2, x_mat, x_far)
        return (x_prev, v_prev, dx_prev, grad_gate, grad_up, grad_down)

    return on_device


def solution(mesh):
    tokens = P(("depth", "col"), "row")
    weights = P(("col", "row"), "depth")
    return jax.shard_map(
        make(mesh.shape["depth"], mesh.shape["row"], mesh.shape["col"]),
        mesh=mesh,
        in_specs=(tokens,) * 4 + (weights,) * 3,
        out_specs=(tokens,) * 3 + (weights,) * 3,
        check_vma=False,
    )
```

time: 219 us -> 209 us (0.954)
  local copies, waits for them, and re-layouts: 31.2 us -> 12.6 us
  waiting for transfers between devices: 19.4 us -> 24.7 us
  starting transfers between devices: 91.3 us -> 96 us
    another operation x8 -> x2, local copies, waits for them, and re-layouts: 13.6 us -> 0.11 us  [on_device(): terms = jnp.stack([blocks_of(y_part), blocks_of(dx_part)], 2)]
    ppermute x7 -> x8, starting transfers between devices: 41.1 us -> 45.5 us  [other_core(): return lax.ppermute(block, 'col', swap_core)]
    all_to_all x2, waiting for transfers between devices: 3.71 us -> 6.82 us  [over_row(): return lax.all_to_all(blocks, 'row', 0, 0)]
    slice x11 -> x5, local copies, waits for them, and re-layouts: 5.47 us -> 2.5 us  [the longest x1 1.48 us: matrix(): return jnp.swapaxes(inputs[:, which], 1, 2).reshape(tokens, wide)]
    unnamed x3 -> x0, other arithmetic: 2.55 us -> none
    reshape x2 -> x0, local copies, waits for them, and re-layouts: 2.5 us -> none  [gradient(): return total.reshape(hid, count_z * 2 * feats)]
    unnamed x38 -> x39, local copies, waits for them, and re-layouts: 5.47 us -> 6.08 us
  transfers between devices with their start and end apart: 11 -> 12, of which waited for: 4 -> 6; matrix products, arithmetic and copies ran while one was open for 11% -> 8% of each run, Pallas kernels for 0% -> 0%
where the time goes in v2:
time: 209 us; the launch traced here: 208 us
  starting transfers between devices  96 us (46%)
  blocking collectives  54.3 us (26%)
  waiting for transfers between devices  24.7 us (12%)
  local copies, waits for them, and re-layouts  12.6 us (6%)
  matrix products  11.1 us (5%)
  other arithmetic  8.07 us (4%)
    ppermute x8, starting transfers between devices, other_core(): return lax.ppermute(block, 'col', swap_core)  45.5 us
    all_to_all x1, starting transfers between devices, over_z(): return lax.all_to_all(blocks, 'col', 0, 0, axis_index_groups=z_groups)  33.6 us
    all_to_all x1, blocking collectives, over_z(): return lax.all_to_all(blocks, 'col', 0, 0, axis_index_groups=z_groups)  27.7 us
    all_to_all x2, blocking collectives, over_x(): return lax.all_to_all(blocks, 'depth', 0, 0, axis_index_groups=x_groups)  26.6 us
    dot_general x12, matrix products, dot(): lax.dot_general(left, right, (((left_dim,), (right_dim,)), ((), ())), pre...  11.1 us
    all_to_all x2, starting transfers between devices, over_row(): return lax.all_to_all(blocks, 'row', 0, 0)  8.96 us
    ppermute x1, waiting for transfers between devices, other_half(): return lax.ppermute(block, 'depth', swap_half)  8.14 us
    ppermute x1, starting transfers between devices, other_half(): return lax.ppermute(block, 'depth', swap_half)  7.94 us
  transfers between devices with their start and end apart: 12, of which 6 were waited for; matrix products, arithmetic and copies ran while one was open for 8% of the time, Pallas kernels for 0%

profile of v2, /device:TPU:1, one launch (start us, length us, event | category | flops | bytes accessed | tf_op | source)
XLA Modules:
  0.0 208.0 jit_solution(9957223132305568188)
XLA Ops:
  0.6 1.5 convert_bitcast_fusion
  3.5 8.8 %collective-permute-start = (bf16[2,96,64]{1,2,0:T(8,128)(2,1)S(1)}, bf16[2,96,64]{1,2,0:T(8,128)(2,1)S(1)}, u32[]{:S(2)}, u32[]{:S(2)}) collective-permute-start(bf16[2,96,64]{1,2,0:T(8,128)(2,1)S(1)} %bitcast.131), channel_id=1, source_target_pairs={{0,1},{1,0},{2,3},{3,2},{4,5},{5,4},{6,7},{7,6},{8,9},{9,8},{10,11... | collective-permute-start | bytes 73736 | tf_op jit(solution)/shard_map/ppermute | solution.py:46
  13.3 27.7 %all_to_all.30 = bf16[8,2,96,128]{3,2,1,0:T(8,128)(2,1)S(1)} all-to-all(bf16[8,2,96,128]{3,2,1,0:T(8,128)(2,1)S(1)} %broadcast_in_dim.6), channel_id=1, replica_groups={{0,2,4,6,8,10,12,14},{1,3,5,7,9,11,13,15},{16,18,20,22,24,26,28,30},{17..., dimensions={0} | all-to-all | bytes 786432 | tf_op jit(solution)/shard_map/all_to_all | solution.py:40
  42.6 4.5 %all-to-all-start.1 = ((bf16[4,2,8,96,128]{4,2,3,1,0:T(8,128)(2,1)}), bf16[4,2,8,96,128]{4,2,3,1,0:T(8,128)(2,1)}, u32[]{:S(2)}, u32[]{:S(2)}) async-start(bf16[4,2,8,96,128]{4,2,3,1,0:T(8,128)(2,1)} %broadcast_in_dim.7), calls=%async_computation.1 | async-start | bytes 3145728 | tf_op jit(solution)/shard_map/all_to_all | solution.py:43
  47.2 5.0 %collective-permute-start.3 = (bf16[224,1024]{1,0:T(8,128)(2,1)S(1)}, bf16[224,1024]{1,0:T(8,128)(2,1)S(1)}, u32[]{:S(2)}, u32[]{:S(2)}) collective-permute-start(bf16[224,1024]{1,0:T(8,128)(2,1)S(1)} %copy-done.6), channel_id=1, source_target_pairs={{0,1},{1,0},{2,3},{3,2},{4,5},{5,4},{6,7},{7,6},{8,9},{9,8},{10,11... | collective-permute-start | bytes 1376264 | tf_op jit(solution)/shard_map/ppermute | solution.py:46
  52.2 1.9 collective-permute-start.2
  54.1 2.4 %collective-permute-start.1 = (bf16[224,1024]{1,0:T(8,128)(2,1)S(1)}, bf16[224,1024]{1,0:T(8,128)(2,1)S(1)}, u32[]{:S(2)}, u32[]{:S(2)}) collective-permute-start(bf16[224,1024]{1,0:T(8,128)(2,1)S(1)} %copy-done.5), channel_id=1, source_target_pairs={{0,1},{1,0},{2,3},{3,2},{4,5},{5,4},{6,7},{7,6},{8,9},{9,8},{10,11... | collective-permute-start | bytes 1376264 | tf_op jit(solution)/shard_map/ppermute | solution.py:46
  58.0 6.8 %all-to-all-done.1 = bf16[4,2,8,96,128]{4,2,3,1,0:T(8,128)(2,1)} async-done(((bf16[4,2,8,96,128]{4,2,3,1,0:T(8,128)(2,1)}), bf16[4,2,8,96,128]{4,2,3,1,0:T(8,128)(2,1)}, u32[]{:S(2)}, u32[]{:S(2)}) %all-to-all-start.1) | async-done | bytes 1572896 | tf_op jit(solution)/shard_map/all_to_all | solution.py:43
  64.8 1.5 fusion.10
  69.0 14.4 %all_to_all.31 = bf16[4,3,112,384]{3,2,1,0:T(8,128)(2,1)S(1)} all-to-all(bf16[4,3,112,384]{3,2,1,0:T(8,128)(2,1)S(1)} %pad_maximum_fusion.1), channel_id=1, replica_groups={{0,128,256,384},{64,192,320,448},{1,129,257,385},{65,193,321,449},{2,13..., dimensions={0} | all-to-all | bytes 2064384 | tf_op jit(solution)/shard_map/all_to_all | solution.py:37
  83.6 7.9 %collective-permute-start.4 = (bf16[3,112,384]{2,1,0:T(8,128)(2,1)S(1)}, bf16[3,112,384]{2,1,0:T(8,128)(2,1)S(1)}, u32[]{:S(2)}, u32[]{:S(2)}) collective-permute-start(bf16[3,112,384]{2,1,0:T(8,128)(2,1)S(1)} %convert_element_type.53), channel_id=1, source_target_pairs={{0,64},{64,0},{128,192},{192,128},{256,320},{320,256},{384,448},{4... | collective-permute-start | bytes 774152 | tf_op jit(solution)/shard_map/ppermute | solution.py:49
  91.5 8.1 %collective-permute-done.4 = bf16[3,112,384]{2,1,0:T(8,128)(2,1)S(1)} collective-permute-done((bf16[3,112,384]{2,1,0:T(8,128)(2,1)S(1)}, bf16[3,112,384]{2,1,0:T(8,128)(2,1)S(1)}, u32[]{:S(2)}, u32[]{:S(2)}) %collective-permute-start.4) | collective-permute-done | bytes 258080 | tf_op jit(solution)/shard_map/ppermute | solution.py:49
  100.0 12.2 %all_to_all.32 = bf16[4,3,112,384]{3,2,1,0:T(8,128)(2,1)S(1)} all-to-all(bf16[4,3,112,384]{3,2,1,0:T(8,128)(2,1)S(1)} %broadcast_in_dim.8), channel_id=1, replica_groups={{0,128,256,384},{64,192,320,448},{1,129,257,385},{65,193,321,449},{2,13..., dimensions={0} | all-to-all | bytes 2064384 | tf_op jit(solution)/shard_map/all_to_all | solution.py:37
  115.9 4.5 %all-to-all-start.4 = ((bf16[4,8,2,96,128]{4,1,3,2,0:T(8,128)(2,1)}), bf16[4,8,2,96,128]{4,1,3,2,0:T(8,128)(2,1)}, u32[]{:S(2)}, u32[]{:S(2)}) async-start(bf16[4,8,2,96,128]{4,1,3,2,0:T(8,128)(2,1)} %pad_maximum_fusion), calls=%async_computation.4 | async-start | bytes 3145728 | tf_op jit(solution)/shard_map/all_to_all | solution.py:43
  124.0 12.1 %collective-permute-start.7 = (bf16[384,1024]{1,0:T(8,128)(2,1)}, bf16[384,1024]{1,0:T(8,128)(2,1)S(1)}, u32[]{:S(2)}, u32[]{:S(2)}) collective-permute-start(bf16[384,1024]{1,0:T(8,128)(2,1)} %bitcast.102), channel_id=1, source_target_pairs={{0,1},{1,0},{2,3},{3,2},{4,5},{5,4},{6,7},{7,6},{8,9},{9,8},{10,11... | collective-permute-start | bytes 2359304 | tf_op jit(solution)/shard_map/ppermute | solution.py:46
  136.1 1.9 collective-permute-start.8
  138.8 2.5 %reduce_sum.31 = bf16[8,2,96,128]{3,0,2,1:T(8,128)(2,1)} reduce(bf16[4,8,2,96,128]{4,1,3,2,0:T(8,128)(2,1)} %all-to-all-done.4, bf16[]{:T(256)} %constant.26.clone.1), dimensions={0}, to_apply=%region_1.2 | reduce | flops 589824 | bytes 1966082 | tf_op jit(solution)/shard_map/reduce_sum | solution.py:107
  141.3 1.8 copy.34
  143.1 33.6 %all-to-all-start.5 = ((bf16[8,2,96,128]{3,2,1,0:T(8,128)(2,1)}), bf16[8,2,96,128]{3,2,1,0:T(8,128)(2,1)}, u32[]{:S(2)}, u32[]{:S(2)}) async-start(bf16[8,2,96,128]{3,2,1,0:T(8,128)(2,1)} %copy.34), calls=%async_computation.5 | async-start | bytes 786432 | tf_op jit(solution)/shard_map/all_to_all | solution.py:40
  176.8 1.4 fusion.9
  178.2 4.8 %collective-permute-start.6 = (bf16[2,3,112,384]{3,2,1,0:T(8,128)(2,1)S(1)}, bf16[2,3,112,384]{3,2,1,0:T(8,128)(2,1)S(1)}, u32[]{:S(2)}, u32[]{:S(2)}) collective-permute-start(bf16[2,3,112,384]{3,2,1,0:T(8,128)(2,1)S(1)} %slice.101), channel_id=1, source_target_pairs={{0,1},{1,0},{2,3},{3,2},{4,5},{5,4},{6,7},{7,6},{8,9},{9,8},{10,11... | collective-permute-start | bytes 1548296 | tf_op jit(solution)/shard_map/ppermute | solution.py:46
  187.2 7.1 %all-to-all-done.5 = bf16[8,2,96,128]{3,2,1,0:T(8,128)(2,1)} async-done(((bf16[8,2,96,128]{3,2,1,0:T(8,128)(2,1)}), bf16[8,2,96,128]{3,2,1,0:T(8,128)(2,1)}, u32[]{:S(2)}, u32[]{:S(2)}) %all-to-all-start.5) | async-done | bytes 393248 | tf_op jit(solution)/shard_map/all_to_all | solution.py:40
  195.5 8.5 %collective-permute-start.5 = (f32[2,96,64]{2,1,0:T(8,128)S(1)}, f32[2,96,64]{2,1,0:T(8,128)S(1)}, u32[]{:S(2)}, u32[]{:S(2)}) collective-permute-start(f32[2,96,64]{2,1,0:T(8,128)S(1)} %get-tuple-element.39), channel_id=1, source_target_pairs={{0,1},{1,0},{2,3},{3,2},{4,5},{5,4},{6,7},{7,6},{8,9},{9,8},{10,11... | collective-permute-start | bytes 147464 | tf_op jit(solution)/shard_map/ppermute | solution.py:46
  204.0 2.5 %convolution_add_fusion = f32[224,1024]{1,0:T(8,128)} fusion(f32[224,1024]{1,0:T(8,128)S(1)} %fusion.7, bf16[224,384]{1,0:T(8,128)(2,1)S(1)} %bitcast.123, bf16[384,1024]{1,0:T(8,128)(2,1)} %collective-permute-done.8), kind=kOutput, calls=%fused_computation.4 | convolution fusion | flops 176390144 | bytes 2793472 | tf_op jit(solution)/shard_map/dot_general | solution.py:16
  (89 shorter events, 23.4 us)
Async XLA Ops:
  3.5 9.6 %collective-permute-start = (bf16[2,96,64]{1,2,0:T(8,128)(2,1)S(1)}, bf16[2,96,64]{1,2,0:T(8,128)(2,1)S(1)}, u32[]{:S(2)}, u32[]{:S(2)}) collective-permute-start(bf16[2,96,64]{1,2,0:T(8,128)(2,1)S(1)} %bitcast.131), channel_id=1, source_target_pairs={{0,1},{1,0},{2,3},{3,2},{4,5},{5,4},{6,7},{7,6},{8,9},{9,8},{10,11... | collective-permute-start | bytes 73736 | tf_op jit(solution)/shard_map/ppermute | solution.py:46
  42.6 4.5 %copy-start.6 = (bf16[224,1024]{1,0:T(8,128)(2,1)S(1)}, bf16[224,1024]{1,0:T(8,128)(2,1)}, u32[]{:S(2)}) copy-start(bf16[224,1024]{1,0:T(8,128)(2,1)} %param.13) | copy-start | bytes 1376260
  42.6 9.5 %copy-start.4 = (bf16[224,1024]{1,0:T(8,128)(2,1)S(1)}, bf16[224,1024]{1,0:T(8,128)(2,1)}, u32[]{:S(2)}) copy-start(bf16[224,1024]{1,0:T(8,128)(2,1)} %param.12) | copy-start | bytes 1376260
  42.6 11.4 %copy-start.5 = (bf16[224,1024]{1,0:T(8,128)(2,1)S(1)}, bf16[224,1024]{1,0:T(8,128)(2,1)}, u32[]{:S(2)}) copy-start(bf16[224,1024]{1,0:T(8,128)(2,1)} %param.11) | copy-start | bytes 1376260
  42.6 22.1 %all-to-all-start.1 = ((bf16[4,2,8,96,128]{4,2,3,1,0:T(8,128)(2,1)}), bf16[4,2,8,96,128]{4,2,3,1,0:T(8,128)(2,1)}, u32[]{:S(2)}, u32[]{:S(2)}) async-start(bf16[4,2,8,96,128]{4,2,3,1,0:T(8,128)(2,1)} %broadcast_in_dim.7), calls=%async_computation.1 | async-start | bytes 3145728 | tf_op jit(solution)/shard_map/all_to_all | solution.py:43
  47.2 9.5 %collective-permute-start.3 = (bf16[224,1024]{1,0:T(8,128)(2,1)S(1)}, bf16[224,1024]{1,0:T(8,128)(2,1)S(1)}, u32[]{:S(2)}, u32[]{:S(2)}) collective-permute-start(bf16[224,1024]{1,0:T(8,128)(2,1)S(1)} %copy-done.6), channel_id=1, source_target_pairs={{0,1},{1,0},{2,3},{3,2},{4,5},{5,4},{6,7},{7,6},{8,9},{9,8},{10,11... | collective-permute-start | bytes 1376264 | tf_op jit(solution)/shard_map/ppermute | solution.py:46
  52.2 4.5 %collective-permute-start.2 = (bf16[224,1024]{1,0:T(8,128)(2,1)S(1)}, bf16[224,1024]{1,0:T(8,128)(2,1)S(1)}, u32[]{:S(2)}, u32[]{:S(2)}) collective-permute-start(bf16[224,1024]{1,0:T(8,128)(2,1)S(1)} %copy-done.4), channel_id=1, source_target_pairs={{0,1},{1,0},{2,3},{3,2},{4,5},{5,4},{6,7},{7,6},{8,9},{9,8},{10,11... | collective-permute-start | bytes 1376264 | tf_op jit(solution)/shard_map/ppermute | solution.py:46
  54.1 3.8 %collective-permute-start.1 = (bf16[224,1024]{1,0:T(8,128)(2,1)S(1)}, bf16[224,1024]{1,0:T(8,128)(2,1)S(1)}, u32[]{:S(2)}, u32[]{:S(2)}) collective-permute-start(bf16[224,1024]{1,0:T(8,128)(2,1)S(1)} %copy-done.5), channel_id=1, source_target_pairs={{0,1},{1,0},{2,3},{3,2},{4,5},{5,4},{6,7},{7,6},{8,9},{9,8},{10,11... | collective-permute-start | bytes 1376264 | tf_op jit(solution)/shard_map/ppermute | solution.py:46
  56.7 1.3 copy-start.11
  56.7 9.5 %copy-start = (bf16[448,1024]{1,0:T(8,128)(2,1)}, bf16[448,1024]{1,0:T(8,128)(2,1)S(1)}, u32[]{:S(2)}) copy-start(bf16[448,1024]{1,0:T(8,128)(2,1)S(1)} %constant_dynamic-update-slice_fusion.4) | copy-start | bytes 2752516
  83.6 16.1 %collective-permute-start.4 = (bf16[3,112,384]{2,1,0:T(8,128)(2,1)S(1)}, bf16[3,112,384]{2,1,0:T(8,128)(2,1)S(1)}, u32[]{:S(2)}, u32[]{:S(2)}) collective-permute-start(bf16[3,112,384]{2,1,0:T(8,128)(2,1)S(1)} %convert_element_type.53), channel_id=1, source_target_pairs={{0,64},{64,0},{128,192},{192,128},{256,320},{320,256},{384,448},{4... | collective-permute-start | bytes 774152 | tf_op jit(solution)/shard_map/ppermute | solution.py:49
  100.0 12.3 %copy-start.1 = (bf16[448,1024]{1,0:T(8,128)(2,1)S(1)}, bf16[448,1024]{1,0:T(8,128)(2,1)}, u32[]{:S(2)}) copy-start(bf16[448,1024]{1,0:T(8,128)(2,1)} %copy-done) | copy-start | bytes 2752516
  115.9 4.5 %copy-start.10 = (f32[64,192]{1,0:T(8,128)S(1)}, f32[64,192]{1,0:T(8,128)}, u32[]{:S(2)}) copy-start(f32[64,192]{1,0:T(8,128)} %param.9) | copy-start | bytes 147460
  115.9 5.2 %copy-start.9 = (f32[64,192]{1,0:T(8,128)S(1)}, f32[64,192]{1,0:T(8,128)}, u32[]{:S(2)}) copy-start(f32[64,192]{1,0:T(8,128)} %param.8) | copy-start | bytes 147460
  115.9 23.0 %all-to-all-start.4 = ((bf16[4,8,2,96,128]{4,1,3,2,0:T(8,128)(2,1)}), bf16[4,8,2,96,128]{4,1,3,2,0:T(8,128)(2,1)}, u32[]{:S(2)}, u32[]{:S(2)}) async-start(bf16[4,8,2,96,128]{4,1,3,2,0:T(8,128)(2,1)} %pad_maximum_fusion), calls=%async_computation.4 | async-start | bytes 3145728 | tf_op jit(solution)/shard_map/all_to_all | solution.py:43
  124.0 60.6 %collective-permute-start.7 = (bf16[384,1024]{1,0:T(8,128)(2,1)}, bf16[384,1024]{1,0:T(8,128)(2,1)S(1)}, u32[]{:S(2)}, u32[]{:S(2)}) collective-permute-start(bf16[384,1024]{1,0:T(8,128)(2,1)} %bitcast.102), channel_id=1, source_target_pairs={{0,1},{1,0},{2,3},{3,2},{4,5},{5,4},{6,7},{7,6},{8,9},{9,8},{10,11... | collective-permute-start | bytes 2359304 | tf_op jit(solution)/shard_map/ppermute | solution.py:46
  136.1 67.9 %collective-permute-start.8 = (bf16[384,1024]{1,0:T(8,128)(2,1)}, bf16[384,1024]{1,0:T(8,128)(2,1)}, u32[]{:S(2)}, u32[]{:S(2)}) collective-permute-start(bf16[384,1024]{1,0:T(8,128)(2,1)} %bitcast.101), channel_id=1, source_target_pairs={{0,1},{1,0},{2,3},{3,2},{4,5},{5,4},{6,7},{7,6},{8,9},{9,8},{10,11... | collective-permute-start | bytes 2359304 | tf_op jit(solution)/shard_map/ppermute | solution.py:46
  143.1 51.2 %all-to-all-start.5 = ((bf16[8,2,96,128]{3,2,1,0:T(8,128)(2,1)}), bf16[8,2,96,128]{3,2,1,0:T(8,128)(2,1)}, u32[]{:S(2)}, u32[]{:S(2)}) async-start(bf16[8,2,96,128]{3,2,1,0:T(8,128)(2,1)} %copy.34), calls=%async_computation.5 | async-start | bytes 786432 | tf_op jit(solution)/shard_map/all_to_all | solution.py:40
  176.8 6.2 %copy-start.3 = (bf16[2,1,112,384]{3,2,1,0:T(8,128)(2,1)S(1)}, bf16[2,1,112,384]{3,2,1,0:T(8,128)(2,1)}, u32[]{:S(2)}) copy-start(bf16[2,1,112,384]{3,2,1,0:T(8,128)(2,1)} %get-tuple-element.25) | copy-start | bytes 516100
  178.1 5.3 %copy-start.2 = (bf16[2,1,112,384]{3,2,1,0:T(8,128)(2,1)S(1)}, bf16[2,1,112,384]{3,2,1,0:T(8,128)(2,1)}, u32[]{:S(2)}) copy-start(bf16[2,1,112,384]{3,2,1,0:T(8,128)(2,1)} %get-tuple-element.24) | copy-start | bytes 516100
  178.2 6.3 %collective-permute-start.6 = (bf16[2,3,112,384]{3,2,1,0:T(8,128)(2,1)S(1)}, bf16[2,3,112,384]{3,2,1,0:T(8,128)(2,1)S(1)}, u32[]{:S(2)}, u32[]{:S(2)}) collective-permute-start(bf16[2,3,112,384]{3,2,1,0:T(8,128)(2,1)S(1)} %slice.101), channel_id=1, source_target_pairs={{0,1},{1,0},{2,3},{3,2},{4,5},{5,4},{6,7},{7,6},{8,9},{9,8},{10,11... | collective-permute-start | bytes 1548296 | tf_op jit(solution)/shard_map/ppermute | solution.py:46
  195.5 11.1 %collective-permute-start.5 = (f32[2,96,64]{2,1,0:T(8,128)S(1)}, f32[2,96,64]{2,1,0:T(8,128)S(1)}, u32[]{:S(2)}, u32[]{:S(2)}) collective-permute-start(f32[2,96,64]{2,1,0:T(8,128)S(1)} %get-tuple-element.39), channel_id=1, source_target_pairs={{0,1},{1,0},{2,3},{3,2},{4,5},{5,4},{6,7},{7,6},{8,9},{9,8},{10,11... | collective-permute-start | bytes 147464 | tf_op jit(solution)/shard_map/ppermute | solution.py:46
  204.0 2.5 %copy-start.7 = (f32[64,192]{0,1:T(8,128)S(1)}, f32[64,192]{0,1:T(8,128)}, u32[]{:S(2)}) copy-start(f32[64,192]{0,1:T(8,128)} %copy.37) | copy-start | bytes 147460
  204.0 2.5 %copy-start.8 = (f32[64,192]{0,1:T(8,128)S(1)}, f32[64,192]{0,1:T(8,128)}, u32[]{:S(2)}) copy-start(f32[64,192]{0,1:T(8,128)} %copy.36) | copy-start | bytes 147460
  (1 other events, 1.2 us)

commit v3 on v2

--- a/solution.py
+++ b/solution.py
@@ -1,6 +1,8 @@
 import jax
 import jax.numpy as jnp
 from jax import lax
+from jax.experimental import pallas as pl
+from jax.experimental.pallas import tpu as pltpu
 from jax.sharding import PartitionSpec as P
 
 momentum = 0.5
@@ -26,6 +28,26 @@
     return jnp.stack([act, d_gate, d_up])
 
 
+def sum_kernel(in_ref, out_ref):
+    total = in_ref[0].astype(F32)
+    for row in range(1, in_ref.shape[0]):
+        total += in_ref[row].astype(F32)
+    for piece in range(out_ref.shape[0]):
+        out_ref[piece] = total[:, :, piece * 128 : (piece + 1) * 128].astype(BF)
+
+
+def sum_rows(terms, lanes=256):
+    rows, arrays, toks, wide = terms.shape
+    return pl.pallas_call(
+        sum_kernel,
+        grid=(wide // lanes,),
+        in_specs=[pl.BlockSpec((rows, arrays, toks, lanes), lambda i: (0, 0, 0, i))],
+        out_specs=pl.BlockSpec((lanes // 128, arrays, toks, 128), lambda i: (i, 0, 0, 0)),
+        out_shape=jax.ShapeDtypeStruct((wide // 128, arrays, toks, 128), BF),
+        compiler_params=pltpu.CompilerParams(vmem_limit_bytes=32 * 1024 * 1024),
+    )(terms)
+
+
 def make(depth, rows, cols):
     count_x, count_z = depth // 2, cols // 2
     x_groups = [[2 * x + h for x in range(count_x)] for h in range(2)]
@@ -38,6 +60,18 @@
 
     def over_z(blocks):
         return lax.all_to_all(blocks, "col", 0, 0, axis_index_groups=z_groups)
+
+    def gather_z(block, place):
+        span = count_z // 2
+        pairs = [(c, (c + 2 * span) % cols) for c in range(cols)]
+        groups = [
+            [2 * (end * span + z) + k for z in range(span)] for end in range(2) for k in range(2)
+        ]
+        far = lax.ppermute(block, "col", pairs)
+        low = place < span
+        both = jnp.stack([jnp.where(low, block, far), jnp.where(low, far, block)])
+        both = lax.all_to_all(copies(both, span), "col", 0, 0, axis_index_groups=groups)
+        return jnp.swapaxes(both, 0, 1).reshape((count_z,) + block.shape)
 
     def over_row(blocks):
         return lax.all_to_all(blocks, "row", 0, 0)
@@ -77,7 +111,7 @@
         up_w = jnp.concatenate([up_weight, other_core(up_weight)])
         down_w = jnp.concatenate([down_weight, other_core(down_weight)])
 
-        along_z = jnp.swapaxes(over_z(copies(block, count_z)), 0, 1)
+        along_z = jnp.swapaxes(gather_z(block, lax.axis_index("col") // 2), 0, 1)
         inputs = over_row(copies(along_z, rows))
 
         def matrix(which):
@@ -100,19 +134,10 @@
         dx_part = dot(d_gate, gate_w, 0, 0) + dot(d_up, up_w, 0, 0)
 
         def blocks_of(total):
-            blocks = total.astype(BF).reshape(rows, half, count_z, 2 * feats)
-            return jnp.swapaxes(blocks, 1, 2)
+            return total.astype(BF).reshape(rows, half, wide)
 
-        terms = jnp.stack([blocks_of(y_part), blocks_of(dx_part)], 2)
-        terms = over_row(terms).astype(F32).sum(0).astype(BF)
-        terms = over_z(terms).astype(F32).sum(0)
-        low, high = terms[..., :feats], terms[..., feats:]
-        theirs = other_core(pick(high, low))
-        mine = pick(low, high)
-        done = pick(jnp.concatenate([mine, theirs], 1), jnp.concatenate([theirs, mine], 1))
-        v_prev = (v_out - (1.0 - momentum) * done[0].T) / momentum
-        dx_prev = dx_out + done[1].T
-
+        terms = sum_rows(over_row(jnp.stack([blocks_of(y_part), blocks_of(dx_part)], 1)))
+        terms = over_z(terms)
         x_far, df_far = other_core(x_mat), other_core(df_mat)
         hidden_far = other_core(hidden[count_x // 2 :])
 
@@ -124,6 +149,17 @@
         grad_down = gradient(0, df_mat, df_far)
         grad_gate = gradient(1, x_mat, x_far)
         grad_up = gradient(2, x_mat, x_far)
+        terms, grad_gate, grad_up, grad_down = lax.optimization_barrier(
+            (terms, grad_gate, grad_up, grad_down)
+        )
+        terms = terms.astype(F32).sum(0)
+        low, high = terms[..., :feats], terms[..., feats:]
+        theirs = other_core(pick(high, low))
+        mine = pick(low, high)
+        done = pick(jnp.concatenate([mine, theirs], 1), jnp.concatenate([theirs, mine], 1))
+        v_prev = (v_out - (1.0 - momentum) * done[0].T) / momentum
+        dx_prev = dx_out + done[1].T
+
         return (x_prev, v_prev, dx_prev, grad_gate, grad_up, grad_down)
 
     return on_device

time: 209 us -> 201 us (0.962)
  blocking collectives: 54.3 us -> 40.2 us
  waiting for transfers between devices: 24.7 us -> 29.7 us
  other arithmetic: 8.07 us -> 4.66 us
  matrix products: 11.1 us -> 14.3 us
  starting transfers between devices: 96 us -> 93.8 us
    all_to_all x1, blocking collectives: 27.7 us -> 13.7 us  [gather_z(): lax.all_to_all(copies(both, span), 'col', 0, 0, axis_index_groups=groups)]
    ppermute x0 -> x1, waiting for transfers between devices: none -> 8.11 us  [gather_z(): far = lax.ppermute(block, 'col', pairs)]
    all_to_all x1, starting transfers between devices: 33.6 us -> 28.7 us  [over_z(): return lax.all_to_all(blocks, 'col', 0, 0, axis_index_groups=z_groups)]
    ppermute x1, starting transfers between devices: 7.94 us -> 12.6 us  [other_half(): return lax.ppermute(block, 'depth', swap_half)]
    ppermute x1, waiting for transfers between devices: 8.14 us -> 4 us  [other_half(): return lax.ppermute(block, 'depth', swap_half)]
    ppermute x8, starting transfers between devices: 45.5 us -> 41.8 us  [other_core(): return lax.ppermute(block, 'col', swap_core)]
    reduce_sum x2 -> x1, other arithmetic: 3.55 us -> 0.05 us  [on_device(): terms = terms.astype(F32).sum(0)]
    ppermute x0 -> x1, starting transfers between devices: none -> 3.44 us  [gather_z(): far = lax.ppermute(block, 'col', pairs)]
  transfers between devices with their start and end apart: 12 -> 13, of which waited for: 6 -> 6; matrix products, arithmetic and copies ran while one was open for 8% -> 9% of each run, Pallas kernels for 0% -> 1%
where the time goes in v3:
time: 201 us; the launch traced here: 200 us
  starting transfers between devices  93.8 us (47%)
  blocking collectives  40.2 us (20%)
  waiting for transfers between devices  29.7 us (15%)
  matrix products  14.3 us (7%)
  local copies, waits for them, and re-layouts  14.2 us (7%)
  other arithmetic  4.66 us (2%)
    ppermute x8, starting transfers between devices, other_core(): return lax.ppermute(block, 'col', swap_core)  41.8 us
    all_to_all x1, starting transfers between devices, over_z(): return lax.all_to_all(blocks, 'col', 0, 0, axis_index_groups=z_groups)  28.7 us
    all_to_all x2, blocking collectives, over_x(): return lax.all_to_all(blocks, 'depth', 0, 0, axis_index_groups=x_groups)  26.5 us
    dot_general x12, matrix products, dot(): lax.dot_general(left, right, (((left_dim,), (right_dim,)), ((), ())), pre...  14.3 us
    all_to_all x1, blocking collectives, gather_z(): lax.all_to_all(copies(both, span), 'col', 0, 0, axis_index_groups=groups)  13.7 us
    ppermute x1, starting transfers between devices, other_half(): return lax.ppermute(block, 'depth', swap_half)  12.6 us
    unnamed x37, local copies, waits for them, and re-layouts  9.07 us
    all_to_all x1, waiting for transfers between devices, over_z(): return lax.all_to_all(blocks, 'col', 0, 0, axis_index_groups=z_groups)  8.29 us
  transfers between devices with their start and end apart: 13, of which 6 were waited for; matrix products, arithmetic and copies ran while one was open for 9% of the time, Pallas kernels for 1%

profile of v3, /device:TPU:1, one launch (start us, length us, event | category | flops | bytes accessed | tf_op | source)
XLA Modules:
  0.0 199.8 jit_solution(7348160709746597697)
XLA Ops:
  3.5 8.8 %collective-permute-start = (bf16[2,96,64]{1,2,0:T(8,128)(2,1)S(1)}, bf16[2,96,64]{1,2,0:T(8,128)(2,1)S(1)}, u32[]{:S(2)}, u32[]{:S(2)}) collective-permute-start(bf16[2,96,64]{1,2,0:T(8,128)(2,1)S(1)} %bitcast.121), channel_id=1, source_target_pairs={{0,1},{1,0},{2,3},{3,2},{4,5},{5,4},{6,7},{7,6},{8,9},{9,8},{10,11... | collective-permute-start | bytes 73736 | tf_op jit(solution)/shard_map/ppermute | solution.py:80
  13.1 3.4 %collective-permute-start.2 = (bf16[2,96,128]{1,2,0:T(8,128)(2,1)S(1)}, bf16[2,96,128]{1,2,0:T(8,128)(2,1)S(1)}, u32[]{:S(2)}, u32[]{:S(2)}) collective-permute-start(bf16[2,96,128]{1,2,0:T(8,128)(2,1)S(1)} %maximum_select_fusion.1), channel_id=1, source_target_pairs={{0,8},{1,9},{2,10},{3,11},{4,12},{5,13},{6,14},{7,15},{8,0},{9,1},... | collective-permute-start | bytes 147464 | tf_op jit(solution)/shard_map/ppermute | solution.py:70
  16.6 8.1 %collective-permute-done.2 = bf16[2,96,128]{1,2,0:T(8,128)(2,1)S(1)} collective-permute-done((bf16[2,96,128]{1,2,0:T(8,128)(2,1)S(1)}, bf16[2,96,128]{1,2,0:T(8,128)(2,1)S(1)}, u32[]{:S(2)}, u32[]{:S(2)}) %collective-permute-start.2) | collective-permute-done | bytes 49184 | tf_op jit(solution)/shard_map/ppermute | solution.py:70
  24.9 13.7 %all_to_all.30 = bf16[4,2,2,96,128]{4,3,2,1,0:T(8,128)(2,1)S(1)} all-to-all(bf16[4,2,2,96,128]{4,3,2,1,0:T(8,128)(2,1)S(1)} %broadcast_in_dim.6), channel_id=1, replica_groups={{0,2,4,6},{1,3,5,7},{8,10,12,14},{9,11,13,15},{16,18,20,22},{17,19,21,2..., dimensions={0} | all-to-all | bytes 786432 | tf_op jit(solution)/shard_map/all_to_all | solution.py:73
  40.3 3.7 %all-to-all-start.1 = ((bf16[4,2,8,96,128]{4,2,3,1,0:T(8,128)(2,1)}), bf16[4,2,8,96,128]{4,2,3,1,0:T(8,128)(2,1)S(1)}, u32[]{:S(2)}, u32[]{:S(2)}) async-start(bf16[4,2,8,96,128]{4,2,3,1,0:T(8,128)(2,1)} %broadcast_in_dim.7), calls=%async_computation.1 | async-start | bytes 3145728 | tf_op jit(solution)/shard_map/all_to_all | solution.py:77
  44.0 3.5 %collective-permute-start.4 = (bf16[224,1024]{1,0:T(8,128)(2,1)}, bf16[224,1024]{1,0:T(8,128)(2,1)S(1)}, u32[]{:S(2)}, u32[]{:S(2)}) collective-permute-start(bf16[224,1024]{1,0:T(8,128)(2,1)} %param.13), channel_id=1, source_target_pairs={{0,1},{1,0},{2,3},{3,2},{4,5},{5,4},{6,7},{7,6},{8,9},{9,8},{10,11... | collective-permute-start | bytes 1376264 | tf_op jit(solution)/shard_map/ppermute | solution.py:80
  47.6 1.9 collective-permute-start.3
  49.5 2.4 %collective-permute-start.1 = (bf16[224,1024]{1,0:T(8,128)(2,1)}, bf16[224,1024]{1,0:T(8,128)(2,1)S(1)}, u32[]{:S(2)}, u32[]{:S(2)}) collective-permute-start(bf16[224,1024]{1,0:T(8,128)(2,1)} %param.11), channel_id=1, source_target_pairs={{0,1},{1,0},{2,3},{3,2},{4,5},{5,4},{6,7},{7,6},{8,9},{9,8},{10,11... | collective-permute-start | bytes 1376264 | tf_op jit(solution)/shard_map/ppermute | solution.py:80
  55.4 7.7 %all-to-all-done.1 = bf16[4,2,8,96,128]{4,2,3,1,0:T(8,128)(2,1)S(1)} async-done(((bf16[4,2,8,96,128]{4,2,3,1,0:T(8,128)(2,1)}), bf16[4,2,8,96,128]{4,2,3,1,0:T(8,128)(2,1)S(1)}, u32[]{:S(2)}, u32[]{:S(2)}) %all-to-all-start.1) | async-done | bytes 1572896 | tf_op jit(solution)/shard_map/all_to_all | solution.py:77
  67.2 14.4 %all_to_all.31 = bf16[4,3,112,384]{3,2,1,0:T(8,128)(2,1)S(1)} all-to-all(bf16[4,3,112,384]{3,2,1,0:T(8,128)(2,1)S(1)} %pad_maximum_fusion.1), channel_id=1, replica_groups={{0,128,256,384},{64,192,320,448},{1,129,257,385},{65,193,321,449},{2,13..., dimensions={0} | all-to-all | bytes 2064384 | tf_op jit(solution)/shard_map/all_to_all | solution.py:59
  81.9 12.6 %collective-permute-start.5 = (bf16[3,112,384]{2,1,0:T(8,128)(2,1)S(1)}, bf16[3,112,384]{2,1,0:T(8,128)(2,1)S(1)}, u32[]{:S(2)}, u32[]{:S(2)}) collective-permute-start(bf16[3,112,384]{2,1,0:T(8,128)(2,1)S(1)} %convert_element_type.51), channel_id=1, source_target_pairs={{0,64},{64,0},{128,192},{192,128},{256,320},{320,256},{384,448},{4... | collective-permute-start | bytes 774152 | tf_op jit(solution)/shard_map/ppermute | solution.py:83
  94.5 4.0 %collective-permute-done.5 = bf16[3,112,384]{2,1,0:T(8,128)(2,1)S(1)} collective-permute-done((bf16[3,112,384]{2,1,0:T(8,128)(2,1)S(1)}, bf16[3,112,384]{2,1,0:T(8,128)(2,1)S(1)}, u32[]{:S(2)}, u32[]{:S(2)}) %collective-permute-start.5) | collective-permute-done | bytes 258080 | tf_op jit(solution)/shard_map/ppermute | solution.py:83
  98.8 12.1 %all_to_all.32 = bf16[4,3,112,384]{3,2,1,0:T(8,128)(2,1)S(1)} all-to-all(bf16[4,3,112,384]{3,2,1,0:T(8,128)(2,1)S(1)} %broadcast_in_dim.8), channel_id=1, replica_groups={{0,128,256,384},{64,192,320,448},{1,129,257,385},{65,193,321,449},{2,13..., dimensions={0} | all-to-all | bytes 2064384 | tf_op jit(solution)/shard_map/all_to_all | solution.py:59
  114.2 3.6 %all-to-all-start.4 = ((bf16[4,2,96,1024]{3,2,1,0:T(8,128)(2,1)}), bf16[4,2,96,1024]{3,2,1,0:T(8,128)(2,1)S(1)}, u32[]{:S(2)}, u32[]{:S(2)}) async-start(bf16[4,2,96,1024]{3,2,1,0:T(8,128)(2,1)} %pad_maximum_fusion), calls=%async_computation.4 | async-start | bytes 3145728 | tf_op jit(solution)/shard_map/all_to_all | solution.py:77
  120.0 12.3 %collective-permute-start.7 = (bf16[384,1024]{1,0:T(8,128)(2,1)}, bf16[384,1024]{1,0:T(8,128)(2,1)}, u32[]{:S(2)}, u32[]{:S(2)}) collective-permute-start(bf16[384,1024]{1,0:T(8,128)(2,1)} %bitcast.94), channel_id=1, source_target_pairs={{0,1},{1,0},{2,3},{3,2},{4,5},{5,4},{6,7},{7,6},{8,9},{9,8},{10,11... | collective-permute-start | bytes 2359304 | tf_op jit(solution)/shard_map/ppermute | solution.py:80
  132.3 1.9 collective-permute-start.8
  137.2 2.4 %collective-permute-start.6 = (bf16[2,3,112,384]{3,2,1,0:T(8,128)(2,1)}, bf16[2,3,112,384]{3,2,1,0:T(8,128)(2,1)}, u32[]{:S(2)}, u32[]{:S(2)}) collective-permute-start(bf16[2,3,112,384]{3,2,1,0:T(8,128)(2,1)} %slice.97), channel_id=1, source_target_pairs={{0,1},{1,0},{2,3},{3,2},{4,5},{5,4},{6,7},{7,6},{8,9},{9,8},{10,11... | collective-permute-start | bytes 1548296 | tf_op jit(solution)/shard_map/ppermute | solution.py:80
  140.9 1.6 shard_map.118
  142.5 28.7 %all-to-all-start.5 = ((bf16[8,2,96,128]{3,2,1,0:T(8,128)(2,1)}), bf16[8,2,96,128]{3,2,1,0:T(8,128)(2,1)S(1)}, u32[]{:S(2)}, u32[]{:S(2)}) async-start(bf16[8,2,96,128]{3,2,1,0:T(8,128)(2,1)} %shard_map.118), calls=%async_computation.5 | async-start | bytes 786432 | tf_op jit(solution)/shard_map/all_to_all | solution.py:62
  172.8 2.5 %convolution_add_fusion.2 = f32[224,1024]{1,0:T(8,128)} fusion(f32[224,1024]{1,0:T(8,128)S(1)} %copy-done.3, bf16[224,384]{1,0:T(8,128)(2,1)S(1)} %bitcast.115, bf16[384,1024]{1,0:T(8,128)(2,1)} %collective-permute-done.7), kind=kOutput, calls=%fused_computation.6 | convolution fusion | flops 176390144 | bytes 2793472 | tf_op jit(solution)/shard_map/dot_general | solution.py:18
  175.4 2.5 %convolution_add_fusion.1 = f32[224,1024]{1,0:T(8,128)} fusion(f32[224,1024]{1,0:T(8,128)S(1)} %copy-done.4, bf16[224,384]{1,0:T(8,128)(2,1)S(1)} %bitcast.114, bf16[384,1024]{1,0:T(8,128)(2,1)} %collective-permute-done.7), kind=kOutput, calls=%fused_computation.5 | convolution fusion | flops 176390144 | bytes 2793472 | tf_op jit(solution)/shard_map/dot_general | solution.py:18
  177.9 2.5 %convolution_add_fusion = f32[224,1024]{1,0:T(8,128)} fusion(f32[224,1024]{1,0:T(8,128)S(1)} %fusion.5, bf16[224,384]{1,0:T(8,128)(2,1)S(1)} %bitcast.113, bf16[384,1024]{1,0:T(8,128)(2,1)} %collective-permute-done.8), kind=kOutput, calls=%fused_computation.4 | convolution fusion | flops 176390144 | bytes 2793472 | tf_op jit(solution)/shard_map/dot_general | solution.py:18
  180.4 8.3 %all-to-all-done.5 = bf16[8,2,96,128]{3,2,1,0:T(8,128)(2,1)S(1)} async-done(((bf16[8,2,96,128]{3,2,1,0:T(8,128)(2,1)}), bf16[8,2,96,128]{3,2,1,0:T(8,128)(2,1)S(1)}, u32[]{:S(2)}, u32[]{:S(2)}) %all-to-all-start.5) | async-done | bytes 393248 | tf_op jit(solution)/shard_map/all_to_all | solution.py:62
  188.8 8.5 %collective-permute-start.9 = (f32[2,96,64]{2,1,0:T(8,128)S(1)}, f32[2,96,64]{2,1,0:T(8,128)S(1)}, u32[]{:S(2)}, u32[]{:S(2)}) collective-permute-start(f32[2,96,64]{2,1,0:T(8,128)S(1)} %get-tuple-element.49), channel_id=1, source_target_pairs={{0,1},{1,0},{2,3},{3,2},{4,5},{5,4},{6,7},{7,6},{8,9},{9,8},{10,11... | collective-permute-start | bytes 147464 | tf_op jit(solution)/shard_map/ppermute | solution.py:80
  (89 shorter events, 27.3 us)
Async XLA Ops:
  3.5 9.6 %collective-permute-start = (bf16[2,96,64]{1,2,0:T(8,128)(2,1)S(1)}, bf16[2,96,64]{1,2,0:T(8,128)(2,1)S(1)}, u32[]{:S(2)}, u32[]{:S(2)}) collective-permute-start(bf16[2,96,64]{1,2,0:T(8,128)(2,1)S(1)} %bitcast.121), channel_id=1, source_target_pairs={{0,1},{1,0},{2,3},{3,2},{4,5},{5,4},{6,7},{7,6},{8,9},{9,8},{10,11... | collective-permute-start | bytes 73736 | tf_op jit(solution)/shard_map/ppermute | solution.py:80
  13.1 11.6 %collective-permute-start.2 = (bf16[2,96,128]{1,2,0:T(8,128)(2,1)S(1)}, bf16[2,96,128]{1,2,0:T(8,128)(2,1)S(1)}, u32[]{:S(2)}, u32[]{:S(2)}) collective-permute-start(bf16[2,96,128]{1,2,0:T(8,128)(2,1)S(1)} %maximum_select_fusion.1), channel_id=1, source_target_pairs={{0,8},{1,9},{2,10},{3,11},{4,12},{5,13},{6,14},{7,15},{8,0},{9,1},... | collective-permute-start | bytes 147464 | tf_op jit(solution)/shard_map/ppermute | solution.py:70
  40.3 7.2 %copy-start.8 = (bf16[224,1024]{1,0:T(8,128)(2,1)S(1)}, bf16[224,1024]{1,0:T(8,128)(2,1)}, u32[]{:S(2)}) copy-start(bf16[224,1024]{1,0:T(8,128)(2,1)} %param.12) | copy-start | bytes 1376260
  40.3 22.8 %all-to-all-start.1 = ((bf16[4,2,8,96,128]{4,2,3,1,0:T(8,128)(2,1)}), bf16[4,2,8,96,128]{4,2,3,1,0:T(8,128)(2,1)S(1)}, u32[]{:S(2)}, u32[]{:S(2)}) async-start(bf16[4,2,8,96,128]{4,2,3,1,0:T(8,128)(2,1)} %broadcast_in_dim.7), calls=%async_computation.1 | async-start | bytes 3145728 | tf_op jit(solution)/shard_map/all_to_all | solution.py:77
  44.0 10.0 %collective-permute-start.4 = (bf16[224,1024]{1,0:T(8,128)(2,1)}, bf16[224,1024]{1,0:T(8,128)(2,1)S(1)}, u32[]{:S(2)}, u32[]{:S(2)}) collective-permute-start(bf16[224,1024]{1,0:T(8,128)(2,1)} %param.13), channel_id=1, source_target_pairs={{0,1},{1,0},{2,3},{3,2},{4,5},{5,4},{6,7},{7,6},{8,9},{9,8},{10,11... | collective-permute-start | bytes 1376264 | tf_op jit(solution)/shard_map/ppermute | solution.py:80
  47.6 6.5 %collective-permute-start.3 = (bf16[224,1024]{1,0:T(8,128)(2,1)S(1)}, bf16[224,1024]{1,0:T(8,128)(2,1)S(1)}, u32[]{:S(2)}, u32[]{:S(2)}) collective-permute-start(bf16[224,1024]{1,0:T(8,128)(2,1)S(1)} %copy-done.8), channel_id=1, source_target_pairs={{0,1},{1,0},{2,3},{3,2},{4,5},{5,4},{6,7},{7,6},{8,9},{9,8},{10,11... | collective-permute-start | bytes 1376264 | tf_op jit(solution)/shard_map/ppermute | solution.py:80
  49.5 4.7 %collective-permute-start.1 = (bf16[224,1024]{1,0:T(8,128)(2,1)}, bf16[224,1024]{1,0:T(8,128)(2,1)S(1)}, u32[]{:S(2)}, u32[]{:S(2)}) collective-permute-start(bf16[224,1024]{1,0:T(8,128)(2,1)} %param.11), channel_id=1, source_target_pairs={{0,1},{1,0},{2,3},{3,2},{4,5},{5,4},{6,7},{7,6},{8,9},{9,8},{10,11... | collective-permute-start | bytes 1376264 | tf_op jit(solution)/shard_map/ppermute | solution.py:80
  63.1 1.5 copy-start.6
  63.2 2.7 %copy-start = (bf16[4,1,8,96,128]{4,2,3,1,0:T(8,128)(2,1)}, bf16[4,1,8,96,128]{4,2,3,1,0:T(8,128)(2,1)S(1)}, u32[]{:S(2)}) copy-start(bf16[4,1,8,96,128]{4,2,3,1,0:T(8,128)(2,1)S(1)} %get-tuple-element.31) | copy-start | bytes 2359300
  65.2 1.2 copy-start.12
  81.9 16.7 %collective-permute-start.5 = (bf16[3,112,384]{2,1,0:T(8,128)(2,1)S(1)}, bf16[3,112,384]{2,1,0:T(8,128)(2,1)S(1)}, u32[]{:S(2)}, u32[]{:S(2)}) collective-permute-start(bf16[3,112,384]{2,1,0:T(8,128)(2,1)S(1)} %convert_element_type.51), channel_id=1, source_target_pairs={{0,64},{64,0},{128,192},{192,128},{256,320},{320,256},{384,448},{4... | collective-permute-start | bytes 774152 | tf_op jit(solution)/shard_map/ppermute | solution.py:83
  114.2 26.8 %all-to-all-start.4 = ((bf16[4,2,96,1024]{3,2,1,0:T(8,128)(2,1)}), bf16[4,2,96,1024]{3,2,1,0:T(8,128)(2,1)S(1)}, u32[]{:S(2)}, u32[]{:S(2)}) async-start(bf16[4,2,96,1024]{3,2,1,0:T(8,128)(2,1)} %pad_maximum_fusion), calls=%async_computation.4 | async-start | bytes 3145728 | tf_op jit(solution)/shard_map/all_to_all | solution.py:77
  117.7 1.2 copy-start.1
  120.0 52.8 %collective-permute-start.7 = (bf16[384,1024]{1,0:T(8,128)(2,1)}, bf16[384,1024]{1,0:T(8,128)(2,1)}, u32[]{:S(2)}, u32[]{:S(2)}) collective-permute-start(bf16[384,1024]{1,0:T(8,128)(2,1)} %bitcast.94), channel_id=1, source_target_pairs={{0,1},{1,0},{2,3},{3,2},{4,5},{5,4},{6,7},{7,6},{8,9},{9,8},{10,11... | collective-permute-start | bytes 2359304 | tf_op jit(solution)/shard_map/ppermute | solution.py:80
  132.3 45.5 %collective-permute-start.8 = (bf16[384,1024]{1,0:T(8,128)(2,1)}, bf16[384,1024]{1,0:T(8,128)(2,1)}, u32[]{:S(2)}, u32[]{:S(2)}) collective-permute-start(bf16[384,1024]{1,0:T(8,128)(2,1)} %bitcast.93), channel_id=1, source_target_pairs={{0,1},{1,0},{2,3},{3,2},{4,5},{5,4},{6,7},{7,6},{8,9},{9,8},{10,11... | collective-permute-start | bytes 2359304 | tf_op jit(solution)/shard_map/ppermute | solution.py:80
  137.2 34.5 %collective-permute-start.6 = (bf16[2,3,112,384]{3,2,1,0:T(8,128)(2,1)}, bf16[2,3,112,384]{3,2,1,0:T(8,128)(2,1)}, u32[]{:S(2)}, u32[]{:S(2)}) collective-permute-start(bf16[2,3,112,384]{3,2,1,0:T(8,128)(2,1)} %slice.97), channel_id=1, source_target_pairs={{0,1},{1,0},{2,3},{3,2},{4,5},{5,4},{6,7},{7,6},{8,9},{9,8},{10,11... | collective-permute-start | bytes 1548296 | tf_op jit(solution)/shard_map/ppermute | solution.py:80
  140.9 30.3 %copy-start.2 = (bf16[4,1,8,96,128]{4,2,3,1,0:T(8,128)(2,1)S(1)}, bf16[4,1,8,96,128]{4,2,3,1,0:T(8,128)(2,1)}, u32[]{:S(2)}) copy-start(bf16[4,1,8,96,128]{4,2,3,1,0:T(8,128)(2,1)} %copy-done) | copy-start | bytes 2359300
  140.9 30.3 %copy-start.7 = (bf16[2,1,112,384]{3,2,1,0:T(8,128)(2,1)S(1)}, bf16[2,1,112,384]{3,2,1,0:T(8,128)(2,1)}, u32[]{:S(2)}) copy-start(bf16[2,1,112,384]{3,2,1,0:T(8,128)(2,1)} %get-tuple-element.32) | copy-start | bytes 516100
  142.5 46.1 %all-to-all-start.5 = ((bf16[8,2,96,128]{3,2,1,0:T(8,128)(2,1)}), bf16[8,2,96,128]{3,2,1,0:T(8,128)(2,1)S(1)}, u32[]{:S(2)}, u32[]{:S(2)}) async-start(bf16[8,2,96,128]{3,2,1,0:T(8,128)(2,1)} %shard_map.118), calls=%async_computation.5 | async-start | bytes 786432 | tf_op jit(solution)/shard_map/all_to_all | solution.py:62
  171.2 1.6 copy-start.3
  172.8 2.6 %copy-start.4 = (f32[224,1024]{1,0:T(8,128)S(1)}, f32[224,1024]{1,0:T(8,128)}, u32[]{:S(2)}) copy-start(f32[224,1024]{1,0:T(8,128)} %fusion.6) | copy-start | bytes 2752516
  177.9 19.5 %copy-start.10 = (f32[64,192]{1,0:T(8,128)S(1)}, f32[64,192]{1,0:T(8,128)}, u32[]{:S(2)}) copy-start(f32[64,192]{1,0:T(8,128)} %param.9) | copy-start | bytes 147460
  177.9 19.6 %copy-start.9 = (f32[64,192]{1,0:T(8,128)S(1)}, f32[64,192]{1,0:T(8,128)}, u32[]{:S(2)}) copy-start(f32[64,192]{1,0:T(8,128)} %param.8) | copy-start | bytes 147460
  188.8 9.5 %collective-permute-start.9 = (f32[2,96,64]{2,1,0:T(8,128)S(1)}, f32[2,96,64]{2,1,0:T(8,128)S(1)}, u32[]{:S(2)}, u32[]{:S(2)}) collective-permute-start(f32[2,96,64]{2,1,0:T(8,128)S(1)} %get-tuple-element.49), channel_id=1, source_target_pairs={{0,1},{1,0},{2,3},{3,2},{4,5},{5,4},{6,7},{7,6},{8,9},{9,8},{10,11... | collective-permute-start | bytes 147464 | tf_op jit(solution)/shard_map/ppermute | solution.py:80
  (2 other events, 2.1 us)

commit v4 on v3

--- a/solution.py
+++ b/solution.py
@@ -8,6 +8,7 @@
 momentum = 0.5
 BF = jnp.bfloat16
 F32 = jnp.float32
+together = lax.optimization_barrier
 
 
 def copies(block, count):
@@ -61,13 +62,15 @@
     def over_z(blocks):
         return lax.all_to_all(blocks, "col", 0, 0, axis_index_groups=z_groups)
 
-    def gather_z(block, place):
+    def across_z(block):
         span = count_z // 2
-        pairs = [(c, (c + 2 * span) % cols) for c in range(cols)]
+        return lax.ppermute(block, "col", [(c, (c + 2 * span) % cols) for c in range(cols)])
+
+    def gather_half(block, far, place):
+        span = count_z // 2
         groups = [
             [2 * (end * span + z) + k for z in range(span)] for end in range(2) for k in range(2)
         ]
-        far = lax.ppermute(block, "col", pairs)
         low = place < span
         both = jnp.stack([jnp.where(low, block, far), jnp.where(low, far, block)])
         both = lax.all_to_all(copies(both, span), "col", 0, 0, axis_index_groups=groups)
@@ -103,21 +106,18 @@
         block = pick(
             jnp.concatenate([mine, theirs], -1), jnp.concatenate([theirs, mine], -1)
         )
-        block, gate_weight, up_weight, down_weight = lax.optimization_barrier(
+        block, gate_weight, up_weight, down_weight = together(
             (block, gate_weight, up_weight, down_weight)
         )
-
-        gate_w = jnp.concatenate([gate_weight, other_core(gate_weight)])
-        up_w = jnp.concatenate([up_weight, other_core(up_weight)])
-        down_w = jnp.concatenate([down_weight, other_core(down_weight)])
-
-        along_z = jnp.swapaxes(gather_z(block, lax.axis_index("col") // 2), 0, 1)
+        along_z = gather_half(block, across_z(block), lax.axis_index("col") // 2)
+        weights = jnp.concatenate([gate_weight, up_weight, down_weight], 1)
+        weights = jnp.concatenate([weights, other_core(weights)])
+        along_z, weights = together((along_z, weights))
+        gate_w, up_w, down_w = [weights[:, i * wide : (i + 1) * wide] for i in range(3)]
+        along_z = along_z.transpose(1, 2, 0, 3).reshape(2, half, wide)
         inputs = over_row(copies(along_z, rows))
 
-        def matrix(which):
-            return jnp.swapaxes(inputs[:, which], 1, 2).reshape(tokens, wide)
-
-        x_mat, df_mat = matrix(0), matrix(1)
+        x_mat, df_mat = [inputs[:, which].reshape(tokens, wide) for which in range(2)]
 
         def hidden_part(weight, mat):
             return dot(weight, mat, 1, 1).astype(BF).reshape(count_x, 1, part, tokens)
@@ -137,19 +137,22 @@
             return total.astype(BF).reshape(rows, half, wide)
 
         terms = sum_rows(over_row(jnp.stack([blocks_of(y_part), blocks_of(dx_part)], 1)))
+        terms, late, v_late, dx_late, x_mat, df_mat = together(
+            (terms, hidden, v_out, dx_out, x_mat, df_mat)
+        )
         terms = over_z(terms)
         x_far, df_far = other_core(x_mat), other_core(df_mat)
-        hidden_far = other_core(hidden[count_x // 2 :])
+        hidden_far = other_core(late[count_x // 2 :])
 
         def gradient(which, near, far):
-            mine = hidden[: count_x // 2, which].reshape(hid, tokens)
+            mine = late[: count_x // 2, which].reshape(hid, tokens)
             theirs = hidden_far[:, which].reshape(hid, tokens)
             return dot(mine, near, 1, 0) + dot(theirs, far, 1, 0)
 
         grad_down = gradient(0, df_mat, df_far)
         grad_gate = gradient(1, x_mat, x_far)
         grad_up = gradient(2, x_mat, x_far)
-        terms, grad_gate, grad_up, grad_down = lax.optimization_barrier(
+        terms, grad_gate, grad_up, grad_down = together(
             (terms, grad_gate, grad_up, grad_down)
         )
         terms = terms.astype(F32).sum(0)
@@ -157,8 +160,8 @@
         theirs = other_core(pick(high, low))
         mine = pick(low, high)
         done = pick(jnp.concatenate([mine, theirs], 1), jnp.concatenate([theirs, mine], 1))
-        v_prev = (v_out - (1.0 - momentum) * done[0].T) / momentum
-        dx_prev = dx_out + done[1].T
+        v_prev = (v_late - (1.0 - momentum) * done[0].T) / momentum
+        dx_prev = dx_late + done[1].T
 
         return (x_prev, v_prev, dx_prev, grad_gate, grad_up, grad_down)
 

time: 201 us -> 195 us (0.970)
  blocking collectives: 40.2 us -> 77.2 us
  waiting for transfers between devices: 29.7 us -> 13.8 us
  local copies, waits for them, and re-layouts: 14.2 us -> 2.89 us
  starting transfers between devices: 93.8 us -> 84.5 us
  matrix products: 14.3 us -> 8.99 us
    all_to_all x1 -> x3, blocking collectives: 13.7 us -> 50.1 us  [the longest x2 36.4 us: over_row(): return lax.all_to_all(blocks, 'row', 0, 0)]
    ppermute x8 -> x6, starting transfers between devices: 41.8 us -> 28.9 us  [other_core(): return lax.ppermute(block, 'col', swap_core)]
    all_to_all x1, starting transfers between devices: 28.7 us -> 39.5 us  [over_z(): return lax.all_to_all(blocks, 'col', 0, 0, axis_index_groups=z_groups)]
    all_to_all x2 -> x0, waiting for transfers between devices: 7.74 us -> none  [over_row(): return lax.all_to_all(blocks, 'row', 0, 0)]
    unnamed x37 -> x17, local copies, waits for them, and re-layouts: 9.07 us -> 1.55 us
    all_to_all x2 -> x0, starting transfers between devices: 7.25 us -> none  [over_row(): return lax.all_to_all(blocks, 'row', 0, 0)]
    all_to_all x1, waiting for transfers between devices: 8.29 us -> 2.9 us  [over_z(): return lax.all_to_all(blocks, 'col', 0, 0, axis_index_groups=z_groups)]
    dot_general x12, matrix products: 14.3 us -> 8.99 us  [dot(): lax.dot_general(left, right, (((left_dim,), (right_dim,)), ((), ())), pre...]
  transfers between devices with their start and end apart: 13 -> 9, of which waited for: 6 -> 5; matrix products, arithmetic and copies ran while one was open for 9% -> 3% of each run, Pallas kernels for 1% -> 0%
where the time goes in v4:
time: 195 us; the launch traced here: 194 us
  starting transfers between devices  84.5 us (43%)
  blocking collectives  77.2 us (40%)
  waiting for transfers between devices  13.8 us (7%)
  matrix products  8.99 us (5%)
  other arithmetic  3.76 us (2%)
  local copies, waits for them, and re-layouts  2.89 us (1%)
    all_to_all x1, starting transfers between devices, over_z(): return lax.all_to_all(blocks, 'col', 0, 0, axis_index_groups=z_groups)  39.5 us
    all_to_all x2, blocking collectives, over_row(): return lax.all_to_all(blocks, 'row', 0, 0)  36.4 us
    ppermute x6, starting transfers between devices, other_core(): return lax.ppermute(block, 'col', swap_core)  28.9 us
    all_to_all x2, blocking collectives, over_x(): return lax.all_to_all(blocks, 'depth', 0, 0, axis_index_groups=x_groups)  27.2 us
    all_to_all x1, blocking collectives, gather_half(): lax.all_to_all(copies(both, span), 'col', 0, 0, axis_index_groups=groups)  13.7 us
    ppermute x1, starting transfers between devices, other_half(): return lax.ppermute(block, 'depth', swap_half)  12.7 us
    dot_general x12, matrix products, dot(): lax.dot_general(left, right, (((left_dim,), (right_dim,)), ((), ())), pre...  8.99 us
    ppermute x1, waiting for transfers between devices, across_z(): lax.ppermute(block, 'col', [(c, (c + 2 * span) % cols) for c in range(col...  5.43 us
  transfers between devices with their start and end apart: 9, of which 5 were waited for; matrix products, arithmetic and copies ran while one was open for 3% of the time, Pallas kernels for 0%

profile of v4, /device:TPU:1, one launch (start us, length us, event | category | flops | bytes accessed | tf_op | source)
XLA Modules:
  0.0 194.0 jit_solution(12719109085793378631)
XLA Ops:
  0.7 1.6 convert_bitcast_fusion
  2.4 0.9 fusion.11
  3.6 8.8 %collective-permute-start = (bf16[2,96,64]{1,2,0:T(8,128)(2,1)S(1)}, bf16[2,96,64]{1,2,0:T(8,128)(2,1)S(1)}, u32[]{:S(2)}, u32[]{:S(2)}) collective-permute-start(bf16[2,96,64]{1,2,0:T(8,128)(2,1)S(1)} %bitcast.105), channel_id=1, source_target_pairs={{0,1},{1,0},{2,3},{3,2},{4,5},{5,4},{6,7},{7,6},{8,9},{9,8},{10,11... | collective-permute-start | bytes 73736 | tf_op jit(solution)/shard_map/ppermute | solution.py:83
  12.4 0.8 collective-permute-done
  13.3 3.4 %collective-permute-start.1 = (bf16[2,96,128]{1,2,0:T(8,128)(2,1)S(1)}, bf16[2,96,128]{1,2,0:T(8,128)(2,1)S(1)}, u32[]{:S(2)}, u32[]{:S(2)}) collective-permute-start(bf16[2,96,128]{1,2,0:T(8,128)(2,1)S(1)} %maximum_select_fusion.1), channel_id=1, source_target_pairs={{0,8},{1,9},{2,10},{3,11},{4,12},{5,13},{6,14},{7,15},{8,0},{9,1},... | collective-permute-start | bytes 147464 | tf_op jit(solution)/shard_map/ppermute | solution.py:67
  16.9 2.5 %collective-permute-start.2 = (bf16[224,3072]{1,0:T(8,128)(2,1)S(1)}, bf16[224,3072]{1,0:T(8,128)(2,1)S(1)}, u32[]{:S(2)}, u32[]{:S(2)}) collective-permute-start(bf16[224,3072]{1,0:T(8,128)(2,1)S(1)} %constant_dynamic-update-slice_fusion.2), channel_id=1, source_target_pairs={{0,1},{1,0},{2,3},{3,2},{4,5},{5,4},{6,7},{7,6},{8,9},{9,8},{10,11... | collective-permute-start | bytes 4128776 | tf_op jit(solution)/shard_map/ppermute | solution.py:83
  19.4 5.4 %collective-permute-done.1 = bf16[2,96,128]{1,2,0:T(8,128)(2,1)S(1)} collective-permute-done((bf16[2,96,128]{1,2,0:T(8,128)(2,1)S(1)}, bf16[2,96,128]{1,2,0:T(8,128)(2,1)S(1)}, u32[]{:S(2)}, u32[]{:S(2)}) %collective-permute-start.1) | collective-permute-done | bytes 49184 | tf_op jit(solution)/shard_map/ppermute | solution.py:67
  25.1 13.7 %all_to_all.30 = bf16[4,2,2,96,128]{4,3,2,1,0:T(8,128)(2,1)S(1)} all-to-all(bf16[4,2,2,96,128]{4,3,2,1,0:T(8,128)(2,1)S(1)} %broadcast_in_dim.8), channel_id=1, replica_groups={{0,2,4,6},{1,3,5,7},{8,10,12,14},{9,11,13,15},{16,18,20,22},{17,19,21,2..., dimensions={0} | all-to-all | bytes 786432 | tf_op jit(solution)/shard_map/all_to_all | solution.py:76
  39.3 21.4 %all_to_all.31 = bf16[4,2,96,1024]{3,2,1,0:T(8,128)(2,1)S(1)} all-to-all(bf16[4,2,96,1024]{3,2,1,0:T(8,128)(2,1)S(1)} %broadcast_in_dim.10), channel_id=1, replica_groups=mesh['depth'=8,'row'=4,'col'=16] {'row'}, dimensions={0} | all-to-all | bytes 3145728 | tf_op jit(solution)/shard_map/all_to_all | solution.py:80
  62.9 15.1 %all_to_all.32 = bf16[4,3,112,384]{3,2,1,0:T(8,128)(2,1)S(1)} all-to-all(bf16[4,3,112,384]{3,2,1,0:T(8,128)(2,1)S(1)} %pad_maximum_fusion.2), channel_id=1, replica_groups={{0,128,256,384},{64,192,320,448},{1,129,257,385},{65,193,321,449},{2,13..., dimensions={0} | all-to-all | bytes 2064384 | tf_op jit(solution)/shard_map/all_to_all | solution.py:60
  78.2 12.7 %collective-permute-start.3 = (bf16[3,112,384]{2,1,0:T(8,128)(2,1)S(1)}, bf16[3,112,384]{2,1,0:T(8,128)(2,1)S(1)}, u32[]{:S(2)}, u32[]{:S(2)}) collective-permute-start(bf16[3,112,384]{2,1,0:T(8,128)(2,1)S(1)} %convert_element_type.51), channel_id=1, source_target_pairs={{0,64},{64,0},{128,192},{192,128},{256,320},{320,256},{384,448},{4... | collective-permute-start | bytes 774152 | tf_op jit(solution)/shard_map/ppermute | solution.py:86
  90.9 4.0 %collective-permute-done.3 = bf16[3,112,384]{2,1,0:T(8,128)(2,1)S(1)} collective-permute-done((bf16[3,112,384]{2,1,0:T(8,128)(2,1)S(1)}, bf16[3,112,384]{2,1,0:T(8,128)(2,1)S(1)}, u32[]{:S(2)}, u32[]{:S(2)}) %collective-permute-start.3) | collective-permute-done | bytes 258080 | tf_op jit(solution)/shard_map/ppermute | solution.py:86
  95.2 12.1 %all_to_all.33 = bf16[4,3,112,384]{3,2,1,0:T(8,128)(2,1)S(1)} all-to-all(bf16[4,3,112,384]{3,2,1,0:T(8,128)(2,1)S(1)} %broadcast_in_dim.22), channel_id=1, replica_groups={{0,128,256,384},{64,192,320,448},{1,129,257,385},{65,193,321,449},{2,13..., dimensions={0} | all-to-all | bytes 2064384 | tf_op jit(solution)/shard_map/all_to_all | solution.py:60
  109.3 15.0 %all_to_all.34.in_ref = bf16[4,2,96,1024]{3,2,1,0:T(8,128)(2,1)S(1)} all-to-all(bf16[4,2,96,1024]{3,2,1,0:T(8,128)(2,1)S(1)} %pad_maximum_fusion.1), channel_id=1, replica_groups=mesh['depth'=8,'row'=4,'col'=16] {'row'}, dimensions={0} | all-to-all | bytes 3145728 | tf_op jit(solution)/shard_map/all_to_all | solution.py:80
  124.3 1.6 shard_map.118
  125.9 39.5 %all-to-all-start.5 = ((bf16[8,2,96,128]{3,2,1,0:T(8,128)(2,1)}), bf16[8,2,96,128]{3,2,1,0:T(8,128)(2,1)S(1)}, u32[]{:S(2)}, u32[]{:S(2)}) async-start(bf16[8,2,96,128]{3,2,1,0:T(8,128)(2,1)} %shard_map.118), calls=%async_computation.5 | async-start | bytes 786432 | tf_op jit(solution)/shard_map/all_to_all | solution.py:63
  165.5 4.7 %collective-permute-start.5 = (bf16[384,1024]{1,0:T(8,128)(2,1)S(1)}, bf16[384,1024]{1,0:T(8,128)(2,1)S(1)}, u32[]{:S(2)}, u32[]{:S(2)}) collective-permute-start(bf16[384,1024]{1,0:T(8,128)(2,1)S(1)} %bitcast.83), channel_id=1, source_target_pairs={{0,1},{1,0},{2,3},{3,2},{4,5},{5,4},{6,7},{7,6},{8,9},{9,8},{10,11... | collective-permute-start | bytes 2359304 | tf_op jit(solution)/shard_map/ppermute | solution.py:83
  170.7 1.9 collective-permute-start.4
  172.6 2.4 %collective-permute-start.6 = (bf16[384,1024]{1,0:T(8,128)(2,1)S(1)}, bf16[384,1024]{1,0:T(8,128)(2,1)S(1)}, u32[]{:S(2)}, u32[]{:S(2)}) collective-permute-start(bf16[384,1024]{1,0:T(8,128)(2,1)S(1)} %bitcast.87), channel_id=1, source_target_pairs={{0,1},{1,0},{2,3},{3,2},{4,5},{5,4},{6,7},{7,6},{8,9},{9,8},{10,11... | collective-permute-start | bytes 2359304 | tf_op jit(solution)/shard_map/ppermute | solution.py:83
  175.9 1.3 convolution_add_fusion.2
  177.3 1.3 convolution_add_fusion.1
  178.6 1.3 convolution_add_fusion
  180.0 2.9 %all-to-all-done.5 = bf16[8,2,96,128]{3,2,1,0:T(8,128)(2,1)S(1)} async-done(((bf16[8,2,96,128]{3,2,1,0:T(8,128)(2,1)}), bf16[8,2,96,128]{3,2,1,0:T(8,128)(2,1)S(1)}, u32[]{:S(2)}, u32[]{:S(2)}) %all-to-all-start.5) | async-done | bytes 393248 | tf_op jit(solution)/shard_map/all_to_all | solution.py:63
  183.0 8.5 %collective-permute-start.7 = (f32[2,96,64]{2,1,0:T(8,128)S(1)}, f32[2,96,64]{2,1,0:T(8,128)S(1)}, u32[]{:S(2)}, u32[]{:S(2)}) collective-permute-start(f32[2,96,64]{2,1,0:T(8,128)S(1)} %get-tuple-element.65), channel_id=1, source_target_pairs={{0,1},{1,0},{2,3},{3,2},{4,5},{5,4},{6,7},{7,6},{8,9},{9,8},{10,11... | collective-permute-start | bytes 147464 | tf_op jit(solution)/shard_map/ppermute | solution.py:83
  (64 shorter events, 9.9 us)
Async XLA Ops:
  0.6 16.1 %copy-start = (bf16[224,1024]{1,0:T(8,128)(2,1)S(1)}, bf16[224,1024]{1,0:T(8,128)(2,1)}, u32[]{:S(2)}) copy-start(bf16[224,1024]{1,0:T(8,128)(2,1)} %param.11) | copy-start | bytes 1376260
  0.6 16.1 %copy-start.1 = (bf16[224,1024]{1,0:T(8,128)(2,1)S(1)}, bf16[224,1024]{1,0:T(8,128)(2,1)}, u32[]{:S(2)}) copy-start(bf16[224,1024]{1,0:T(8,128)(2,1)} %param.12) | copy-start | bytes 1376260
  0.7 16.2 %copy-start.2 = (bf16[224,1024]{1,0:T(8,128)(2,1)S(1)}, bf16[224,1024]{1,0:T(8,128)(2,1)}, u32[]{:S(2)}) copy-start(bf16[224,1024]{1,0:T(8,128)(2,1)} %param.13) | copy-start | bytes 1376260
  3.6 9.6 %collective-permute-start = (bf16[2,96,64]{1,2,0:T(8,128)(2,1)S(1)}, bf16[2,96,64]{1,2,0:T(8,128)(2,1)S(1)}, u32[]{:S(2)}, u32[]{:S(2)}) collective-permute-start(bf16[2,96,64]{1,2,0:T(8,128)(2,1)S(1)} %bitcast.105), channel_id=1, source_target_pairs={{0,1},{1,0},{2,3},{3,2},{4,5},{5,4},{6,7},{7,6},{8,9},{9,8},{10,11... | collective-permute-start | bytes 73736 | tf_op jit(solution)/shard_map/ppermute | solution.py:83
  13.3 11.6 %collective-permute-start.1 = (bf16[2,96,128]{1,2,0:T(8,128)(2,1)S(1)}, bf16[2,96,128]{1,2,0:T(8,128)(2,1)S(1)}, u32[]{:S(2)}, u32[]{:S(2)}) collective-permute-start(bf16[2,96,128]{1,2,0:T(8,128)(2,1)S(1)} %maximum_select_fusion.1), channel_id=1, source_target_pairs={{0,8},{1,9},{2,10},{3,11},{4,12},{5,13},{6,14},{7,15},{8,0},{9,1},... | collective-permute-start | bytes 147464 | tf_op jit(solution)/shard_map/ppermute | solution.py:67
  16.9 22.0 %collective-permute-start.2 = (bf16[224,3072]{1,0:T(8,128)(2,1)S(1)}, bf16[224,3072]{1,0:T(8,128)(2,1)S(1)}, u32[]{:S(2)}, u32[]{:S(2)}) collective-permute-start(bf16[224,3072]{1,0:T(8,128)(2,1)S(1)} %constant_dynamic-update-slice_fusion.2), channel_id=1, source_target_pairs={{0,1},{1,0},{2,3},{3,2},{4,5},{5,4},{6,7},{7,6},{8,9},{9,8},{10,11... | collective-permute-start | bytes 4128776 | tf_op jit(solution)/shard_map/ppermute | solution.py:83
  78.2 16.6 %collective-permute-start.3 = (bf16[3,112,384]{2,1,0:T(8,128)(2,1)S(1)}, bf16[3,112,384]{2,1,0:T(8,128)(2,1)S(1)}, u32[]{:S(2)}, u32[]{:S(2)}) collective-permute-start(bf16[3,112,384]{2,1,0:T(8,128)(2,1)S(1)} %convert_element_type.51), channel_id=1, source_target_pairs={{0,64},{64,0},{128,192},{192,128},{256,320},{320,256},{384,448},{4... | collective-permute-start | bytes 774152 | tf_op jit(solution)/shard_map/ppermute | solution.py:86
  125.9 56.9 %all-to-all-start.5 = ((bf16[8,2,96,128]{3,2,1,0:T(8,128)(2,1)}), bf16[8,2,96,128]{3,2,1,0:T(8,128)(2,1)S(1)}, u32[]{:S(2)}, u32[]{:S(2)}) async-start(bf16[8,2,96,128]{3,2,1,0:T(8,128)(2,1)} %shard_map.118), calls=%async_computation.5 | async-start | bytes 786432 | tf_op jit(solution)/shard_map/all_to_all | solution.py:63
  165.5 10.5 %collective-permute-start.5 = (bf16[384,1024]{1,0:T(8,128)(2,1)S(1)}, bf16[384,1024]{1,0:T(8,128)(2,1)S(1)}, u32[]{:S(2)}, u32[]{:S(2)}) collective-permute-start(bf16[384,1024]{1,0:T(8,128)(2,1)S(1)} %bitcast.83), channel_id=1, source_target_pairs={{0,1},{1,0},{2,3},{3,2},{4,5},{5,4},{6,7},{7,6},{8,9},{9,8},{10,11... | collective-permute-start | bytes 2359304 | tf_op jit(solution)/shard_map/ppermute | solution.py:83
  170.7 5.2 %collective-permute-start.4 = (bf16[2,3,112,384]{3,2,1,0:T(8,128)(2,1)S(1)}, bf16[2,3,112,384]{3,2,1,0:T(8,128)(2,1)S(1)}, u32[]{:S(2)}, u32[]{:S(2)}) collective-permute-start(bf16[2,3,112,384]{3,2,1,0:T(8,128)(2,1)S(1)} %slice.88), channel_id=1, source_target_pairs={{0,1},{1,0},{2,3},{3,2},{4,5},{5,4},{6,7},{7,6},{8,9},{9,8},{10,11... | collective-permute-start | bytes 1548296 | tf_op jit(solution)/shard_map/ppermute | solution.py:83
  172.6 6.0 %collective-permute-start.6 = (bf16[384,1024]{1,0:T(8,128)(2,1)S(1)}, bf16[384,1024]{1,0:T(8,128)(2,1)S(1)}, u32[]{:S(2)}, u32[]{:S(2)}) collective-permute-start(bf16[384,1024]{1,0:T(8,128)(2,1)S(1)} %bitcast.87), channel_id=1, source_target_pairs={{0,1},{1,0},{2,3},{3,2},{4,5},{5,4},{6,7},{7,6},{8,9},{9,8},{10,11... | collective-permute-start | bytes 2359304 | tf_op jit(solution)/shard_map/ppermute | solution.py:83
  178.6 12.9 %copy-start.4 = (f32[64,192]{1,0:T(8,128)S(1)}, f32[64,192]{1,0:T(8,128)}, u32[]{:S(2)}) copy-start(f32[64,192]{1,0:T(8,128)} %param.9) | copy-start | bytes 147460
  178.6 13.0 %copy-start.3 = (f32[64,192]{1,0:T(8,128)S(1)}, f32[64,192]{1,0:T(8,128)}, u32[]{:S(2)}) copy-start(f32[64,192]{1,0:T(8,128)} %param.8) | copy-start | bytes 147460
  183.0 9.5 %collective-permute-start.7 = (f32[2,96,64]{2,1,0:T(8,128)S(1)}, f32[2,96,64]{2,1,0:T(8,128)S(1)}, u32[]{:S(2)}, u32[]{:S(2)}) collective-permute-start(f32[2,96,64]{2,1,0:T(8,128)S(1)} %get-tuple-element.65), channel_id=1, source_target_pairs={{0,1},{1,0},{2,3},{3,2},{4,5},{5,4},{6,7},{7,6},{8,9},{9,8},{10,11... | collective-permute-start | bytes 147464 | tf_op jit(solution)/shard_map/ppermute | solution.py:83

commit v5 on v4

--- a/solution.py
+++ b/solution.py
@@ -30,20 +30,20 @@
 
 
 def sum_kernel(in_ref, out_ref):
-    total = in_ref[0].astype(F32)
-    for row in range(1, in_ref.shape[0]):
-        total += in_ref[row].astype(F32)
     for piece in range(out_ref.shape[0]):
-        out_ref[piece] = total[:, :, piece * 128 : (piece + 1) * 128].astype(BF)
+        lanes = slice(piece * 128, (piece + 1) * 128)
+        total = in_ref[0, :, :, lanes].astype(F32)
+        for row in range(1, in_ref.shape[0]):
+            total += in_ref[row, :, :, lanes].astype(F32)
+        out_ref[piece] = total.astype(BF)
 
 
-def sum_rows(terms, lanes=256):
+def sum_rows(terms):
     rows, arrays, toks, wide = terms.shape
     return pl.pallas_call(
         sum_kernel,
-        grid=(wide // lanes,),
-        in_specs=[pl.BlockSpec((rows, arrays, toks, lanes), lambda i: (0, 0, 0, i))],
-        out_specs=pl.BlockSpec((lanes // 128, arrays, toks, 128), lambda i: (i, 0, 0, 0)),
+        in_specs=[pl.BlockSpec(memory_space=pltpu.VMEM)],
+        out_specs=pl.BlockSpec(memory_space=pltpu.VMEM),
         out_shape=jax.ShapeDtypeStruct((wide // 128, arrays, toks, 128), BF),
         compiler_params=pltpu.CompilerParams(vmem_limit_bytes=32 * 1024 * 1024),
     )(terms)
@@ -62,9 +62,8 @@
     def over_z(blocks):
         return lax.all_to_all(blocks, "col", 0, 0, axis_index_groups=z_groups)
 
-    def across_z(block):
-        span = count_z // 2
-        return lax.ppermute(block, "col", [(c, (c + 2 * span) % cols) for c in range(cols)])
+    def across_z(block, flip):
+        return lax.ppermute(block, "col", [(c, (c + count_z) % cols ^ flip) for c in range(cols)])
 
     def gather_half(block, far, place):
         span = count_z // 2
@@ -101,15 +100,20 @@
         x_half = x_prev.astype(BF)
         df_half = ((1.0 - momentum) * (dx_out + dv_out)).astype(BF)
         both = jnp.stack([x_half.T, df_half.T]).reshape(2, 2, half, feats)
-        mine = pick(both[:, 0], both[:, 1])
-        theirs = other_core(pick(both[:, 1], both[:, 0]))
-        block = pick(
-            jnp.concatenate([mine, theirs], -1), jnp.concatenate([theirs, mine], -1)
+        mine, theirs = pick(both[:, 0], both[:, 1]), pick(both[:, 1], both[:, 0])
+        mine, theirs, gate_weight, up_weight, down_weight = together(
+            (mine, theirs, gate_weight, up_weight, down_weight)
         )
-        block, gate_weight, up_weight, down_weight = together(
-            (block, gate_weight, up_weight, down_weight)
-        )
-        along_z = gather_half(block, across_z(block), lax.axis_index("col") // 2)
+
+        def chip_block(own, other):
+            return pick(
+                jnp.concatenate([own, other], -1), jnp.concatenate([other, own], -1)
+            )
+
+        block = chip_block(mine, other_core(theirs))
+        far = chip_block(across_z(mine, 0), across_z(theirs, 1))
+
+        along_z = gather_half(block, far, lax.axis_index("col") // 2)
         weights = jnp.concatenate([gate_weight, up_weight, down_weight], 1)
         weights = jnp.concatenate([weights, other_core(weights)])
         along_z, weights = together((along_z, weights))

time: 195 us -> 187 us (0.959)
  starting transfers between devices: 84.5 us -> 57.9 us
  waiting for transfers between devices: 13.8 us -> 24.8 us
  blocking collectives: 77.2 us -> 85.2 us
    all_to_all x1, starting transfers between devices: 39.5 us -> 14.4 us  [over_z(): return lax.all_to_all(blocks, 'col', 0, 0, axis_index_groups=z_groups)]
    ppermute x1, waiting for transfers between devices: 3.96 us -> 21.8 us  [other_half(): return lax.ppermute(block, 'depth', swap_half)]
    ppermute x1 -> x2, starting transfers between devices: 3.44 us -> 16 us  [across_z(): lax.ppermute(block, 'col', [(c, (c + count_z) % cols ^ flip) for c in ran...]
    ppermute x1, starting transfers between devices: 12.7 us -> 4.63 us  [other_half(): return lax.ppermute(block, 'depth', swap_half)]
    ppermute x6, starting transfers between devices: 28.9 us -> 22.9 us  [other_core(): return lax.ppermute(block, 'col', swap_core)]
    ppermute x1 -> x2, waiting for transfers between devices: 5.43 us -> 0.01 us  [across_z(): lax.ppermute(block, 'col', [(c, (c + count_z) % cols ^ flip) for c in ran...]
    all_to_all x2, blocking collectives: 36.4 us -> 41.1 us  [over_row(): return lax.all_to_all(blocks, 'row', 0, 0)]
    all_to_all x2, blocking collectives: 27.2 us -> 29.3 us  [over_x(): return lax.all_to_all(blocks, 'depth', 0, 0, axis_index_groups=x_groups)]
  transfers between devices with their start and end apart: 9 -> 10, of which waited for: 5 -> 3; matrix products, arithmetic and copies ran while one was open for 3% -> 4% of each run, Pallas kernels for 0% -> 0%
where the time goes in v5:
time: 187 us
  blocking collectives  85.2 us (46%)
  starting transfers between devices  57.9 us (31%)
  waiting for transfers between devices  24.8 us (13%)
  matrix products  8.99 us (5%)
  local copies, waits for them, and re-layouts  3.9 us (2%)
  other arithmetic  3.75 us (2%)
    all_to_all x2, blocking collectives, over_row(): return lax.all_to_all(blocks, 'row', 0, 0)  41.1 us
    all_to_all x2, blocking collectives, over_x(): return lax.all_to_all(blocks, 'depth', 0, 0, axis_index_groups=x_groups)  29.3 us
    ppermute x6, starting transfers between devices, other_core(): return lax.ppermute(block, 'col', swap_core)  22.9 us
    ppermute x1, waiting for transfers between devices, other_half(): return lax.ppermute(block, 'depth', swap_half)  21.8 us
    ppermute x2, starting transfers between devices, across_z(): lax.ppermute(block, 'col', [(c, (c + count_z) % cols ^ flip) for c in ran...  16 us
    all_to_all x1, blocking collectives, gather_half(): lax.all_to_all(copies(both, span), 'col', 0, 0, axis_index_groups=groups)  14.8 us
    all_to_all x1, starting transfers between devices, over_z(): return lax.all_to_all(blocks, 'col', 0, 0, axis_index_groups=z_groups)  14.4 us
    dot_general x12, matrix products, dot(): lax.dot_general(left, right, (((left_dim,), (right_dim,)), ((), ())), pre...  8.99 us
  transfers between devices with their start and end apart: 10, of which 3 were waited for; matrix products, arithmetic and copies ran while one was open for 4% of the time, Pallas kernels for 0%

profile of v5, /device:TPU:1, one launch (start us, length us, event | category | flops | bytes accessed | tf_op | source)
XLA Modules:
  0.0 186.6 jit_solution(5714682262618330680)
XLA Ops:
  0.7 1.6 convert_bitcast_fusion
  2.4 0.9 fusion.11
  3.6 10.2 %collective-permute-start.2 = (bf16[2,96,64]{1,2,0:T(8,128)(2,1)S(1)}, bf16[2,96,64]{1,2,0:T(8,128)(2,1)S(1)}, u32[]{:S(2)}, u32[]{:S(2)}) collective-permute-start(bf16[2,96,64]{1,2,0:T(8,128)(2,1)S(1)} %get-tuple-element.24), channel_id=1, source_target_pairs={{0,9},{1,8},{2,11},{3,10},{4,13},{5,12},{6,15},{7,14},{8,1},{9,0},... | collective-permute-start | bytes 73736 | tf_op jit(solution)/shard_map/ppermute | solution.py:66
  13.8 1.9 %collective-permute-start = (bf16[2,96,64]{1,2,0:T(8,128)(2,1)S(1)}, bf16[2,96,64]{1,2,0:T(8,128)(2,1)S(1)}, u32[]{:S(2)}, u32[]{:S(2)}) collective-permute-start(bf16[2,96,64]{1,2,0:T(8,128)(2,1)S(1)} %get-tuple-element.24), channel_id=1, source_target_pairs={{0,1},{1,0},{2,3},{3,2},{4,5},{5,4},{6,7},{7,6},{8,9},{9,8},{10,11... | collective-permute-start | bytes 73736 | tf_op jit(solution)/shard_map/ppermute | solution.py:82
  15.7 5.7 %collective-permute-start.1 = (bf16[2,96,64]{1,2,0:T(8,128)(2,1)S(1)}, bf16[2,96,64]{1,2,0:T(8,128)(2,1)S(1)}, u32[]{:S(2)}, u32[]{:S(2)}) collective-permute-start(bf16[2,96,64]{1,2,0:T(8,128)(2,1)S(1)} %get-tuple-element.23), channel_id=1, source_target_pairs={{0,8},{1,9},{2,10},{3,11},{4,12},{5,13},{6,14},{7,15},{8,0},{9,1},... | collective-permute-start | bytes 73736 | tf_op jit(solution)/shard_map/ppermute | solution.py:66
  21.5 1.1 constant_dynamic-update-slice_fusion.4
  22.6 2.7 %collective-permute-start.3 = (bf16[224,3072]{1,0:T(8,128)(2,1)S(1)}, bf16[224,3072]{1,0:T(8,128)(2,1)S(1)}, u32[]{:S(2)}, u32[]{:S(2)}) collective-permute-start(bf16[224,3072]{1,0:T(8,128)(2,1)S(1)} %constant_dynamic-update-slice_fusion.2), channel_id=1, source_target_pairs={{0,1},{1,0},{2,3},{3,2},{4,5},{5,4},{6,7},{7,6},{8,9},{9,8},{10,11... | collective-permute-start | bytes 4128776 | tf_op jit(solution)/shard_map/ppermute | solution.py:82
  25.6 14.8 %all_to_all.30 = bf16[4,2,2,96,128]{4,3,2,1,0:T(8,128)(2,1)S(1)} all-to-all(bf16[4,2,2,96,128]{4,3,2,1,0:T(8,128)(2,1)S(1)} %broadcast_in_dim.8), channel_id=1, replica_groups={{0,2,4,6},{1,3,5,7},{8,10,12,14},{9,11,13,15},{16,18,20,22},{17,19,21,2..., dimensions={0} | all-to-all | bytes 786432 | tf_op jit(solution)/shard_map/all_to_all | solution.py:75
  40.9 22.3 %all_to_all.31 = bf16[4,2,96,1024]{3,2,1,0:T(8,128)(2,1)S(1)} all-to-all(bf16[4,2,96,1024]{3,2,1,0:T(8,128)(2,1)S(1)} %broadcast_in_dim.10), channel_id=1, replica_groups=mesh['depth'=8,'row'=4,'col'=16] {'row'}, dimensions={0} | all-to-all | bytes 3145728 | tf_op jit(solution)/shard_map/all_to_all | solution.py:79
  65.5 15.1 %all_to_all.32 = bf16[4,3,112,384]{3,2,1,0:T(8,128)(2,1)S(1)} all-to-all(bf16[4,3,112,384]{3,2,1,0:T(8,128)(2,1)S(1)} %pad_maximum_fusion.2), channel_id=1, replica_groups={{0,128,256,384},{64,192,320,448},{1,129,257,385},{65,193,321,449},{2,13..., dimensions={0} | all-to-all | bytes 2064384 | tf_op jit(solution)/shard_map/all_to_all | solution.py:60
  80.8 4.6 %collective-permute-start.4 = (bf16[3,112,384]{2,1,0:T(8,128)(2,1)S(1)}, bf16[3,112,384]{2,1,0:T(8,128)(2,1)S(1)}, u32[]{:S(2)}, u32[]{:S(2)}) collective-permute-start(bf16[3,112,384]{2,1,0:T(8,128)(2,1)S(1)} %convert_element_type.51), channel_id=1, source_target_pairs={{0,64},{64,0},{128,192},{192,128},{256,320},{320,256},{384,448},{4... | collective-permute-start | bytes 774152 | tf_op jit(solution)/shard_map/ppermute | solution.py:85
  85.5 21.8 %collective-permute-done.4 = bf16[3,112,384]{2,1,0:T(8,128)(2,1)S(1)} collective-permute-done((bf16[3,112,384]{2,1,0:T(8,128)(2,1)S(1)}, bf16[3,112,384]{2,1,0:T(8,128)(2,1)S(1)}, u32[]{:S(2)}, u32[]{:S(2)}) %collective-permute-start.4) | collective-permute-done | bytes 258080 | tf_op jit(solution)/shard_map/ppermute | solution.py:85
  107.6 14.2 %all_to_all.33 = bf16[4,3,112,384]{3,2,1,0:T(8,128)(2,1)S(1)} all-to-all(bf16[4,3,112,384]{3,2,1,0:T(8,128)(2,1)S(1)} %broadcast_in_dim.22), channel_id=1, replica_groups={{0,128,256,384},{64,192,320,448},{1,129,257,385},{65,193,321,449},{2,13..., dimensions={0} | all-to-all | bytes 2064384 | tf_op jit(solution)/shard_map/all_to_all | solution.py:60
  123.9 18.8 %all_to_all.34.in_ref = bf16[4,2,96,1024]{3,2,1,0:T(8,128)(2,1)S(1)} all-to-all(bf16[4,2,96,1024]{3,2,1,0:T(8,128)(2,1)S(1)} %pad_maximum_fusion.1), channel_id=1, replica_groups=mesh['depth'=8,'row'=4,'col'=16] {'row'}, dimensions={0} | all-to-all | bytes 3145728 | tf_op jit(solution)/shard_map/all_to_all | solution.py:79
  142.6 1.0 shard_map.118
  143.7 14.4 %all-to-all-start.5 = ((bf16[8,2,96,128]{3,2,1,0:T(8,128)(2,1)}), bf16[8,2,96,128]{3,2,1,0:T(8,128)(2,1)S(1)}, u32[]{:S(2)}, u32[]{:S(2)}) async-start(bf16[8,2,96,128]{3,2,1,0:T(8,128)(2,1)} %shard_map.118), calls=%async_computation.5 | async-start | bytes 786432 | tf_op jit(solution)/shard_map/all_to_all | solution.py:63
  158.1 5.4 %collective-permute-start.6 = (bf16[384,1024]{1,0:T(8,128)(2,1)S(1)}, bf16[384,1024]{1,0:T(8,128)(2,1)S(1)}, u32[]{:S(2)}, u32[]{:S(2)}) collective-permute-start(bf16[384,1024]{1,0:T(8,128)(2,1)S(1)} %bitcast.81), channel_id=1, source_target_pairs={{0,1},{1,0},{2,3},{3,2},{4,5},{5,4},{6,7},{7,6},{8,9},{9,8},{10,11... | collective-permute-start | bytes 2359304 | tf_op jit(solution)/shard_map/ppermute | solution.py:82
  164.0 1.9 %collective-permute-start.5 = (bf16[2,3,112,384]{3,2,1,0:T(8,128)(2,1)S(1)}, bf16[2,3,112,384]{3,2,1,0:T(8,128)(2,1)S(1)}, u32[]{:S(2)}, u32[]{:S(2)}) collective-permute-start(bf16[2,3,112,384]{3,2,1,0:T(8,128)(2,1)S(1)} %slice.88), channel_id=1, source_target_pairs={{0,1},{1,0},{2,3},{3,2},{4,5},{5,4},{6,7},{7,6},{8,9},{9,8},{10,11... | collective-permute-start | bytes 1548296 | tf_op jit(solution)/shard_map/ppermute | solution.py:82
  166.0 2.4 %collective-permute-start.7 = (bf16[384,1024]{1,0:T(8,128)(2,1)S(1)}, bf16[384,1024]{1,0:T(8,128)(2,1)S(1)}, u32[]{:S(2)}, u32[]{:S(2)}) collective-permute-start(bf16[384,1024]{1,0:T(8,128)(2,1)S(1)} %bitcast.85), channel_id=1, source_target_pairs={{0,1},{1,0},{2,3},{3,2},{4,5},{5,4},{6,7},{7,6},{8,9},{9,8},{10,11... | collective-permute-start | bytes 2359304 | tf_op jit(solution)/shard_map/ppermute | solution.py:82
  169.3 1.3 convolution_add_fusion.2
  170.6 1.3 convolution_add_fusion.1
  172.0 1.3 convolution_add_fusion
  173.3 2.2 %all-to-all-done.5 = bf16[8,2,96,128]{3,2,1,0:T(8,128)(2,1)S(1)} async-done(((bf16[8,2,96,128]{3,2,1,0:T(8,128)(2,1)}), bf16[8,2,96,128]{3,2,1,0:T(8,128)(2,1)S(1)}, u32[]{:S(2)}, u32[]{:S(2)}) %all-to-all-start.5) | async-done | bytes 393248 | tf_op jit(solution)/shard_map/all_to_all | solution.py:63
  175.7 8.5 %collective-permute-start.8 = (f32[2,96,64]{2,1,0:T(8,128)S(1)}, f32[2,96,64]{2,1,0:T(8,128)S(1)}, u32[]{:S(2)}, u32[]{:S(2)}) collective-permute-start(f32[2,96,64]{2,1,0:T(8,128)S(1)} %get-tuple-element.67), channel_id=1, source_target_pairs={{0,1},{1,0},{2,3},{3,2},{4,5},{5,4},{6,7},{7,6},{8,9},{9,8},{10,11... | collective-permute-start | bytes 147464 | tf_op jit(solution)/shard_map/ppermute | solution.py:82
  (62 shorter events, 9.9 us)
Async XLA Ops:
  0.6 21.9 %copy-start = (bf16[224,1024]{1,0:T(8,128)(2,1)S(1)}, bf16[224,1024]{1,0:T(8,128)(2,1)}, u32[]{:S(2)}) copy-start(bf16[224,1024]{1,0:T(8,128)(2,1)} %param.12) | copy-start | bytes 1376260
  0.6 21.9 %copy-start.1 = (bf16[224,1024]{1,0:T(8,128)(2,1)S(1)}, bf16[224,1024]{1,0:T(8,128)(2,1)}, u32[]{:S(2)}) copy-start(bf16[224,1024]{1,0:T(8,128)(2,1)} %param.13) | copy-start | bytes 1376260
  3.6 21.8 %collective-permute-start.2 = (bf16[2,96,64]{1,2,0:T(8,128)(2,1)S(1)}, bf16[2,96,64]{1,2,0:T(8,128)(2,1)S(1)}, u32[]{:S(2)}, u32[]{:S(2)}) collective-permute-start(bf16[2,96,64]{1,2,0:T(8,128)(2,1)S(1)} %get-tuple-element.24), channel_id=1, source_target_pairs={{0,9},{1,8},{2,11},{3,10},{4,13},{5,12},{6,15},{7,14},{8,1},{9,0},... | collective-permute-start | bytes 73736 | tf_op jit(solution)/shard_map/ppermute | solution.py:66
  13.8 11.6 %collective-permute-start = (bf16[2,96,64]{1,2,0:T(8,128)(2,1)S(1)}, bf16[2,96,64]{1,2,0:T(8,128)(2,1)S(1)}, u32[]{:S(2)}, u32[]{:S(2)}) collective-permute-start(bf16[2,96,64]{1,2,0:T(8,128)(2,1)S(1)} %get-tuple-element.24), channel_id=1, source_target_pairs={{0,1},{1,0},{2,3},{3,2},{4,5},{5,4},{6,7},{7,6},{8,9},{9,8},{10,11... | collective-permute-start | bytes 73736 | tf_op jit(solution)/shard_map/ppermute | solution.py:82
  15.7 9.6 %collective-permute-start.1 = (bf16[2,96,64]{1,2,0:T(8,128)(2,1)S(1)}, bf16[2,96,64]{1,2,0:T(8,128)(2,1)S(1)}, u32[]{:S(2)}, u32[]{:S(2)}) collective-permute-start(bf16[2,96,64]{1,2,0:T(8,128)(2,1)S(1)} %get-tuple-element.23), channel_id=1, source_target_pairs={{0,8},{1,9},{2,10},{3,11},{4,12},{5,13},{6,14},{7,15},{8,0},{9,1},... | collective-permute-start | bytes 73736 | tf_op jit(solution)/shard_map/ppermute | solution.py:66
  22.6 17.9 %collective-permute-start.3 = (bf16[224,3072]{1,0:T(8,128)(2,1)S(1)}, bf16[224,3072]{1,0:T(8,128)(2,1)S(1)}, u32[]{:S(2)}, u32[]{:S(2)}) collective-permute-start(bf16[224,3072]{1,0:T(8,128)(2,1)S(1)} %constant_dynamic-update-slice_fusion.2), channel_id=1, source_target_pairs={{0,1},{1,0},{2,3},{3,2},{4,5},{5,4},{6,7},{7,6},{8,9},{9,8},{10,11... | collective-permute-start | bytes 4128776 | tf_op jit(solution)/shard_map/ppermute | solution.py:82
  80.8 26.5 %collective-permute-start.4 = (bf16[3,112,384]{2,1,0:T(8,128)(2,1)S(1)}, bf16[3,112,384]{2,1,0:T(8,128)(2,1)S(1)}, u32[]{:S(2)}, u32[]{:S(2)}) collective-permute-start(bf16[3,112,384]{2,1,0:T(8,128)(2,1)S(1)} %convert_element_type.51), channel_id=1, source_target_pairs={{0,64},{64,0},{128,192},{192,128},{256,320},{320,256},{384,448},{4... | collective-permute-start | bytes 774152 | tf_op jit(solution)/shard_map/ppermute | solution.py:85
  143.7 31.8 %all-to-all-start.5 = ((bf16[8,2,96,128]{3,2,1,0:T(8,128)(2,1)}), bf16[8,2,96,128]{3,2,1,0:T(8,128)(2,1)S(1)}, u32[]{:S(2)}, u32[]{:S(2)}) async-start(bf16[8,2,96,128]{3,2,1,0:T(8,128)(2,1)} %shard_map.118), calls=%async_computation.5 | async-start | bytes 786432 | tf_op jit(solution)/shard_map/all_to_all | solution.py:63
  158.1 11.1 %collective-permute-start.6 = (bf16[384,1024]{1,0:T(8,128)(2,1)S(1)}, bf16[384,1024]{1,0:T(8,128)(2,1)S(1)}, u32[]{:S(2)}, u32[]{:S(2)}) collective-permute-start(bf16[384,1024]{1,0:T(8,128)(2,1)S(1)} %bitcast.81), channel_id=1, source_target_pairs={{0,1},{1,0},{2,3},{3,2},{4,5},{5,4},{6,7},{7,6},{8,9},{9,8},{10,11... | collective-permute-start | bytes 2359304 | tf_op jit(solution)/shard_map/ppermute | solution.py:82
  164.0 5.2 %collective-permute-start.5 = (bf16[2,3,112,384]{3,2,1,0:T(8,128)(2,1)S(1)}, bf16[2,3,112,384]{3,2,1,0:T(8,128)(2,1)S(1)}, u32[]{:S(2)}, u32[]{:S(2)}) collective-permute-start(bf16[2,3,112,384]{3,2,1,0:T(8,128)(2,1)S(1)} %slice.88), channel_id=1, source_target_pairs={{0,1},{1,0},{2,3},{3,2},{4,5},{5,4},{6,7},{7,6},{8,9},{9,8},{10,11... | collective-permute-start | bytes 1548296 | tf_op jit(solution)/shard_map/ppermute | solution.py:82
  166.0 6.0 %collective-permute-start.7 = (bf16[384,1024]{1,0:T(8,128)(2,1)S(1)}, bf16[384,1024]{1,0:T(8,128)(2,1)S(1)}, u32[]{:S(2)}, u32[]{:S(2)}) collective-permute-start(bf16[384,1024]{1,0:T(8,128)(2,1)S(1)} %bitcast.85), channel_id=1, source_target_pairs={{0,1},{1,0},{2,3},{3,2},{4,5},{5,4},{6,7},{7,6},{8,9},{9,8},{10,11... | collective-permute-start | bytes 2359304 | tf_op jit(solution)/shard_map/ppermute | solution.py:82
  171.9 12.3 %copy-start.3 = (f32[64,192]{1,0:T(8,128)S(1)}, f32[64,192]{1,0:T(8,128)}, u32[]{:S(2)}) copy-start(f32[64,192]{1,0:T(8,128)} %param.9) | copy-start | bytes 147460
  172.0 12.4 %copy-start.2 = (f32[64,192]{1,0:T(8,128)S(1)}, f32[64,192]{1,0:T(8,128)}, u32[]{:S(2)}) copy-start(f32[64,192]{1,0:T(8,128)} %param.8) | copy-start | bytes 147460
  175.7 9.5 %collective-permute-start.8 = (f32[2,96,64]{2,1,0:T(8,128)S(1)}, f32[2,96,64]{2,1,0:T(8,128)S(1)}, u32[]{:S(2)}, u32[]{:S(2)}) collective-permute-start(f32[2,96,64]{2,1,0:T(8,128)S(1)} %get-tuple-element.67), channel_id=1, source_target_pairs={{0,1},{1,0},{2,3},{3,2},{4,5},{5,4},{6,7},{7,6},{8,9},{9,8},{10,11... | collective-permute-start | bytes 147464 | tf_op jit(solution)/shard_map/ppermute | solution.py:82

commit v6 on v5

--- a/solution.py
+++ b/solution.py
@@ -96,8 +96,7 @@
         def pick(one, two):
             return jnp.where(first, one, two)
 
-        x_prev = x_out - v_out
-        x_half = x_prev.astype(BF)
+        x_half = (x_out - v_out).astype(BF)
         df_half = ((1.0 - momentum) * (dx_out + dv_out)).astype(BF)
         both = jnp.stack([x_half.T, df_half.T]).reshape(2, 2, half, feats)
         mine, theirs = pick(both[:, 0], both[:, 1]), pick(both[:, 1], both[:, 0])
@@ -131,7 +130,9 @@
         )
         sums = over_x(parts).astype(F32).sum(0)
         sums = sums + other_half(sums.astype(BF)).astype(F32)
-        hidden = over_x(copies(nonlinear(sums[0], sums[1], sums[2]), count_x))
+        hidden = lax.all_gather(
+            nonlinear(sums[0], sums[1], sums[2]), "depth", axis_index_groups=x_groups
+        )
         act, d_gate, d_up = [hidden[:, i].reshape(2 * hid, tokens) for i in range(3)]
 
         y_part = dot(act, down_w, 0, 0)
@@ -141,9 +142,10 @@
             return total.astype(BF).reshape(rows, half, wide)
 
         terms = sum_rows(over_row(jnp.stack([blocks_of(y_part), blocks_of(dx_part)], 1)))
-        terms, late, v_late, dx_late, x_mat, df_mat = together(
-            (terms, hidden, v_out, dx_out, x_mat, df_mat)
+        terms, late, x_late, v_late, dx_late, x_mat, df_mat = together(
+            (terms, hidden, x_out, v_out, dx_out, x_mat, df_mat)
         )
+        x_prev = x_late - v_late
         terms = over_z(terms)
         x_far, df_far = other_core(x_mat), other_core(df_mat)
         hidden_far = other_core(late[count_x // 2 :])
@@ -156,17 +158,16 @@
         grad_down = gradient(0, df_mat, df_far)
         grad_gate = gradient(1, x_mat, x_far)
         grad_up = gradient(2, x_mat, x_far)
-        terms, grad_gate, grad_up, grad_down = together(
-            (terms, grad_gate, grad_up, grad_down)
+        terms, x_prev, grad_gate, grad_up, grad_down = together(
+            (terms, x_prev, grad_gate, grad_up, grad_down)
         )
-        terms = terms.astype(F32).sum(0)
-        low, high = terms[..., :feats], terms[..., feats:]
+        terms = jnp.swapaxes(terms.astype(F32).sum(0), 1, 2)
+        low, high = terms[:, :feats], terms[:, feats:]
         theirs = other_core(pick(high, low))
         mine = pick(low, high)
-        done = pick(jnp.concatenate([mine, theirs], 1), jnp.concatenate([theirs, mine], 1))
-        v_prev = (v_late - (1.0 - momentum) * done[0].T) / momentum
-        dx_prev = dx_late + done[1].T
-
+        done = pick(jnp.concatenate([mine, theirs], 2), jnp.concatenate([theirs, mine], 2))
+        v_prev = (v_late - (1.0 - momentum) * done[0]) / momentum
+        dx_prev = dx_late + done[1]
         return (x_prev, v_prev, dx_prev, grad_gate, grad_up, grad_down)
 
     return on_device

time: 187 us -> 181 us (0.968)
  waiting for transfers between devices: 24.8 us -> 22.6 us
  blocking collectives: 85.2 us -> 83.1 us
    all_to_all x2 -> x1, blocking collectives: 29.3 us -> 15.1 us  [over_x(): return lax.all_to_all(blocks, 'depth', 0, 0, axis_index_groups=x_groups)]
    all_gather x0 -> x1, blocking collectives: none -> 12.3 us  [on_device(): lax.all_gather(nonlinear(sums[0], sums[1], sums[2]), 'depth', axis_index_...]
    all_to_all x1, starting transfers between devices: 14.4 us -> 10.8 us  [over_z(): return lax.all_to_all(blocks, 'col', 0, 0, axis_index_groups=z_groups)]
    all_to_all x1, waiting for transfers between devices: 2.22 us -> 0.01 us  [over_z(): return lax.all_to_all(blocks, 'col', 0, 0, axis_index_groups=z_groups)]
    ppermute x6, starting transfers between devices: 22.9 us -> 24.8 us  [other_core(): return lax.ppermute(block, 'col', swap_core)]
  transfers between devices with their start and end apart: 10 -> 10, of which waited for: 3 -> 2; matrix products, arithmetic and copies ran while one was open for 4% -> 4% of each run, Pallas kernels for 0% -> 0%
where the time goes in v6:
time: 181 us
  blocking collectives  83.1 us (46%)
  starting transfers between devices  56.2 us (31%)
  waiting for transfers between devices  22.6 us (12%)
  matrix products  8.99 us (5%)
  local copies, waits for them, and re-layouts  3.82 us (2%)
  other arithmetic  3.77 us (2%)
    all_to_all x2, blocking collectives, over_row(): return lax.all_to_all(blocks, 'row', 0, 0)  40.8 us
    ppermute x6, starting transfers between devices, other_core(): return lax.ppermute(block, 'col', swap_core)  24.8 us
    ppermute x1, waiting for transfers between devices, other_half(): return lax.ppermute(block, 'depth', swap_half)  21.8 us
    ppermute x2, starting transfers between devices, across_z(): lax.ppermute(block, 'col', [(c, (c + count_z) % cols ^ flip) for c in ran...  16 us
    all_to_all x1, blocking collectives, over_x(): return lax.all_to_all(blocks, 'depth', 0, 0, axis_index_groups=x_groups)  15.1 us
    all_to_all x1, blocking collectives, gather_half(): lax.all_to_all(copies(both, span), 'col', 0, 0, axis_index_groups=groups)  14.8 us
    all_gather x1, blocking collectives, on_device(): lax.all_gather(nonlinear(sums[0], sums[1], sums[2]), 'depth', axis_index_...  12.3 us
    all_to_all x1, starting transfers between devices, over_z(): return lax.all_to_all(blocks, 'col', 0, 0, axis_index_groups=z_groups)  10.8 us
  transfers between devices with their start and end apart: 10, of which 2 were waited for; matrix products, arithmetic and copies ran while one was open for 4% of the time, Pallas kernels for 0%

profile of v6, /device:TPU:1, one launch (start us, length us, event | category | flops | bytes accessed | tf_op | source)
XLA Modules:
  0.0 180.5 jit_solution(18392738735128058502)
XLA Ops:
  0.7 1.0 fusion.11
  1.7 0.9 fusion.12
  2.9 10.2 %collective-permute-start.2 = (bf16[2,96,64]{1,2,0:T(8,128)(2,1)S(1)}, bf16[2,96,64]{1,2,0:T(8,128)(2,1)S(1)}, u32[]{:S(2)}, u32[]{:S(2)}) collective-permute-start(bf16[2,96,64]{1,2,0:T(8,128)(2,1)S(1)} %get-tuple-element.26), channel_id=1, source_target_pairs={{0,9},{1,8},{2,11},{3,10},{4,13},{5,12},{6,15},{7,14},{8,1},{9,0},... | collective-permute-start | bytes 73736 | tf_op jit(solution)/shard_map/ppermute | solution.py:66
  13.2 1.9 %collective-permute-start = (bf16[2,96,64]{1,2,0:T(8,128)(2,1)S(1)}, bf16[2,96,64]{1,2,0:T(8,128)(2,1)S(1)}, u32[]{:S(2)}, u32[]{:S(2)}) collective-permute-start(bf16[2,96,64]{1,2,0:T(8,128)(2,1)S(1)} %get-tuple-element.26), channel_id=1, source_target_pairs={{0,1},{1,0},{2,3},{3,2},{4,5},{5,4},{6,7},{7,6},{8,9},{9,8},{10,11... | collective-permute-start | bytes 73736 | tf_op jit(solution)/shard_map/ppermute | solution.py:82
  15.1 5.7 %collective-permute-start.1 = (bf16[2,96,64]{1,2,0:T(8,128)(2,1)S(1)}, bf16[2,96,64]{1,2,0:T(8,128)(2,1)S(1)}, u32[]{:S(2)}, u32[]{:S(2)}) collective-permute-start(bf16[2,96,64]{1,2,0:T(8,128)(2,1)S(1)} %get-tuple-element.25), channel_id=1, source_target_pairs={{0,8},{1,9},{2,10},{3,11},{4,12},{5,13},{6,14},{7,15},{8,0},{9,1},... | collective-permute-start | bytes 73736 | tf_op jit(solution)/shard_map/ppermute | solution.py:66
  20.8 1.1 constant_dynamic-update-slice_fusion.4
  22.0 2.7 %collective-permute-start.3 = (bf16[224,3072]{1,0:T(8,128)(2,1)S(1)}, bf16[224,3072]{1,0:T(8,128)(2,1)S(1)}, u32[]{:S(2)}, u32[]{:S(2)}) collective-permute-start(bf16[224,3072]{1,0:T(8,128)(2,1)S(1)} %constant_dynamic-update-slice_fusion.2), channel_id=1, source_target_pairs={{0,1},{1,0},{2,3},{3,2},{4,5},{5,4},{6,7},{7,6},{8,9},{9,8},{10,11... | collective-permute-start | bytes 4128776 | tf_op jit(solution)/shard_map/ppermute | solution.py:82
  25.0 14.8 %all_to_all.25 = bf16[4,2,2,96,128]{4,3,2,1,0:T(8,128)(2,1)S(1)} all-to-all(bf16[4,2,2,96,128]{4,3,2,1,0:T(8,128)(2,1)S(1)} %broadcast_in_dim.6), channel_id=1, replica_groups={{0,2,4,6},{1,3,5,7},{8,10,12,14},{9,11,13,15},{16,18,20,22},{17,19,21,2..., dimensions={0} | all-to-all | bytes 786432 | tf_op jit(solution)/shard_map/all_to_all | solution.py:75
  40.3 22.3 %all_to_all.26 = bf16[4,2,96,1024]{3,2,1,0:T(8,128)(2,1)S(1)} all-to-all(bf16[4,2,96,1024]{3,2,1,0:T(8,128)(2,1)S(1)} %broadcast_in_dim.15), channel_id=1, replica_groups=mesh['depth'=8,'row'=4,'col'=16] {'row'}, dimensions={0} | all-to-all | bytes 3145728 | tf_op jit(solution)/shard_map/all_to_all | solution.py:79
  64.9 15.1 %all_to_all.27 = bf16[4,3,112,384]{3,2,1,0:T(8,128)(2,1)S(1)} all-to-all(bf16[4,3,112,384]{3,2,1,0:T(8,128)(2,1)S(1)} %pad_maximum_fusion.2), channel_id=1, replica_groups={{0,128,256,384},{64,192,320,448},{1,129,257,385},{65,193,321,449},{2,13..., dimensions={0} | all-to-all | bytes 2064384 | tf_op jit(solution)/shard_map/all_to_all | solution.py:60
  80.2 4.6 %collective-permute-start.4 = (bf16[3,112,384]{2,1,0:T(8,128)(2,1)S(1)}, bf16[3,112,384]{2,1,0:T(8,128)(2,1)S(1)}, u32[]{:S(2)}, u32[]{:S(2)}) collective-permute-start(bf16[3,112,384]{2,1,0:T(8,128)(2,1)S(1)} %convert_element_type.51), channel_id=1, source_target_pairs={{0,64},{64,0},{128,192},{192,128},{256,320},{320,256},{384,448},{4... | collective-permute-start | bytes 774152 | tf_op jit(solution)/shard_map/ppermute | solution.py:85
  84.8 21.8 %collective-permute-done.4 = bf16[3,112,384]{2,1,0:T(8,128)(2,1)S(1)} collective-permute-done((bf16[3,112,384]{2,1,0:T(8,128)(2,1)S(1)}, bf16[3,112,384]{2,1,0:T(8,128)(2,1)S(1)}, u32[]{:S(2)}, u32[]{:S(2)}) %collective-permute-start.4) | collective-permute-done | bytes 258080 | tf_op jit(solution)/shard_map/ppermute | solution.py:85
  106.9 12.3 %all-gather = bf16[12,112,384]{2,1,0:T(8,128)(2,1)S(1)} all-gather(bf16[3,112,384]{2,1,0:T(8,128)(2,1)S(1)} %pad_maximum_fusion.3), channel_id=2, replica_groups={{0,128,256,384},{64,192,320,448},{1,129,257,385},{65,193,321,449},{2,13..., dimensions={0}, use_global_device_ids=true | all-gather | bytes 1290240 | tf_op jit(solution)/shard_map/all_gather | solution.py:133
  121.3 18.5 %all_to_all.28.in_ref = bf16[4,2,96,1024]{3,2,1,0:T(8,128)(2,1)S(1)} all-to-all(bf16[4,2,96,1024]{3,2,1,0:T(8,128)(2,1)S(1)} %pad_maximum_fusion.1), channel_id=1, replica_groups=mesh['depth'=8,'row'=4,'col'=16] {'row'}, dimensions={0} | all-to-all | bytes 3145728 | tf_op jit(solution)/shard_map/all_to_all | solution.py:79
  139.8 1.0 shard_map.118
  140.8 10.8 %all-to-all-start.4 = ((bf16[8,2,96,128]{3,2,1,0:T(8,128)(2,1)}), bf16[8,2,96,128]{3,2,1,0:T(8,128)(2,1)S(1)}, u32[]{:S(2)}, u32[]{:S(2)}) async-start(bf16[8,2,96,128]{3,2,1,0:T(8,128)(2,1)} %shard_map.118), calls=%async_computation.4 | async-start | bytes 786432 | tf_op jit(solution)/shard_map/all_to_all | solution.py:63
  151.7 7.8 %collective-permute-start.6 = (bf16[384,1024]{1,0:T(8,128)(2,1)S(1)}, bf16[384,1024]{1,0:T(8,128)(2,1)S(1)}, u32[]{:S(2)}, u32[]{:S(2)}) collective-permute-start(bf16[384,1024]{1,0:T(8,128)(2,1)S(1)} %bitcast.82), channel_id=1, source_target_pairs={{0,1},{1,0},{2,3},{3,2},{4,5},{5,4},{6,7},{7,6},{8,9},{9,8},{10,11... | collective-permute-start | bytes 2359304 | tf_op jit(solution)/shard_map/ppermute | solution.py:82
  159.9 1.9 %collective-permute-start.5 = (bf16[2,3,112,384]{3,2,1,0:T(8,128)(2,1)S(1)}, bf16[2,3,112,384]{3,2,1,0:T(8,128)(2,1)S(1)}, u32[]{:S(2)}, u32[]{:S(2)}) collective-permute-start(bf16[2,3,112,384]{3,2,1,0:T(8,128)(2,1)S(1)} %slice.88), channel_id=1, source_target_pairs={{0,1},{1,0},{2,3},{3,2},{4,5},{5,4},{6,7},{7,6},{8,9},{9,8},{10,11... | collective-permute-start | bytes 1548296 | tf_op jit(solution)/shard_map/ppermute | solution.py:82
  161.9 2.4 %collective-permute-start.7 = (bf16[384,1024]{1,0:T(8,128)(2,1)S(1)}, bf16[384,1024]{1,0:T(8,128)(2,1)S(1)}, u32[]{:S(2)}, u32[]{:S(2)}) collective-permute-start(bf16[384,1024]{1,0:T(8,128)(2,1)S(1)} %bitcast.86), channel_id=1, source_target_pairs={{0,1},{1,0},{2,3},{3,2},{4,5},{5,4},{6,7},{7,6},{8,9},{9,8},{10,11... | collective-permute-start | bytes 2359304 | tf_op jit(solution)/shard_map/ppermute | solution.py:82
  165.8 1.3 convolution_add_fusion.2
  167.2 1.3 convolution_add_fusion.1
  168.5 1.3 convolution_add_fusion
  170.0 8.1 %collective-permute-start.8 = (f32[2,64,96]{1,2,0:T(8,128)S(1)}, f32[2,64,96]{1,2,0:T(8,128)S(1)}, u32[]{:S(2)}, u32[]{:S(2)}) collective-permute-start(f32[2,64,96]{1,2,0:T(8,128)S(1)} %get-tuple-element.69), channel_id=1, source_target_pairs={{0,1},{1,0},{2,3},{3,2},{4,5},{5,4},{6,7},{7,6},{8,9},{9,8},{10,11... | collective-permute-start | bytes 147464 | tf_op jit(solution)/shard_map/ppermute | solution.py:82
  178.3 0.7 collective-permute-done.8
  (64 shorter events, 9.7 us)
Async XLA Ops:
  0.6 21.3 %copy-start.1 = (bf16[224,1024]{1,0:T(8,128)(2,1)S(1)}, bf16[224,1024]{1,0:T(8,128)(2,1)}, u32[]{:S(2)}) copy-start(bf16[224,1024]{1,0:T(8,128)(2,1)} %param.12) | copy-start | bytes 1376260
  0.6 21.3 %copy-start.2 = (bf16[224,1024]{1,0:T(8,128)(2,1)S(1)}, bf16[224,1024]{1,0:T(8,128)(2,1)}, u32[]{:S(2)}) copy-start(bf16[224,1024]{1,0:T(8,128)(2,1)} %param.13) | copy-start | bytes 1376260
  2.9 21.8 %collective-permute-start.2 = (bf16[2,96,64]{1,2,0:T(8,128)(2,1)S(1)}, bf16[2,96,64]{1,2,0:T(8,128)(2,1)S(1)}, u32[]{:S(2)}, u32[]{:S(2)}) collective-permute-start(bf16[2,96,64]{1,2,0:T(8,128)(2,1)S(1)} %get-tuple-element.26), channel_id=1, source_target_pairs={{0,9},{1,8},{2,11},{3,10},{4,13},{5,12},{6,15},{7,14},{8,1},{9,0},... | collective-permute-start | bytes 73736 | tf_op jit(solution)/shard_map/ppermute | solution.py:66
  13.2 11.6 %collective-permute-start = (bf16[2,96,64]{1,2,0:T(8,128)(2,1)S(1)}, bf16[2,96,64]{1,2,0:T(8,128)(2,1)S(1)}, u32[]{:S(2)}, u32[]{:S(2)}) collective-permute-start(bf16[2,96,64]{1,2,0:T(8,128)(2,1)S(1)} %get-tuple-element.26), channel_id=1, source_target_pairs={{0,1},{1,0},{2,3},{3,2},{4,5},{5,4},{6,7},{7,6},{8,9},{9,8},{10,11... | collective-permute-start | bytes 73736 | tf_op jit(solution)/shard_map/ppermute | solution.py:82
  15.1 9.6 %collective-permute-start.1 = (bf16[2,96,64]{1,2,0:T(8,128)(2,1)S(1)}, bf16[2,96,64]{1,2,0:T(8,128)(2,1)S(1)}, u32[]{:S(2)}, u32[]{:S(2)}) collective-permute-start(bf16[2,96,64]{1,2,0:T(8,128)(2,1)S(1)} %get-tuple-element.25), channel_id=1, source_target_pairs={{0,8},{1,9},{2,10},{3,11},{4,12},{5,13},{6,14},{7,15},{8,0},{9,1},... | collective-permute-start | bytes 73736 | tf_op jit(solution)/shard_map/ppermute | solution.py:66
  22.0 17.9 %collective-permute-start.3 = (bf16[224,3072]{1,0:T(8,128)(2,1)S(1)}, bf16[224,3072]{1,0:T(8,128)(2,1)S(1)}, u32[]{:S(2)}, u32[]{:S(2)}) collective-permute-start(bf16[224,3072]{1,0:T(8,128)(2,1)S(1)} %constant_dynamic-update-slice_fusion.2), channel_id=1, source_target_pairs={{0,1},{1,0},{2,3},{3,2},{4,5},{5,4},{6,7},{7,6},{8,9},{9,8},{10,11... | collective-permute-start | bytes 4128776 | tf_op jit(solution)/shard_map/ppermute | solution.py:82
  80.2 26.5 %collective-permute-start.4 = (bf16[3,112,384]{2,1,0:T(8,128)(2,1)S(1)}, bf16[3,112,384]{2,1,0:T(8,128)(2,1)S(1)}, u32[]{:S(2)}, u32[]{:S(2)}) collective-permute-start(bf16[3,112,384]{2,1,0:T(8,128)(2,1)S(1)} %convert_element_type.51), channel_id=1, source_target_pairs={{0,64},{64,0},{128,192},{192,128},{256,320},{320,256},{384,448},{4... | collective-permute-start | bytes 774152 | tf_op jit(solution)/shard_map/ppermute | solution.py:85
  140.8 29.0 %all-to-all-start.4 = ((bf16[8,2,96,128]{3,2,1,0:T(8,128)(2,1)}), bf16[8,2,96,128]{3,2,1,0:T(8,128)(2,1)S(1)}, u32[]{:S(2)}, u32[]{:S(2)}) async-start(bf16[8,2,96,128]{3,2,1,0:T(8,128)(2,1)} %shard_map.118), calls=%async_computation.4 | async-start | bytes 786432 | tf_op jit(solution)/shard_map/all_to_all | solution.py:63
  151.7 12.6 %copy-start = (f32[64,192]{1,0:T(8,128)S(1)}, f32[64,192]{1,0:T(8,128)}, u32[]{:S(2)}) copy-start(f32[64,192]{1,0:T(8,128)} %param.8) | copy-start | bytes 147460
  151.7 12.6 %copy-start.3 = (f32[64,192]{1,0:T(8,128)S(1)}, f32[64,192]{1,0:T(8,128)}, u32[]{:S(2)}) copy-start(f32[64,192]{1,0:T(8,128)} %param.7) | copy-start | bytes 147460
  151.7 14.1 %collective-permute-start.6 = (bf16[384,1024]{1,0:T(8,128)(2,1)S(1)}, bf16[384,1024]{1,0:T(8,128)(2,1)S(1)}, u32[]{:S(2)}, u32[]{:S(2)}) collective-permute-start(bf16[384,1024]{1,0:T(8,128)(2,1)S(1)} %bitcast.82), channel_id=1, source_target_pairs={{0,1},{1,0},{2,3},{3,2},{4,5},{5,4},{6,7},{7,6},{8,9},{9,8},{10,11... | collective-permute-start | bytes 2359304 | tf_op jit(solution)/shard_map/ppermute | solution.py:82
  159.9 5.8 %collective-permute-start.5 = (bf16[2,3,112,384]{3,2,1,0:T(8,128)(2,1)S(1)}, bf16[2,3,112,384]{3,2,1,0:T(8,128)(2,1)S(1)}, u32[]{:S(2)}, u32[]{:S(2)}) collective-permute-start(bf16[2,3,112,384]{3,2,1,0:T(8,128)(2,1)S(1)} %slice.88), channel_id=1, source_target_pairs={{0,1},{1,0},{2,3},{3,2},{4,5},{5,4},{6,7},{7,6},{8,9},{9,8},{10,11... | collective-permute-start | bytes 1548296 | tf_op jit(solution)/shard_map/ppermute | solution.py:82
  161.9 6.6 %collective-permute-start.7 = (bf16[384,1024]{1,0:T(8,128)(2,1)S(1)}, bf16[384,1024]{1,0:T(8,128)(2,1)S(1)}, u32[]{:S(2)}, u32[]{:S(2)}) collective-permute-start(bf16[384,1024]{1,0:T(8,128)(2,1)S(1)} %bitcast.86), channel_id=1, source_target_pairs={{0,1},{1,0},{2,3},{3,2},{4,5},{5,4},{6,7},{7,6},{8,9},{9,8},{10,11... | collective-permute-start | bytes 2359304 | tf_op jit(solution)/shard_map/ppermute | solution.py:82
  168.5 9.7 %copy-start.4 = (f32[64,192]{1,0:T(8,128)S(1)}, f32[64,192]{1,0:T(8,128)}, u32[]{:S(2)}) copy-start(f32[64,192]{1,0:T(8,128)} %param.9) | copy-start | bytes 147460
  170.0 9.0 %collective-permute-start.8 = (f32[2,64,96]{1,2,0:T(8,128)S(1)}, f32[2,64,96]{1,2,0:T(8,128)S(1)}, u32[]{:S(2)}, u32[]{:S(2)}) collective-permute-start(f32[2,64,96]{1,2,0:T(8,128)S(1)} %get-tuple-element.69), channel_id=1, source_target_pairs={{0,1},{1,0},{2,3},{3,2},{4,5},{5,4},{6,7},{7,6},{8,9},{9,8},{10,11... | collective-permute-start | bytes 147464 | tf_op jit(solution)/shard_map/ppermute | solution.py:82

commit v7 on v6

--- a/solution.py
+++ b/solution.py
@@ -158,9 +158,7 @@
         grad_down = gradient(0, df_mat, df_far)
         grad_gate = gradient(1, x_mat, x_far)
         grad_up = gradient(2, x_mat, x_far)
-        terms, x_prev, grad_gate, grad_up, grad_down = together(
-            (terms, x_prev, grad_gate, grad_up, grad_down)
-        )
+        terms, x_prev, grad_gate, grad_up = together((terms, x_prev, grad_gate, grad_up))
         terms = jnp.swapaxes(terms.astype(F32).sum(0), 1, 2)
         low, high = terms[:, :feats], terms[:, feats:]
         theirs = other_core(pick(high, low))

time: 181 us -> 187 us (1.033)
  local copies, waits for them, and re-layouts: 3.82 us -> 9.45 us
  starting transfers between devices: 56.2 us -> 50.6 us
  matrix products: 8.99 us -> 14.3 us
  other arithmetic: 3.77 us -> 5.65 us
    ppermute x6, starting transfers between devices: 24.8 us -> 18.4 us  [other_core(): return lax.ppermute(block, 'col', swap_core)]
    dot_general x12, matrix products: 8.99 us -> 14.3 us  [dot(): lax.dot_general(left, right, (((left_dim,), (right_dim,)), ((), ())), pre...]
    optimization_barrier x2, local copies, waits for them, and re-layouts: 0.18 us -> 2.51 us  [on_device(): together((terms, hidden, x_out, v_out, dx_out, x_mat, df_mat))]
  transfers between devices with their start and end apart: 10 -> 10, of which waited for: 2 -> 1; matrix products, arithmetic and copies ran while one was open for 4% -> 11% of each run, Pallas kernels for 0% -> 0%
where the time goes in v7:
time: 187 us; the launch traced here: 186 us
  blocking collectives  82.3 us (44%)
  starting transfers between devices  50.6 us (27%)
  waiting for transfers between devices  21.9 us (12%)
  matrix products  14.3 us (8%)
  local copies, waits for them, and re-layouts  9.45 us (5%)
  other arithmetic  5.65 us (3%)
    all_to_all x2, blocking collectives, over_row(): return lax.all_to_all(blocks, 'row', 0, 0)  40.3 us
    ppermute x1, waiting for transfers between devices, other_half(): return lax.ppermute(block, 'depth', swap_half)  21.8 us
    ppermute x6, starting transfers between devices, other_core(): return lax.ppermute(block, 'col', swap_core)  18.4 us
    ppermute x2, starting transfers between devices, across_z(): lax.ppermute(block, 'col', [(c, (c + count_z) % cols ^ flip) for c in ran...  16 us
    all_to_all x1, blocking collectives, over_x(): return lax.all_to_all(blocks, 'depth', 0, 0, axis_index_groups=x_groups)  15.1 us
    all_to_all x1, blocking collectives, gather_half(): lax.all_to_all(copies(both, span), 'col', 0, 0, axis_index_groups=groups)  14.8 us
    dot_general x12, matrix products, dot(): lax.dot_general(left, right, (((left_dim,), (right_dim,)), ((), ())), pre...  14.3 us
    all_gather x1, blocking collectives, on_device(): lax.all_gather(nonlinear(sums[0], sums[1], sums[2]), 'depth', axis_index_...  12 us
  transfers between devices with their start and end apart: 10, of which 1 were waited for; matrix products, arithmetic and copies ran while one was open for 11% of the time, Pallas kernels for 0%

profile of v7, /device:TPU:1, one launch (start us, length us, event | category | flops | bytes accessed | tf_op | source)
XLA Modules:
  0.0 186.2 jit_solution(5377015953299416561)
XLA Ops:
  2.9 10.2 %collective-permute-start.2 = (bf16[2,96,64]{1,2,0:T(8,128)(2,1)S(1)}, bf16[2,96,64]{1,2,0:T(8,128)(2,1)S(1)}, u32[]{:S(2)}, u32[]{:S(2)}) collective-permute-start(bf16[2,96,64]{1,2,0:T(8,128)(2,1)S(1)} %get-tuple-element.25), channel_id=1, source_target_pairs={{0,9},{1,8},{2,11},{3,10},{4,13},{5,12},{6,15},{7,14},{8,1},{9,0},... | collective-permute-start | bytes 73736 | tf_op jit(solution)/shard_map/ppermute | solution.py:66
  13.2 1.9 %collective-permute-start = (bf16[2,96,64]{1,2,0:T(8,128)(2,1)S(1)}, bf16[2,96,64]{1,2,0:T(8,128)(2,1)S(1)}, u32[]{:S(2)}, u32[]{:S(2)}) collective-permute-start(bf16[2,96,64]{1,2,0:T(8,128)(2,1)S(1)} %get-tuple-element.25), channel_id=1, source_target_pairs={{0,1},{1,0},{2,3},{3,2},{4,5},{5,4},{6,7},{7,6},{8,9},{9,8},{10,11... | collective-permute-start | bytes 73736 | tf_op jit(solution)/shard_map/ppermute | solution.py:82
  15.1 5.7 %collective-permute-start.1 = (bf16[2,96,64]{1,2,0:T(8,128)(2,1)S(1)}, bf16[2,96,64]{1,2,0:T(8,128)(2,1)S(1)}, u32[]{:S(2)}, u32[]{:S(2)}) collective-permute-start(bf16[2,96,64]{1,2,0:T(8,128)(2,1)S(1)} %get-tuple-element.24), channel_id=1, source_target_pairs={{0,8},{1,9},{2,10},{3,11},{4,12},{5,13},{6,14},{7,15},{8,0},{9,1},... | collective-permute-start | bytes 73736 | tf_op jit(solution)/shard_map/ppermute | solution.py:66
  22.0 2.7 %collective-permute-start.3 = (bf16[224,3072]{1,0:T(8,128)(2,1)S(1)}, bf16[224,3072]{1,0:T(8,128)(2,1)S(1)}, u32[]{:S(2)}, u32[]{:S(2)}) collective-permute-start(bf16[224,3072]{1,0:T(8,128)(2,1)S(1)} %constant_dynamic-update-slice_fusion.2), channel_id=1, source_target_pairs={{0,1},{1,0},{2,3},{3,2},{4,5},{5,4},{6,7},{7,6},{8,9},{9,8},{10,11... | collective-permute-start | bytes 4128776 | tf_op jit(solution)/shard_map/ppermute | solution.py:82
  25.0 14.8 %all_to_all.25 = bf16[4,2,2,96,128]{4,3,2,1,0:T(8,128)(2,1)S(1)} all-to-all(bf16[4,2,2,96,128]{4,3,2,1,0:T(8,128)(2,1)S(1)} %broadcast_in_dim.6), channel_id=1, replica_groups={{0,2,4,6},{1,3,5,7},{8,10,12,14},{9,11,13,15},{16,18,20,22},{17,19,21,2..., dimensions={0} | all-to-all | bytes 786432 | tf_op jit(solution)/shard_map/all_to_all | solution.py:75
  40.3 22.3 %all_to_all.26 = bf16[4,2,96,1024]{3,2,1,0:T(8,128)(2,1)S(1)} all-to-all(bf16[4,2,96,1024]{3,2,1,0:T(8,128)(2,1)S(1)} %broadcast_in_dim.15), channel_id=1, replica_groups=mesh['depth'=8,'row'=4,'col'=16] {'row'}, dimensions={0} | all-to-all | bytes 3145728 | tf_op jit(solution)/shard_map/all_to_all | solution.py:79
  64.9 15.1 %all_to_all.27 = bf16[4,3,112,384]{3,2,1,0:T(8,128)(2,1)S(1)} all-to-all(bf16[4,3,112,384]{3,2,1,0:T(8,128)(2,1)S(1)} %pad_maximum_fusion.2), channel_id=1, replica_groups={{0,128,256,384},{64,192,320,448},{1,129,257,385},{65,193,321,449},{2,13..., dimensions={0} | all-to-all | bytes 2064384 | tf_op jit(solution)/shard_map/all_to_all | solution.py:60
  80.3 4.6 %collective-permute-start.4 = (bf16[3,112,384]{2,1,0:T(8,128)(2,1)S(1)}, bf16[3,112,384]{2,1,0:T(8,128)(2,1)S(1)}, u32[]{:S(2)}, u32[]{:S(2)}) collective-permute-start(bf16[3,112,384]{2,1,0:T(8,128)(2,1)S(1)} %convert_element_type.51), channel_id=1, source_target_pairs={{0,64},{64,0},{128,192},{192,128},{256,320},{320,256},{384,448},{4... | collective-permute-start | bytes 774152 | tf_op jit(solution)/shard_map/ppermute | solution.py:85
  84.9 21.8 %collective-permute-done.4 = bf16[3,112,384]{2,1,0:T(8,128)(2,1)S(1)} collective-permute-done((bf16[3,112,384]{2,1,0:T(8,128)(2,1)S(1)}, bf16[3,112,384]{2,1,0:T(8,128)(2,1)S(1)}, u32[]{:S(2)}, u32[]{:S(2)}) %collective-permute-start.4) | collective-permute-done | bytes 258080 | tf_op jit(solution)/shard_map/ppermute | solution.py:85
  106.9 12.0 %all-gather = bf16[12,112,384]{2,1,0:T(8,128)(2,1)S(1)} all-gather(bf16[3,112,384]{2,1,0:T(8,128)(2,1)S(1)} %pad_maximum_fusion.3), channel_id=2, replica_groups={{0,128,256,384},{64,192,320,448},{1,129,257,385},{65,193,321,449},{2,13..., dimensions={0}, use_global_device_ids=true | all-gather | bytes 1290240 | tf_op jit(solution)/shard_map/all_gather | solution.py:133
  121.0 18.0 %all_to_all.28.in_ref = bf16[4,2,96,1024]{3,2,1,0:T(8,128)(2,1)S(1)} all-to-all(bf16[4,2,96,1024]{3,2,1,0:T(8,128)(2,1)S(1)} %pad_maximum_fusion.1), channel_id=1, replica_groups=mesh['depth'=8,'row'=4,'col'=16] {'row'}, dimensions={0} | all-to-all | bytes 3145728 | tf_op jit(solution)/shard_map/all_to_all | solution.py:79
  140.0 11.6 %all-to-all-start.4 = ((bf16[8,2,96,128]{3,2,1,0:T(8,128)(2,1)}), bf16[8,2,96,128]{3,2,1,0:T(8,128)(2,1)}, u32[]{:S(2)}, u32[]{:S(2)}) async-start(bf16[8,2,96,128]{3,2,1,0:T(8,128)(2,1)} %shard_map.118), calls=%async_computation.4 | async-start | bytes 786432 | tf_op jit(solution)/shard_map/all_to_all | solution.py:63
  152.4 7.6 %collective-permute-start.6 = (bf16[384,1024]{1,0:T(8,128)(2,1)S(1)}, bf16[384,1024]{1,0:T(8,128)(2,1)}, u32[]{:S(2)}, u32[]{:S(2)}) collective-permute-start(bf16[384,1024]{1,0:T(8,128)(2,1)S(1)} %bitcast.82), channel_id=1, source_target_pairs={{0,1},{1,0},{2,3},{3,2},{4,5},{5,4},{6,7},{7,6},{8,9},{9,8},{10,11... | collective-permute-start | bytes 2359304 | tf_op jit(solution)/shard_map/ppermute | solution.py:82
  162.2 1.5 sub.20
  163.7 1.9 %collective-permute-start.5 = (bf16[2,3,112,384]{3,2,1,0:T(8,128)(2,1)}, bf16[2,3,112,384]{3,2,1,0:T(8,128)(2,1)}, u32[]{:S(2)}, u32[]{:S(2)}) collective-permute-start(bf16[2,3,112,384]{3,2,1,0:T(8,128)(2,1)} %slice.88), channel_id=1, source_target_pairs={{0,1},{1,0},{2,3},{3,2},{4,5},{5,4},{6,7},{7,6},{8,9},{9,8},{10,11... | collective-permute-start | bytes 1548296 | tf_op jit(solution)/shard_map/ppermute | solution.py:82
  165.6 1.6 copy.31
  167.2 2.4 %collective-permute-start.8 = (bf16[384,1024]{1,0:T(8,128)(2,1)S(1)}, bf16[384,1024]{1,0:T(8,128)(2,1)}, u32[]{:S(2)}, u32[]{:S(2)}) collective-permute-start(bf16[384,1024]{1,0:T(8,128)(2,1)S(1)} %bitcast.86), channel_id=1, source_target_pairs={{0,1},{1,0},{2,3},{3,2},{4,5},{5,4},{6,7},{7,6},{8,9},{9,8},{10,11... | collective-permute-start | bytes 2359304 | tf_op jit(solution)/shard_map/ppermute | solution.py:82
  169.6 1.3 fusion.18
  170.9 1.3 fusion.19
  172.3 1.8 fusion.16
  174.1 2.5 %convolution_add_fusion.2 = f32[224,1024]{1,0:T(8,128)} fusion(f32[224,1024]{1,0:T(8,128)S(1)} %fusion.17, bf16[224,384]{1,0:T(8,128)(2,1)S(1)} %bitcast.99, bf16[384,1024]{1,0:T(8,128)(2,1)} %collective-permute-done.6), kind=kOutput, calls=%fused_computation.7 | convolution fusion | flops 176390144 | bytes 2793472 | tf_op jit(solution)/shard_map/dot_general | solution.py:19
  176.6 2.5 %convolution_add_fusion.1 = f32[224,1024]{1,0:T(8,128)} fusion(f32[224,1024]{1,0:T(8,128)S(1)} %fusion.18, bf16[224,384]{1,0:T(8,128)(2,1)S(1)} %bitcast.98, bf16[384,1024]{1,0:T(8,128)(2,1)} %collective-permute-done.6), kind=kOutput, calls=%fused_computation.6 | convolution fusion | flops 176390144 | bytes 2793472 | tf_op jit(solution)/shard_map/dot_general | solution.py:19
  180.2 1.9 %collective-permute-start.7 = (f32[2,64,96]{1,2,0:T(8,128)S(1)}, f32[2,64,96]{1,2,0:T(8,128)S(1)}, u32[]{:S(2)}, u32[]{:S(2)}) collective-permute-start(f32[2,64,96]{1,2,0:T(8,128)S(1)} %get-tuple-element.67), channel_id=1, source_target_pairs={{0,1},{1,0},{2,3},{3,2},{4,5},{5,4},{6,7},{7,6},{8,9},{9,8},{10,11... | collective-permute-start | bytes 147464 | tf_op jit(solution)/shard_map/ppermute | solution.py:82
  182.2 2.5 %convolution_add_fusion = f32[224,1024]{1,0:T(8,128)} fusion(f32[224,1024]{1,0:T(8,128)S(1)} %fusion.19, bf16[224,384]{1,0:T(8,128)(2,1)S(1)} %bitcast.97, bf16[384,1024]{1,0:T(8,128)(2,1)} %collective-permute-done.8), kind=kOutput, calls=%fused_computation.5 | convolution fusion | flops 176390144 | bytes 2793472 | tf_op jit(solution)/shard_map/dot_general | solution.py:19
  (62 shorter events, 15.4 us)
Async XLA Ops:
  0.6 21.3 %copy-start.1 = (bf16[224,1024]{1,0:T(8,128)(2,1)S(1)}, bf16[224,1024]{1,0:T(8,128)(2,1)}, u32[]{:S(2)}) copy-start(bf16[224,1024]{1,0:T(8,128)(2,1)} %param.12) | copy-start | bytes 1376260
  0.6 21.3 %copy-start.2 = (bf16[224,1024]{1,0:T(8,128)(2,1)S(1)}, bf16[224,1024]{1,0:T(8,128)(2,1)}, u32[]{:S(2)}) copy-start(bf16[224,1024]{1,0:T(8,128)(2,1)} %param.13) | copy-start | bytes 1376260
  2.9 21.8 %collective-permute-start.2 = (bf16[2,96,64]{1,2,0:T(8,128)(2,1)S(1)}, bf16[2,96,64]{1,2,0:T(8,128)(2,1)S(1)}, u32[]{:S(2)}, u32[]{:S(2)}) collective-permute-start(bf16[2,96,64]{1,2,0:T(8,128)(2,1)S(1)} %get-tuple-element.25), channel_id=1, source_target_pairs={{0,9},{1,8},{2,11},{3,10},{4,13},{5,12},{6,15},{7,14},{8,1},{9,0},... | collective-permute-start | bytes 73736 | tf_op jit(solution)/shard_map/ppermute | solution.py:66
  13.2 11.6 %collective-permute-start = (bf16[2,96,64]{1,2,0:T(8,128)(2,1)S(1)}, bf16[2,96,64]{1,2,0:T(8,128)(2,1)S(1)}, u32[]{:S(2)}, u32[]{:S(2)}) collective-permute-start(bf16[2,96,64]{1,2,0:T(8,128)(2,1)S(1)} %get-tuple-element.25), channel_id=1, source_target_pairs={{0,1},{1,0},{2,3},{3,2},{4,5},{5,4},{6,7},{7,6},{8,9},{9,8},{10,11... | collective-permute-start | bytes 73736 | tf_op jit(solution)/shard_map/ppermute | solution.py:82
  15.1 9.6 %collective-permute-start.1 = (bf16[2,96,64]{1,2,0:T(8,128)(2,1)S(1)}, bf16[2,96,64]{1,2,0:T(8,128)(2,1)S(1)}, u32[]{:S(2)}, u32[]{:S(2)}) collective-permute-start(bf16[2,96,64]{1,2,0:T(8,128)(2,1)S(1)} %get-tuple-element.24), channel_id=1, source_target_pairs={{0,8},{1,9},{2,10},{3,11},{4,12},{5,13},{6,14},{7,15},{8,0},{9,1},... | collective-permute-start | bytes 73736 | tf_op jit(solution)/shard_map/ppermute | solution.py:66
  22.0 17.9 %collective-permute-start.3 = (bf16[224,3072]{1,0:T(8,128)(2,1)S(1)}, bf16[224,3072]{1,0:T(8,128)(2,1)S(1)}, u32[]{:S(2)}, u32[]{:S(2)}) collective-permute-start(bf16[224,3072]{1,0:T(8,128)(2,1)S(1)} %constant_dynamic-update-slice_fusion.2), channel_id=1, source_target_pairs={{0,1},{1,0},{2,3},{3,2},{4,5},{5,4},{6,7},{7,6},{8,9},{9,8},{10,11... | collective-permute-start | bytes 4128776 | tf_op jit(solution)/shard_map/ppermute | solution.py:82
  80.3 26.4 %collective-permute-start.4 = (bf16[3,112,384]{2,1,0:T(8,128)(2,1)S(1)}, bf16[3,112,384]{2,1,0:T(8,128)(2,1)S(1)}, u32[]{:S(2)}, u32[]{:S(2)}) collective-permute-start(bf16[3,112,384]{2,1,0:T(8,128)(2,1)S(1)} %convert_element_type.51), channel_id=1, source_target_pairs={{0,64},{64,0},{128,192},{192,128},{256,320},{320,256},{384,448},{4... | collective-permute-start | bytes 774152 | tf_op jit(solution)/shard_map/ppermute | solution.py:85
  140.0 39.1 %all-to-all-start.4 = ((bf16[8,2,96,128]{3,2,1,0:T(8,128)(2,1)}), bf16[8,2,96,128]{3,2,1,0:T(8,128)(2,1)}, u32[]{:S(2)}, u32[]{:S(2)}) async-start(bf16[8,2,96,128]{3,2,1,0:T(8,128)(2,1)} %shard_map.118), calls=%async_computation.4 | async-start | bytes 786432 | tf_op jit(solution)/shard_map/all_to_all | solution.py:63
  152.4 21.7 %collective-permute-start.6 = (bf16[384,1024]{1,0:T(8,128)(2,1)S(1)}, bf16[384,1024]{1,0:T(8,128)(2,1)}, u32[]{:S(2)}, u32[]{:S(2)}) collective-permute-start(bf16[384,1024]{1,0:T(8,128)(2,1)S(1)} %bitcast.82), channel_id=1, source_target_pairs={{0,1},{1,0},{2,3},{3,2},{4,5},{5,4},{6,7},{7,6},{8,9},{9,8},{10,11... | collective-permute-start | bytes 2359304 | tf_op jit(solution)/shard_map/ppermute | solution.py:82
  163.7 8.5 %collective-permute-start.5 = (bf16[2,3,112,384]{3,2,1,0:T(8,128)(2,1)}, bf16[2,3,112,384]{3,2,1,0:T(8,128)(2,1)}, u32[]{:S(2)}, u32[]{:S(2)}) collective-permute-start(bf16[2,3,112,384]{3,2,1,0:T(8,128)(2,1)} %slice.88), channel_id=1, source_target_pairs={{0,1},{1,0},{2,3},{3,2},{4,5},{5,4},{6,7},{7,6},{8,9},{9,8},{10,11... | collective-permute-start | bytes 1548296 | tf_op jit(solution)/shard_map/ppermute | solution.py:82
  167.2 15.0 %collective-permute-start.8 = (bf16[384,1024]{1,0:T(8,128)(2,1)S(1)}, bf16[384,1024]{1,0:T(8,128)(2,1)}, u32[]{:S(2)}, u32[]{:S(2)}) collective-permute-start(bf16[384,1024]{1,0:T(8,128)(2,1)S(1)} %bitcast.86), channel_id=1, source_target_pairs={{0,1},{1,0},{2,3},{3,2},{4,5},{5,4},{6,7},{7,6},{8,9},{9,8},{10,11... | collective-permute-start | bytes 2359304 | tf_op jit(solution)/shard_map/ppermute | solution.py:82
  176.6 5.6 %copy-start = (bf16[2,1,112,384]{3,2,1,0:T(8,128)(2,1)S(1)}, bf16[2,1,112,384]{3,2,1,0:T(8,128)(2,1)}, u32[]{:S(2)}) copy-start(bf16[2,1,112,384]{3,2,1,0:T(8,128)(2,1)} %get-tuple-element.56) | copy-start | bytes 516100
  180.2 4.5 %collective-permute-start.7 = (f32[2,64,96]{1,2,0:T(8,128)S(1)}, f32[2,64,96]{1,2,0:T(8,128)S(1)}, u32[]{:S(2)}, u32[]{:S(2)}) collective-permute-start(f32[2,64,96]{1,2,0:T(8,128)S(1)} %get-tuple-element.67), channel_id=1, source_target_pairs={{0,1},{1,0},{2,3},{3,2},{4,5},{5,4},{6,7},{7,6},{8,9},{9,8},{10,11... | collective-permute-start | bytes 147464 | tf_op jit(solution)/shard_map/ppermute | solution.py:82
  182.2 2.5 %copy-start.3 = (f32[64,192]{0,1:T(8,128)S(1)}, f32[64,192]{0,1:T(8,128)}, u32[]{:S(2)}) copy-start(f32[64,192]{0,1:T(8,128)} %copy.31) | copy-start | bytes 147460
